TPU v7x, 32 devices: a whole 2x2x4 slice. The times are simulated.
32 devices in a mesh: dp: 8 (over y, x, core), mp: 4 (over z).
Axes of the slice: x: 2, y: 2, z: 4, core: 2. Of those that a mesh axis runs over, the one named last changes fastest.
Arguments:
- image_states: bfloat16 [16, 1024, 1024], P('dp', 'mp'), may hold values from -6 to 6
- text_states: bfloat16 [16, 128, 1024], P('dp'), may hold values from -6 to 6
- text_mask: int32 [16, 128], P('dp'), may hold values from 0 to 1, as said below
- cotangent: bfloat16 [16, 1024, 1024], P('dp', 'mp'), may hold values from -6 to 6
- input_weights: float32 [6, 1024, 1024], P(None, 'dp', 'mp'), may hold values from -0.1875 to 0.1875
- output_weights: float32 [2, 1024, 1024], P(None, 'dp', 'mp'), may hold values from -1 to 1
- hidden_weights: float32 [2, 1024, 4096], P(None, 'dp', 'mp'), may hold values from -0.1875 to 0.1875
- norm_gains: float32 [6, 1024], P(None, ('dp', 'mp')), may hold values from -0.3 to 1.95, as said below
- input_momentum: float32 [6, 1024, 1024], P(None, 'dp', 'mp'), may hold values from -0.0004272461 to 0.0004272461
- output_momentum: float32 [2, 1024, 1024], P(None, 'dp', 'mp'), may hold values from -0.00015258789 to 0.00015258789
- hidden_momentum: float32 [2, 1024, 4096], P(None, 'dp', 'mp'), may hold values from -0.0004272461 to 0.0004272461
- gains_momentum: float32 [6, 1024], P(None, ('dp', 'mp')), may hold values from -0.00030517578 to 0.00030517578
- input_variance: float32 [6, 1024, 1024], P(None, 'dp', 'mp'), may hold values from 1.5258789e-09 to 2.4795533e-08
- output_variance: float32 [2, 1024, 1024], P(None, 'dp', 'mp'), may hold values from 4.768372e-10 to 1.9073487e-09
- hidden_variance: float32 [2, 1024, 4096], P(None, 'dp', 'mp'), may hold values from 1.5258789e-09 to 2.4795533e-08
- gains_variance: float32 [6, 1024], P(None, ('dp', 'mp')), may hold values from 1.9073487e-09 to 1.525879e-08
Outputs:
- layer_out: float32 [16, 1024, 1024], P('dp', 'mp')
- image_gradient: float32 [16, 1024, 1024], P('dp', 'mp')
- text_gradient: float32 [16, 128, 1024], P('dp', 'mp')
- global_norm: float32 [], replicated
- input_updated: float32 [6, 1024, 1024], P(None, 'dp', 'mp')
- output_updated: float32 [2, 1024, 1024], P(None, 'dp', 'mp')
- hidden_updated: float32 [2, 1024, 4096], P(None, 'dp', 'mp')
- gains_updated: float32 [6, 1024], P(None, ('dp', 'mp'))
- input_moment: float32 [6, 1024, 1024], P(None, 'dp', 'mp')
- output_moment: float32 [2, 1024, 1024], P(None, 'dp', 'mp')
- hidden_moment: float32 [2, 1024, 4096], P(None, 'dp', 'mp')
- gains_moment: float32 [6, 1024], P(None, ('dp', 'mp'))
- input_square: float32 [6, 1024, 1024], P(None, 'dp', 'mp')
- output_square: float32 [2, 1024, 1024], P(None, 'dp', 'mp')
- hidden_square: float32 [2, 1024, 4096], P(None, 'dp', 'mp')
- gains_square: float32 [6, 1024], P(None, ('dp', 'mp'))
Inputs may be any that keep to these rules, and one draw needn't show every extreme that they name: `text_mask`: each item's row is 1 on its first n positions and 0 after them, with n from 8 to 128; some item has all 128 valid. `norm_gains`: rows 0, 2 and 4 are gains, rows 1, 3 and 5 biases.
All inputs are finite; a program needn't handle non-finite values.
Results may differ from a plain program's by a relative error of at most 0.023.
Values may be sent and summed in bfloat16 or wider, within the bound.
No kernel may reach another device: no remote copies, remote signals or barrier semaphores. Data moves between devices by JAX's collectives and lax.ppermute only.
A program may use at most 192 MiB of HBM per device.

v0:
```python
import math

import jax
import jax.numpy as jnp
from jax import lax
from jax.sharding import PartitionSpec as P

HEAD_DIM = 64
STEP = 10


NORM_EPSILON = 1e-05
MASKED_SCORE = -1e30
BETA_FIRST = 0.9
BETA_SECOND = 0.95
LEARN_RATE = 0.1
GAIN_RATE = 0.5
WEIGHT_DECAY = 0.1
ADAM_EPSILON = 1e-08
CLIP_LIMIT = 1.0
GELU_SCALE = 0.7978845608028654
GELU_CUBIC = 0.044715


def normalize(values, gain_row, shift_row):
    center = values - jnp.mean(values, axis=-1, keepdims=True)
    spread = jnp.mean(center * center, axis=-1, keepdims=True)
    return center * lax.rsqrt(spread + NORM_EPSILON) * gain_row + shift_row


def gelu_tanh(values):
    return (
        0.5
        * values
        * (1.0 + jnp.tanh(GELU_SCALE * (values + GELU_CUBIC * values * values * values)))
    )


def spread_rows(normed):
    return lax.all_gather(normed, "mp", axis=1, tiled=True)


def collect_rows(partial_value):
    return lax.psum_scatter(partial_value, "mp", scatter_dimension=1, tiled=True)


def spread_grads(residual):
    return lax.all_gather(residual.astype(jnp.bfloat16), "mp", axis=1, tiled=True)


def collect_grads(partial_value):
    return lax.psum_scatter(partial_value, "mp", scatter_dimension=1, tiled=True)


def lower_weights(input_weights, output_weights, hidden_weights):
    return (
        lax.all_gather(input_weights.astype(jnp.bfloat16), "dp", axis=1, tiled=True),
        lax.all_gather(output_weights.astype(jnp.bfloat16), "dp", axis=1, tiled=True),
        lax.all_gather(hidden_weights.astype(jnp.bfloat16), "dp", axis=1, tiled=True),
    )


def lower_again(input_weights, output_weights, hidden_weights):
    return (
        lax.all_gather(input_weights.astype(jnp.bfloat16), "dp", axis=1, tiled=True),
        lax.all_gather(output_weights.astype(jnp.bfloat16), "dp", axis=1, tiled=True),
        lax.all_gather(hidden_weights.astype(jnp.bfloat16), "dp", axis=1, tiled=True),
    )


def attend_forward(queries, key_rows, value_rows, allow_rule):
    item_count, seq_length, column_count = queries.shape
    key_count = key_rows.shape[1]
    head_count = column_count // HEAD_DIM
    block_rows = min(512, seq_length)
    block_count = seq_length // block_rows
    score_scale = 1.0 / math.sqrt(HEAD_DIM)
    query_blocks = queries.reshape(item_count, block_count, block_rows, head_count, HEAD_DIM)
    key_heads = key_rows.reshape(item_count, key_count, head_count, HEAD_DIM)
    value_heads = value_rows.reshape(item_count, key_count, head_count, HEAD_DIM)
    block_starts = jnp.arange(block_count, dtype=jnp.int32) * block_rows

    def per_item(packed):
        item_blocks, item_keys, item_values, item_index = packed

        def per_block(inner_pack):
            query_block, block_start = inner_pack
            scores = (
                jnp.einsum(
                    "qhe,khe->hqk", query_block, item_keys, preferred_element_type=jnp.float32
                )
                * score_scale
            )
            scores = jnp.where(
                allow_rule(item_index, block_start, block_rows, key_count)[None],
                scores,
                MASKED_SCORE,
            )
            maximum = jnp.max(scores, axis=-1, keepdims=True)
            raised = jnp.exp(scores - maximum)
            row_total = jnp.sum(raised, axis=-1, keepdims=True)
            soft_weights = (raised / row_total).astype(jnp.bfloat16)
            mixed_rows = jnp.einsum(
                "hqk,khe->qhe", soft_weights, item_values, preferred_element_type=jnp.float32
            )
            return (mixed_rows.astype(jnp.bfloat16), (maximum + jnp.log(row_total))[..., 0])

        return lax.map(per_block, (item_blocks, block_starts))

    item_order = jnp.arange(item_count, dtype=jnp.int32)
    mixed_rows, log_totals = lax.map(per_item, (query_blocks, key_heads, value_heads, item_order))
    return (mixed_rows.reshape(item_count, seq_length, column_count), log_totals)


def attend_backward(queries, key_rows, value_rows, log_totals, mixed_grad, allow_rule):
    item_count, seq_length, column_count = queries.shape
    key_count = key_rows.shape[1]
    head_count = column_count // HEAD_DIM
    block_rows = min(512, seq_length)
    block_count = seq_length // block_rows
    score_scale = 1.0 / math.sqrt(HEAD_DIM)
    query_blocks = queries.reshape(item_count, block_count, block_rows, head_count, HEAD_DIM)
    grad_blocks = mixed_grad.reshape(item_count, block_count, block_rows, head_count, HEAD_DIM)
    key_heads = key_rows.reshape(item_count, key_count, head_count, HEAD_DIM)
    value_heads = value_rows.reshape(item_count, key_count, head_count, HEAD_DIM)
    block_starts = jnp.arange(block_count, dtype=jnp.int32) * block_rows

    def per_item(packed):
        item_blocks, item_grads, item_totals, item_keys, item_values, item_index = packed

        def per_block(carry_sums, inner_pack):
            key_sum, value_sum = carry_sums
            query_block, grad_block, total_block, block_start = inner_pack
            scores = (
                jnp.einsum(
                    "qhe,khe->hqk", query_block, item_keys, preferred_element_type=jnp.float32
                )
                * score_scale
            )
            scores = jnp.where(
                allow_rule(item_index, block_start, block_rows, key_count)[None],
                scores,
                MASKED_SCORE,
            )
            soft_float = jnp.exp(scores - total_block[..., None])
            soft_weights = soft_float.astype(jnp.bfloat16)
            value_sum = value_sum + jnp.einsum(
                "hqk,qhe->khe", soft_weights, grad_block, preferred_element_type=jnp.float32
            )
            weight_grad = jnp.einsum(
                "qhe,khe->hqk", grad_block, item_values, preferred_element_type=jnp.float32
            )
            row_delta = jnp.sum(soft_float * weight_grad, axis=-1, keepdims=True)
            score_grad = (soft_float * (weight_grad - row_delta)).astype(jnp.bfloat16)
            query_grad = (
                jnp.einsum(
                    "hqk,khe->qhe", score_grad, item_keys, preferred_element_type=jnp.float32
                )
                * score_scale
            )
            key_sum = (
                key_sum
                + jnp.einsum(
                    "hqk,qhe->khe", score_grad, query_block, preferred_element_type=jnp.float32
                )
                * score_scale
            )
            return ((key_sum, value_sum), query_grad.astype(jnp.bfloat16))

        zero_sums = jnp.zeros((key_count, head_count, HEAD_DIM), jnp.float32)
        (key_sum, value_sum), query_grads = lax.scan(
            per_block, (zero_sums, zero_sums), (item_blocks, item_grads, item_totals, block_starts)
        )
        return (query_grads, key_sum.astype(jnp.bfloat16), value_sum.astype(jnp.bfloat16))

    item_order = jnp.arange(item_count, dtype=jnp.int32)
    query_grads, key_grads, value_grads = lax.map(
        per_item, (query_blocks, grad_blocks, log_totals, key_heads, value_heads, item_order)
    )
    return (
        query_grads.reshape(item_count, seq_length, column_count),
        key_grads.reshape(item_count, key_count, column_count),
        value_grads.reshape(item_count, key_count, column_count),
    )


def adam_update(master, gradient, momentum, variance, factor, rate, decay_rate):
    clipped = gradient * factor
    moment = BETA_FIRST * momentum + (1.0 - BETA_FIRST) * clipped
    square = BETA_SECOND * variance + (1.0 - BETA_SECOND) * clipped * clipped
    step_ratio = (
        moment
        / (1.0 - BETA_FIRST**STEP)
        / (jnp.sqrt(square / (1.0 - BETA_SECOND**STEP)) + ADAM_EPSILON)
    )
    return (master - rate * (step_ratio + decay_rate * master), moment, square)


def per_device(
    image_states,
    text_states,
    text_mask,
    cotangent,
    input_weights,
    output_weights,
    hidden_weights,
    norm_gains,
    input_momentum,
    output_momentum,
    hidden_momentum,
    gains_momentum,
    input_variance,
    output_variance,
    hidden_variance,
    gains_variance,
):
    input_low, output_low, hidden_low = lower_weights(input_weights, output_weights, hidden_weights)
    gain_rows = lax.all_gather(norm_gains, ("dp", "mp"), axis=1, tiled=True)

    def attention_out(mixed, which):
        return collect_rows(
            jnp.einsum("isc,dc->isd", mixed, output_low[which], preferred_element_type=jnp.float32)
        )

    def causal(item_index, block_start, block_rows, key_count):
        query_place = block_start + jnp.arange(block_rows, dtype=jnp.int32)
        return query_place[:, None] >= jnp.arange(key_count, dtype=jnp.int32)[None, :]

    def masked(item_index, block_start, block_rows, key_count):
        return (text_mask[item_index] > 0)[None, :]

    image_float = image_states.astype(jnp.float32)
    normed_one, norm_one_back = jax.vjp(normalize, image_float, gain_rows[0], gain_rows[1])
    rows_one = spread_rows(normed_one.astype(jnp.bfloat16))
    self_proj = jnp.einsum(
        "isd,jdc->jisc", rows_one, input_low[0:3], preferred_element_type=jnp.float32
    ).astype(jnp.bfloat16)
    self_mixed, self_totals = attend_forward(self_proj[0], self_proj[1], self_proj[2], causal)
    first_sum = image_float + attention_out(self_mixed, 0)
    normed_two, norm_two_back = jax.vjp(normalize, first_sum, gain_rows[2], gain_rows[3])
    rows_two = spread_rows(normed_two.astype(jnp.bfloat16))
    cross_query = jnp.einsum(
        "isd,dc->isc", rows_two, input_low[3], preferred_element_type=jnp.float32
    ).astype(jnp.bfloat16)
    cross_text = jnp.einsum(
        "itd,jdc->jitc", text_states, input_low[4:6], preferred_element_type=jnp.float32
    ).astype(jnp.bfloat16)
    cross_mixed, cross_totals = attend_forward(cross_query, cross_text[0], cross_text[1], masked)
    second_sum = first_sum + attention_out(cross_mixed, 1)
    normed_three, norm_three_back = jax.vjp(normalize, second_sum, gain_rows[4], gain_rows[5])
    rows_three = spread_rows(normed_three.astype(jnp.bfloat16))
    hidden_pre = jnp.einsum(
        "isd,df->isf", rows_three, hidden_low[0], preferred_element_type=jnp.float32
    )
    hidden_float, gelu_back = jax.vjp(gelu_tanh, hidden_pre)
    hidden_act = hidden_float.astype(jnp.bfloat16)
    layer_out = second_sum + collect_rows(
        jnp.einsum("isf,df->isd", hidden_act, hidden_low[1], preferred_element_type=jnp.float32)
    )
    input_low, output_low, hidden_low = lower_again(input_weights, output_weights, hidden_weights)
    cotangent_float = cotangent.astype(jnp.float32)
    out_rows = spread_grads(cotangent_float)
    (hidden_grad_pre,) = gelu_back(
        jnp.einsum("isd,df->isf", out_rows, hidden_low[1], preferred_element_type=jnp.float32)
    )
    hidden_pre_low = hidden_grad_pre.astype(jnp.bfloat16)
    down_grad = jnp.einsum("isd,isf->df", out_rows, hidden_act, preferred_element_type=jnp.float32)
    up_grad = jnp.einsum(
        "isd,isf->df", rows_three, hidden_pre_low, preferred_element_type=jnp.float32
    )
    normed_three_grad = collect_grads(
        jnp.einsum("isf,df->isd", hidden_pre_low, hidden_low[0], preferred_element_type=jnp.float32)
    )
    back_three, gain_five, shift_six = norm_three_back(normed_three_grad)
    residual_grad = cotangent_float + back_three
    cross_rows = spread_grads(residual_grad)
    cross_mixed_grad = jnp.einsum(
        "isd,dc->isc", cross_rows, output_low[1], preferred_element_type=jnp.float32
    ).astype(jnp.bfloat16)
    cross_out_grad = jnp.einsum(
        "isd,isc->dc", cross_rows, cross_mixed, preferred_element_type=jnp.float32
    )
    cross_query_grad, cross_key_grad, cross_value_grad = attend_backward(
        cross_query, cross_text[0], cross_text[1], cross_totals, cross_mixed_grad, masked
    )
    cross_text_grad = jnp.stack([cross_key_grad, cross_value_grad])
    cross_in_grad = jnp.concatenate(
        [
            jnp.einsum(
                "isd,isc->dc", rows_two, cross_query_grad, preferred_element_type=jnp.float32
            )[None],
            jnp.einsum(
                "itd,jitc->jdc", text_states, cross_text_grad, preferred_element_type=jnp.float32
            ),
        ],
        0,
    )
    text_gradient = lax.psum_scatter(
        jnp.einsum(
            "jitc,jdc->itd", cross_text_grad, input_low[4:6], preferred_element_type=jnp.float32
        ),
        "mp",
        scatter_dimension=1,
        tiled=True,
    )
    normed_two_grad = collect_grads(
        jnp.einsum(
            "isc,dc->isd", cross_query_grad, input_low[3], preferred_element_type=jnp.float32
        )
    )
    back_two, gain_three, shift_four = norm_two_back(normed_two_grad)
    residual_grad = residual_grad + back_two
    self_rows = spread_grads(residual_grad)
    self_mixed_grad = jnp.einsum(
        "isd,dc->isc", self_rows, output_low[0], preferred_element_type=jnp.float32
    ).astype(jnp.bfloat16)
    self_out_grad = jnp.einsum(
        "isd,isc->dc", self_rows, self_mixed, preferred_element_type=jnp.float32
    )
    query_grad, key_grad, value_grad = attend_backward(
        self_proj[0], self_proj[1], self_proj[2], self_totals, self_mixed_grad, causal
    )
    self_grads = jnp.stack([query_grad, key_grad, value_grad])
    self_in_grad = jnp.einsum(
        "isd,jisc->jdc", rows_one, self_grads, preferred_element_type=jnp.float32
    )
    normed_one_grad = collect_grads(
        jnp.einsum("jisc,jdc->isd", self_grads, input_low[0:3], preferred_element_type=jnp.float32)
    )
    back_one, gain_one, shift_two = norm_one_back(normed_one_grad)
    image_gradient = residual_grad + back_one
    gains_shard = lax.psum_scatter(
        jnp.stack([gain_one, shift_two, gain_three, shift_four, gain_five, shift_six]),
        ("dp", "mp"),
        scatter_dimension=1,
        tiled=True,
    )
    input_shard, output_shard, hidden_shard = (
        lax.psum_scatter(
            jnp.concatenate([self_in_grad, cross_in_grad], 0), "dp", scatter_dimension=1, tiled=True
        ),
        lax.psum_scatter(
            jnp.stack([self_out_grad, cross_out_grad]), "dp", scatter_dimension=1, tiled=True
        ),
        lax.psum_scatter(jnp.stack([up_grad, down_grad]), "dp", scatter_dimension=1, tiled=True),
    )
    square_total = jnp.sum(input_shard * input_shard) + jnp.sum(output_shard * output_shard)
    square_total = (
        square_total + jnp.sum(hidden_shard * hidden_shard) + jnp.sum(gains_shard * gains_shard)
    )
    global_norm = jnp.sqrt(lax.psum(square_total, ("dp", "mp")))
    factor = jnp.minimum(1.0, CLIP_LIMIT / (global_norm + 1e-06))
    input_updated, input_moment, input_square = adam_update(
        input_weights, input_shard, input_momentum, input_variance, factor, LEARN_RATE, WEIGHT_DECAY
    )
    output_updated, output_moment, output_square = adam_update(
        output_weights,
        output_shard,
        output_momentum,
        output_variance,
        factor,
        LEARN_RATE,
        WEIGHT_DECAY,
    )
    hidden_updated, hidden_moment, hidden_square = adam_update(
        hidden_weights,
        hidden_shard,
        hidden_momentum,
        hidden_variance,
        factor,
        LEARN_RATE,
        WEIGHT_DECAY,
    )
    gains_updated, gains_moment, gains_square = adam_update(
        norm_gains, gains_shard, gains_momentum, gains_variance, factor, GAIN_RATE, 0.0
    )
    return (
        layer_out,
        image_gradient,
        text_gradient,
        global_norm,
        input_updated,
        output_updated,
        hidden_updated,
        gains_updated,
        input_moment,
        output_moment,
        hidden_moment,
        gains_moment,
        input_square,
        output_square,
        hidden_square,
        gains_square,
    )


def solution(mesh):
    placed = (
        P("dp", "mp", None),
        P("dp", None, None),
        P("dp", None),
        P("dp", "mp", None),
        P(None, "dp", "mp"),
        P(None, "dp", "mp"),
        P(None, "dp", "mp"),
        P(None, ("dp", "mp")),
        P(None, "dp", "mp"),
        P(None, "dp", "mp"),
        P(None, "dp", "mp"),
        P(None, ("dp", "mp")),
        P(None, "dp", "mp"),
        P(None, "dp", "mp"),
        P(None, "dp", "mp"),
        P(None, ("dp", "mp")),
    )
    return jax.shard_map(
        per_device,
        mesh=mesh,
        in_specs=placed,
        out_specs=(
            P("dp", "mp", None),
            P("dp", "mp", None),
            P("dp", "mp", None),
            P(),
            P(None, "dp", "mp"),
            P(None, "dp", "mp"),
            P(None, "dp", "mp"),
            P(None, ("dp", "mp")),
            P(None, "dp", "mp"),
            P(None, "dp", "mp"),
            P(None, "dp", "mp"),
            P(None, ("dp", "mp")),
            P(None, "dp", "mp"),
            P(None, "dp", "mp"),
            P(None, "dp", "mp"),
            P(None, ("dp", "mp")),
        ),
        check_vma=False,
    )
```

profile of v0, /device:TPU:0, one launch (start us, length us, event | category | flops | bytes accessed | tf_op | source)
XLA Modules:
  0.0 2093.7 jit_solution(549006168456044598)
XLA Ops:
  9.7 71.0 %all-gather = f32[32,32,6]{1,2,0:T(8,128)S(1)} all-gather(f32[1,32,6]{1,2,0:T(8,128)S(1)} %bitcast.455), channel_id=1, replica_groups=mesh['dp'=8,'mp'=4] {'dp','mp'}, dimensions={0}, use_global_device_ids=true | all-gather | bytes 25344 | tf_op jit(solution)/shard_map/all_gather | solution.py:218
  85.0 76.4 %all-gather.11.cloned.1.call-done = bf16[2,1024,1024]{2,1,0:T(8,128)(2,1)} async-done(((bf16[2,256,1024]{2,1,0:T(8,128)(2,1)}), bf16[2,1024,1024]{2,1,0:T(8,128)(2,1)}) %all-gather.11.cloned.1.call-update) | async-done | bytes 4194320 | tf_op jit(solution)/shard_map/all_gather | solution.py:40
  172.8 43.3 %while.119 = (s32[]{:T(128)}, bf16[2,2,512,4,64]{2,1,4,3,0:T(2,128)(2,1)}, f32[2,2,4,512]{3,2,1,0:T(4,128)S(1)}, bf16[2,2,512,4,64]{2,4,3,1,0:T(8,128)(2,1)}, bf...) while((s32[]{:T(128)}, ...), condition=%wide.region_7.8_spmd.clone, body=%wide.region_2.7_spmd.clone.sunk | while | flops 562690560 | bytes 33132860 | solution.py:111
  175.2 17.9 while.124
  196.8 17.9 while.124
  224.0 143.1 %reduce-scatter.14.cloned.1.call-done = f32[2,256,1024]{2,1,0:T(8,128)} async-done(((f32[2,1024,1024]{2,1,0:T(8,128)}), f32[2,256,1024]{2,1,0:T(8,128)}) %reduce-scatter.14.cloned.1.call-update) | async-done | bytes 2097168 | tf_op jit(solution)/shard_map/reduce_scatter | solution.py:44
  375.4 78.7 %all-gather.17.cloned.1.call-done = bf16[2,1024,1024]{2,1,0:T(8,128)(2,1)} async-done(((bf16[2,256,1024]{2,1,0:T(8,128)(2,1)}), bf16[2,1024,1024]{2,1,0:T(8,128)(2,1)}) %all-gather.17.cloned.1.call-update) | async-done | bytes 4194320 | tf_op jit(solution)/shard_map/all_gather | solution.py:40
  469.3 22.9 %while.115 = (s32[]{:T(128)}, bf16[2,2,512,4,64]{2,1,4,3,0:T(2,128)(2,1)}, f32[2,2,4,512]{3,2,1,0:T(4,128)}, bf16[2,2,512,4,64]{2,4,3,1,0:T(8,128)(2,1)}, bf16[2...) while((s32[]{:T(128)}, ...), condition=%wide.region_16.17_spmd, body=%wide.region_11.16_spmd.sunk | while | flops 69335168 | bytes 6261232 | solution.py:111
  502.9 140.9 %reduce-scatter.16.cloned.1.call-done = f32[2,256,1024]{2,1,0:T(8,128)} async-done(((f32[2,1024,1024]{2,1,0:T(8,128)}), f32[2,256,1024]{2,1,0:T(8,128)}) %reduce-scatter.16.cloned.1.call-update) | async-done | bytes 2097168 | tf_op jit(solution)/shard_map/reduce_scatter | solution.py:44
  649.4 34.4 %all-gather.21.cloned.1.call-done = bf16[2,1024,1024]{2,1,0:T(8,128)(2,1)} async-done(((bf16[2,128,1024]{2,1,0:T(8,128)(2,1)}), bf16[2,1024,1024]{2,1,0:T(8,128)(2,1)}) %all-gather.21.cloned.1.call-update) | async-done | bytes 4194320 | tf_op jit(solution)/shard_map/all_gather | solution.py:59
  683.8 82.9 %all-gather.19.cloned.1.call-done = bf16[2,1024,1024]{2,1,0:T(8,128)(2,1)} async-done(((bf16[2,256,1024]{2,1,0:T(8,128)(2,1)}), bf16[2,1024,1024]{2,1,0:T(8,128)(2,1)}) %all-gather.19.cloned.1.call-update) | async-done | bytes 4194320 | tf_op jit(solution)/shard_map/all_gather | solution.py:40
  766.7 10.8 fusion.104
  777.5 70.1 %all-gather.23.cloned.1.call-done = bf16[2,1024,1024]{2,1,0:T(8,128)(2,1)} async-done(((bf16[2,256,1024]{2,1,0:T(8,128)(2,1)}), bf16[2,1024,1024]{2,1,0:T(8,128)(2,1)}) %all-gather.23.cloned.1.call-update) | async-done | bytes 4194320 | tf_op jit(solution)/shard_map/all_gather | solution.py:48
  847.6 13.8 fusion.80
  870.6 12.6 fusion.105
  883.3 130.2 %reduce-scatter.20.cloned.1.call-done = f32[2,256,1024]{2,1,0:T(8,128)} async-done(((f32[2,1024,1024]{2,1,0:T(8,128)}), f32[2,256,1024]{2,1,0:T(8,128)}) %reduce-scatter.20.cloned.1.call-update) | async-done | bytes 2097168 | tf_op jit(solution)/shard_map/reduce_scatter | solution.py:52
  1016.5 144.6 %reduce-scatter.18.cloned.1.call-done = f32[2,256,1024]{2,1,0:T(8,128)} async-done(((f32[2,1024,1024]{2,1,0:T(8,128)}), f32[2,256,1024]{2,1,0:T(8,128)}) %reduce-scatter.18.cloned.1.call-update) | async-done | bytes 2097168 | tf_op jit(solution)/shard_map/reduce_scatter | solution.py:44
  1168.4 81.3 %all-gather.25.cloned.1.call-done = bf16[2,1024,1024]{2,1,0:T(8,128)(2,1)} async-done(((bf16[2,256,1024]{2,1,0:T(8,128)(2,1)}), bf16[2,1024,1024]{2,1,0:T(8,128)(2,1)}) %all-gather.25.cloned.1.call-update) | async-done | bytes 4194320 | tf_op jit(solution)/shard_map/all_gather | solution.py:48
  1261.1 29.5 %while.117 = (s32[]{:T(128)}, bf16[2,2,512,4,64]{2,1,4,3,0:T(2,128)(2,1)}, bf16[2,128,4,64]{1,3,2,0:T(8,128)(2,1)}, bf16[2,128,4,64]{1,3,2,0:T(8,128)(2,1)}, bf1...) while((s32[]{:T(128)}, ...), condition=%wide.region_28.29_spmd, body=%wide.region_24.28_spmd.sunk | while | flops 170621056 | bytes 13773423 | solution.py:177
  1298.5 143.1 %reduce-scatter.22.cloned.1.call-done = f32[2,256,1024]{2,1,0:T(8,128)} async-done(((f32[2,1024,1024]{2,1,0:T(8,128)}), f32[2,256,1024]{2,1,0:T(8,128)}) %reduce-scatter.22.cloned.1.call-update) | async-done | bytes 2097168 | tf_op jit(solution)/shard_map/reduce_scatter | solution.py:52
  1449.0 7.7 convolution_bitcast_fusion.3
  1456.8 7.5 convolution_bitcast_fusion.2
  1468.5 61.7 %all-gather.27.cloned.1.call-done = bf16[2,1024,1024]{2,1,0:T(8,128)(2,1)} async-done(((bf16[2,256,1024]{2,1,0:T(8,128)(2,1)}), bf16[2,1024,1024]{2,1,0:T(8,128)(2,1)}) %all-gather.27.cloned.1.call-update) | async-done | bytes 4194320 | tf_op jit(solution)/shard_map/all_gather | solution.py:48
  1540.4 74.2 %while.121 = (s32[]{:T(128)}, bf16[2,2,512,4,64]{2,4,3,1,0:T(8,128)(2,1)}, bf16[2,1024,4,64]{1,3,2,0:T(8,128)(2,1)}, bf16[2,1024,4,64]{1,3,2,0:T(8,128)(2,1)}, b...) while((s32[]{:T(128)}, ...), condition=%wide.region_36.37_spmd.clone, body=%wide.region_32.36_spmd.clone.sunk | while | flops 1376254464 | bytes 95253072 | solution.py:177
  1546.1 27.4 %while.125 = (s32[]{:T(128)}, f32[1024,4,64]{0,2,1:T(8,128)S(1)}, f32[1024,4,64]{0,2,1:T(8,128)}, bf16[2,512,4,64]{1,3,2,0:T(8,128)(2,1)}, bf16[2,512,4,64]{1,3,...) while((s32[]{:T(128)}, f32[1024,4,64]{0,2,1:T(8,128)S(1)}, ...), condition=%wide.region_35.35_spmd.clone, body=%wide.region_33.34_spmd.clone.sunk | while | flops 1375730176 | bytes 86831424 | solution.py:171
  1583.0 27.3 %while.125 = (s32[]{:T(128)}, f32[1024,4,64]{0,2,1:T(8,128)S(1)}, f32[1024,4,64]{0,2,1:T(8,128)}, bf16[2,512,4,64]{1,3,2,0:T(8,128)(2,1)}, bf16[2,512,4,64]{1,3,...) while((s32[]{:T(128)}, f32[1024,4,64]{0,2,1:T(8,128)S(1)}, ...), condition=%wide.region_35.35_spmd.clone, body=%wide.region_33.34_spmd.clone.sunk | while | flops 1375730176 | bytes 86831424 | solution.py:171
  1624.3 9.0 convolution_bitcast_fusion.1
  1659.2 117.5 %reduce-scatter.24.cloned.1.call-done = f32[2,256,1024]{2,1,0:T(8,128)} async-done(((f32[2,1024,1024]{2,1,0:T(8,128)}), f32[2,256,1024]{2,1,0:T(8,128)}) %reduce-scatter.24.cloned.1.call-update) | async-done | bytes 2097168 | tf_op jit(solution)/shard_map/reduce_scatter | solution.py:52
  1784.0 38.2 %reduce-scatter.30.cloned.1.call-done = f32[2,128,256]{2,1,0:T(8,128)} async-done(((f32[2,1024,256]{2,1,0:T(8,128)}), f32[2,128,256]{2,1,0:T(8,128)}) %reduce-scatter.30.cloned.1.call-update) | async-done | bytes 262160 | tf_op jit(solution)/shard_map/reduce_scatter | solution.py:342
  1823.8 63.4 %reduce-scatter.28.cloned.1.call-done = f32[6,128,256]{1,2,0:T(8,128)} async-done(((f32[6,1024,256]{1,2,0:T(8,128)}), f32[6,128,256]{1,2,0:T(8,128)}) %reduce-scatter.28.cloned.1.call-update) | async-done | bytes 786448 | tf_op jit(solution)/shard_map/reduce_scatter | solution.py:339
  1891.0 133.5 %reduce-scatter.34.cloned.1.call-done = f32[32,6]{1,0:T(8,128)} async-done(((f32[1024,6]{1,0:T(8,128)}), f32[32,6]{1,0:T(8,128)}) %reduce-scatter.34.cloned.1.call-update) | async-done | bytes 784
  2030.9 38.0 %psum.7 = f32[]{:T(128)} all-reduce(f32[]{:T(128)S(6)} %add.309), channel_id=1, replica_groups=mesh['dp'=8,'mp'=4] {'dp','mp'}, use_global_device_ids=true, to_apply=%region_55.56 | all-reduce | flops 1 | bytes 8 | tf_op jit(solution)/shard_map/psum | solution.py:351
  (520 shorter events, 371.5 us)
Async XLA Ops:
  7.2 365.8 %copy-start = (bf16[2,128,1024]{2,1,0:T(8,128)(2,1)S(1)}, bf16[2,128,1024]{2,1,0:T(8,128)(2,1)}, u32[]{:S(2)}) copy-start(bf16[2,128,1024]{2,1,0:T(8,128)(2,1)} %param.33) | copy-start | bytes 1572868
  7.2 77.8 %all-gather.13.cloned.1.call-start = ((), (), s32[]{:S(2)}) async-start(), calls=%async_computation.12 | async-start | bytes 3538944 | tf_op jit(solution)/shard_map/all_gather | solution.py:57
  9.7 151.8 %all-gather.11.cloned.1.call-start = ((), (), s32[]{:S(2)}) async-start(), calls=%async_computation.11 | async-start | bytes 5242880 | tf_op jit(solution)/shard_map/all_gather | solution.py:40
  84.2 133.7 %all-gather.15.cloned.1.call-start = ((), (), s32[]{:S(2)}) async-start(), calls=%async_computation.13 | async-start | bytes 1179648 | tf_op jit(solution)/shard_map/all_gather | solution.py:58
  85.0 282.1 %reduce-scatter.14.cloned.1.call-start = ((), (), s32[]{:S(2)}) async-start(), calls=%async_computation.14 | async-start | bytes 10485760 | tf_op jit(solution)/shard_map/reduce_scatter | solution.py:44
  223.9 147.1 %copy-start.41 = (f32[1,1024]{1,0:T(1,128)S(1)}, f32[1,1024]{1,0:T(1,128)}, u32[]{:S(2)}) copy-start(f32[1,1024]{1,0:T(1,128)} %get-tuple-element.995) | copy-start | bytes 12292
  223.9 147.1 %copy-start.60 = (f32[1,1024]{1,0:T(1,128)S(1)}, f32[1,1024]{1,0:T(1,128)}, u32[]{:S(2)}) copy-start(f32[1,1024]{1,0:T(1,128)} %get-tuple-element.994) | copy-start | bytes 12292
  224.0 230.1 %all-gather.17.cloned.1.call-start = ((), (), s32[]{:S(2)}) async-start(), calls=%async_computation.15 | async-start | bytes 5242880 | tf_op jit(solution)/shard_map/all_gather | solution.py:40
  369.2 274.6 %copy-start.2 = (f32[2,256,1024]{2,1,0:T(8,128)}, f32[2,256,1024]{2,1,0:T(8,128)S(1)}, u32[]{:S(2)}) copy-start(f32[2,256,1024]{2,1,0:T(8,128)S(1)} %get-tuple-element.967) | copy-start | bytes 6291460
  372.4 271.4 %reduce-scatter.16.cloned.1.call-start = ((), (), s32[]{:S(2)}) async-start(), calls=%async_computation.16 | async-start | bytes 10485760 | tf_op jit(solution)/shard_map/reduce_scatter | solution.py:44
  500.7 183.1 %all-gather.21.cloned.1.call-start = ((), (), s32[]{:S(2)}) async-start(), calls=%async_computation.18 | async-start | bytes 4718592 | tf_op jit(solution)/shard_map/all_gather | solution.py:59
  502.9 144.2 %copy-start.47 = (f32[1,1024]{1,0:T(1,128)S(1)}, f32[1,1024]{1,0:T(1,128)}, u32[]{:S(2)}) copy-start(f32[1,1024]{1,0:T(1,128)} %get-tuple-element.992) | copy-start | bytes 12292
  502.9 144.2 %copy-start.59 = (f32[1,1024]{1,0:T(1,128)S(1)}, f32[1,1024]{1,0:T(1,128)}, u32[]{:S(2)}) copy-start(f32[1,1024]{1,0:T(1,128)} %get-tuple-element.993) | copy-start | bytes 12292
  502.9 263.9 %all-gather.19.cloned.1.call-start = ((), (), s32[]{:S(2)}) async-start(), calls=%async_computation.17 | async-start | bytes 5242880 | tf_op jit(solution)/shard_map/all_gather | solution.py:40
  648.4 199.2 %all-gather.23.cloned.1.call-start = ((), (), s32[]{:S(2)}) async-start(), calls=%async_computation.20 | async-start | bytes 5242880 | tf_op jit(solution)/shard_map/all_gather | solution.py:48
  649.2 364.4 %reduce-scatter.20.cloned.1.call-start = ((), (), s32[]{:S(2)}) async-start(), calls=%async_computation.21 | async-start | bytes 10485760 | tf_op jit(solution)/shard_map/reduce_scatter | solution.py:52
  870.4 290.7 %reduce-scatter.18.cloned.1.call-start = ((), (), s32[]{:S(2)}) async-start(), calls=%async_computation.19 | async-start | bytes 10485760 | tf_op jit(solution)/shard_map/reduce_scatter | solution.py:44
  883.3 130.3 %copy-start.5 = (f32[2,256,1024]{2,1,0:T(8,128)S(1)}, f32[2,256,1024]{2,1,0:T(8,128)}, u32[]{:S(2)}) copy-start(f32[2,256,1024]{2,1,0:T(8,128)} %copy-done.4) | copy-start | bytes 6291460
  883.3 366.5 %all-gather.25.cloned.1.call-start = ((), (), s32[]{:S(2)}) async-start(), calls=%async_computation.22 | async-start | bytes 5242880 | tf_op jit(solution)/shard_map/all_gather | solution.py:48
  1168.1 273.5 %reduce-scatter.22.cloned.1.call-start = ((), (), s32[]{:S(2)}) async-start(), calls=%async_computation.23 | async-start | bytes 10485760 | tf_op jit(solution)/shard_map/reduce_scatter | solution.py:52
  1298.4 143.2 %copy-start.3 = (f32[2,256,1024]{2,1,0:T(8,128)S(1)}, f32[2,256,1024]{2,1,0:T(8,128)}, u32[]{:S(2)}) copy-start(f32[2,256,1024]{2,1,0:T(8,128)} %copy-done.2) | copy-start | bytes 6291460
  1298.4 143.2 %copy-start.42 = (f32[1,1024]{1,0:T(1,128)S(1)}, f32[1,1024]{1,0:T(1,128)}, u32[]{:S(2)}) copy-start(f32[1,1024]{1,0:T(1,128)} %get-tuple-element.995) | copy-start | bytes 12292
  1298.4 143.2 %copy-start.44 = (f32[2,256]{1,0:T(2,128)S(1)}, f32[2,256]{1,0:T(2,128)}, u32[]{:S(2)}) copy-start(f32[2,256]{1,0:T(2,128)} %copy-done.43) | copy-start | bytes 6148
  1298.4 146.0 %copy-start.57 = (f32[2,256]{1,0:T(2,128)S(1)}, f32[2,256]{1,0:T(2,128)}, u32[]{:S(2)}) copy-start(f32[2,256]{1,0:T(2,128)} %copy-done.56) | copy-start | bytes 6148
  1298.5 146.0 %copy-start.49 = (f32[2,256]{1,0:T(2,128)S(1)}, f32[2,256]{1,0:T(2,128)}, u32[]{:S(2)}) copy-start(f32[2,256]{1,0:T(2,128)} %copy-done.48) | copy-start | bytes 6148
  1298.5 231.7 %all-gather.27.cloned.1.call-start = ((), (), s32[]{:S(2)}) async-start(), calls=%async_computation.24 | async-start | bytes 5242880 | tf_op jit(solution)/shard_map/all_gather | solution.py:48
  1448.5 208.6 %reduce-scatter.32.cloned.1.call-start = ((), (), s32[]{:S(2)}) async-start(), calls=%async_computation.29 | async-start | bytes 9437184 | tf_op jit(solution)/shard_map/reduce_scatter | solution.py:345
  1468.4 308.3 %reduce-scatter.24.cloned.1.call-start = ((), (), s32[]{:S(2)}) async-start(), calls=%async_computation.25 | async-start | bytes 10485760 | tf_op jit(solution)/shard_map/reduce_scatter | solution.py:52
  1633.4 188.8 %reduce-scatter.30.cloned.1.call-start = ((), (), s32[]{:S(2)}) async-start(), calls=%async_computation.28 | async-start | bytes 2359296 | tf_op jit(solution)/shard_map/reduce_scatter | solution.py:342
  1641.2 246.0 %reduce-scatter.28.cloned.1.call-start = ((), (), s32[]{:S(2)}) async-start(), calls=%async_computation.27 | async-start | bytes 7077888 | tf_op jit(solution)/shard_map/reduce_scatter | solution.py:339
  1653.1 371.4 %reduce-scatter.34.cloned.1.call-start = ((), (), s32[]{:S(2)}) async-start(), calls=%async_computation.30 | async-start | bytes 540672
  1781.3 304.0 %reduce-scatter.26.cloned.1.call-start = ((), (), s32[]{:S(2)}) async-start(), calls=%async_computation.26 | async-start | bytes 1310720 | tf_op jit(solution)/shard_map/reduce_scatter | solution.py:298
  (76 other events, 1967.2 us)
Sparse Core Ops, SparseCore 0:
  10.5 35.6 all-gather.12
  84.3 77.0 all-gather.10
  163.9 22.0 all-gather.14
  224.1 142.9 reduce-scatter.13
  372.6 81.4 all-gather.16
  500.8 142.9 reduce-scatter.15
  646.3 37.4 all-gather.20
  685.9 80.7 all-gather.18
  768.3 79.2 all-gather.22
  870.5 142.9 reduce-scatter.19
  1015.9 145.1 reduce-scatter.17
  1168.2 81.4 all-gather.24
  1298.6 142.9 reduce-scatter.21
  1448.6 81.4 all-gather.26
  1533.4 69.7 reduce-scatter.31
  1633.5 143.1 reduce-scatter.23
  1780.2 41.9 reduce-scatter.29
  1825.4 61.7 reduce-scatter.27
  1890.0 134.4 reduce-scatter.33
  2027.2 23.7 reduce-scatter.25
where the time goes:
time: 2110 us; the launch traced here: 2090 us
  waiting for transfers between devices  1540 us (73%)
  matrix products  191 us (9%)
  local copies, waits for them, and re-layouts  121 us (6%)
  blocking collectives  109 us (5%)
  other arithmetic  99.7 us (5%)
    reduce_scatter x3, waiting for transfers between devices, collect_rows(): lax.psum_scatter(partial_value, 'mp', scatter_dimension=1, tiled=True)  429 us
    reduce_scatter x3, waiting for transfers between devices, collect_grads(): lax.psum_scatter(partial_value, 'mp', scatter_dimension=1, tiled=True)  391 us
    all_gather x3, waiting for transfers between devices, spread_rows(): return lax.all_gather(normed, 'mp', axis=1, tiled=True)  238 us
    all_gather x3, waiting for transfers between devices, spread_grads(): lax.all_gather(residual.astype(jnp.bfloat16), 'mp', axis=1, tiled=True)  213 us
    unnamed x21, waiting for transfers between devices  134 us
    all_gather x1, blocking collectives, per_device(): gain_rows = lax.all_gather(norm_gains, ('dp', 'mp'), axis=1, tiled=True)  71 us
    reduce_scatter x1, waiting for transfers between devices, per_device(): lax.psum_scatter(jnp.concatenate([self_in_grad, cross_in_grad], 0), 'dp',...  63.4 us
  transfers between devices with their start and end apart: 20, of which 16 were waited for; matrix products, arithmetic and copies ran while one was open for 13% of the time, Pallas kernels for 0%

commit v1 on v0

v1 whole, which is shorter than its diff:
```python
import math
import jax, jax.numpy as jnp
from jax import lax
from jax.experimental import pallas as pl
from jax.experimental.pallas import tpu as pltpu
BF=jnp.bfloat16; F32=jnp.float32
HEAD_DIM=64; MASKED=-1e30; BQ=256
NT=(((1,),(1,)),((),())); NN=(((1,),(0,)),((),())); TN=(((0,),(0,)),((),()))
def dot(a,b,dims): return lax.dot_general(a,b,dims,preferred_element_type=F32)

def place_of(block, core, half):
    return pl.multiple_of(((block % 2) ^ core) * half + (block // 2) * 128, 128)

def self_fwd_kernel(core_ref, q_ref, k_ref, v_ref, o_ref, l_ref, qs, ks, vs, *, seq):
    core=core_ref[0]; half=seq//2
    for b in range(seq//128):
        at=pl.ds(place_of(b,core,half),128); to=slice(b*128,b*128+128)
        qs[to,:]=(q_ref[at,:].astype(F32)*0.125).astype(BF)
        ks[to,:]=k_ref[at,:]
        vs[to,:]=v_ref[at,:]
    low=lax.broadcasted_iota(jnp.int32,(1,128),1)<HEAD_DIM
    for i in range(seq//BQ):
        n=(i+1)*BQ
        q=qs[i*BQ:n,:]
        outs=[]
        for h in range(2):
            keep=low if h==0 else ~low
            kh=jnp.where(keep,ks[0:n,:],jnp.zeros((),BF))
            s=dot(kh,q,NT)
            tri=lax.broadcasted_iota(jnp.int32,(BQ,BQ),0)<=lax.broadcasted_iota(jnp.int32,(BQ,BQ),1)
            diag=jnp.where(tri,s[n-BQ:,:],MASKED)
            s=diag if n==BQ else jnp.concatenate([s[:n-BQ],diag],0)
            m=jnp.max(s,axis=0,keepdims=True)
            e=jnp.exp(s-m)
            t=jnp.sum(e,axis=0,keepdims=True)
            l_ref[0,h:h+1,i*BQ:n]=m+jnp.log(t)
            vh=vs[0:n,h*64:h*64+64]
            o=dot(vh,e.astype(BF),TN)
            outs.append(o*(1.0/t))
        o=jnp.concatenate(outs,0).T.astype(BF)
        for j in range(BQ//128):
            o_ref[pl.ds(place_of(i*(BQ//128)+j,core,half),128),:]=o[j*128:j*128+128]

def self_bwd_kernel(core_ref, q_ref, k_ref, v_ref, g_ref, l_ref, dq_ref, dk_ref, dv_ref, qs, ks, vs, gs, dka, dva, *, seq):
    core=core_ref[0]; half=seq//2
    for b in range(seq//128):
        at=pl.ds(place_of(b,core,half),128); to=slice(b*128,b*128+128)
        qs[to,:]=(q_ref[at,:].astype(F32)*0.125).astype(BF)
        ks[to,:]=k_ref[at,:]
        vs[to,:]=v_ref[at,:]
        gs[to,:]=g_ref[at,:]
    dka[...]=jnp.zeros_like(dka); dva[...]=jnp.zeros_like(dva)
    low=lax.broadcasted_iota(jnp.int32,(1,128),1)<HEAD_DIM
    zero=jnp.zeros((),BF)
    for i in range(seq//BQ):
        n=(i+1)*BQ; rows=slice(i*BQ,n)
        q=qs[rows,:]; g=gs[rows,:]
        ps=[]; dss=[]
        for h in range(2):
            keep=low if h==0 else ~low
            kh=jnp.where(keep,ks[0:n,:],zero)
            vh=jnp.where(keep,vs[0:n,:],zero)
            s=dot(kh,q,NT)
            tri=lax.broadcasted_iota(jnp.int32,(BQ,BQ),0)<=lax.broadcasted_iota(jnp.int32,(BQ,BQ),1)
            diag=jnp.where(tri,s[n-BQ:,:],MASKED)
            s=diag if n==BQ else jnp.concatenate([s[:n-BQ],diag],0)
            p=jnp.exp(s-l_ref[0,h:h+1,rows])
            dp=dot(vh,g,NT)
            delta=jnp.sum(p*dp,axis=0,keepdims=True)
            ds=(p*(dp-delta)).astype(BF)
            ps.append(p.astype(BF)); dss.append(ds)
        qa=jnp.concatenate([jnp.where(low,q,zero),jnp.where(low,zero,q)],0)
        ga=jnp.concatenate([jnp.where(low,g,zero),jnp.where(low,zero,g)],0)
        dva[0:n,:]+=dot(jnp.concatenate(ps,1),ga,NN)
        dka[0:n,:]+=dot(jnp.concatenate(dss,1),qa,NN)
        k=ks[0:n,:]
        dqt=jnp.concatenate([dot(ks[0:n,0:64],dss[0],TN),dot(ks[0:n,64:128],dss[1],TN)],0)
        dq=(dqt.T*0.125).astype(BF)
        for j in range(BQ//128):
            dq_ref[pl.ds(place_of(i*(BQ//128)+j,core,half),128),:]=dq[j*128:j*128+128]
    for b in range(seq//128):
        at=pl.ds(place_of(b,core,half),128)
        dk_ref[at,:]=dka[b*128:b*128+128,:].astype(BF)
        dv_ref[at,:]=dva[b*128:b*128+128,:].astype(BF)

def cross_fwd_kernel(mask_ref, q_ref, k_ref, v_ref, o_ref, l_ref, *, seq):
    low=lax.broadcasted_iota(jnp.int32,(1,128),1)<HEAD_DIM
    zero=jnp.zeros((),BF)
    valid=mask_ref[:,0:1]>0
    k=k_ref[...]; v=v_ref[...]
    for i in range(seq//BQ):
        rows=slice(i*BQ,(i+1)*BQ)
        q=(q_ref[rows,:].astype(F32)*0.125).astype(BF)
        outs=[]
        for h in range(2):
            kh=jnp.where(low if h==0 else ~low,k,zero)
            s=jnp.where(valid,dot(kh,q,NT),MASKED)
            m=jnp.max(s,axis=0,keepdims=True)
            e=jnp.exp(s-m)
            t=jnp.sum(e,axis=0,keepdims=True)
            l_ref[0,h:h+1,rows]=m+jnp.log(t)
            outs.append(dot(v[:,h*64:h*64+64],e.astype(BF),TN)*(1.0/t))
        o_ref[rows,:]=jnp.concatenate(outs,0).T.astype(BF)

def cross_bwd_kernel(mask_ref, q_ref, k_ref, v_ref, g_ref, l_ref, dq_ref, dk_ref, dv_ref, *, seq):
    low=lax.broadcasted_iota(jnp.int32,(1,128),1)<HEAD_DIM
    zero=jnp.zeros((),BF)
    valid=mask_ref[:,0:1]>0
    k=k_ref[...]; v=v_ref[...]
    dk=jnp.zeros(k.shape,F32); dv=jnp.zeros(k.shape,F32)
    for i in range(seq//BQ):
        rows=slice(i*BQ,(i+1)*BQ)
        q=(q_ref[rows,:].astype(F32)*0.125).astype(BF); g=g_ref[rows,:]
        ps=[]; dss=[]; dqs=[]
        for h in range(2):
            keep=low if h==0 else ~low
            kh=jnp.where(keep,k,zero); vh=jnp.where(keep,v,zero)
            s=jnp.where(valid,dot(kh,q,NT),MASKED)
            p=jnp.exp(s-l_ref[0,h:h+1,rows])
            dp=dot(vh,g,NT)
            delta=jnp.sum(p*dp,axis=0,keepdims=True)
            ds=(p*(dp-delta)).astype(BF)
            ps.append(p.astype(BF)); dss.append(ds)
            dqs.append(dot(k[:,h*64:h*64+64],ds,TN))
        qa=jnp.concatenate([jnp.where(low,q,zero),jnp.where(low,zero,q)],0)
        ga=jnp.concatenate([jnp.where(low,g,zero),jnp.where(low,zero,g)],0)
        dv=dv+dot(jnp.concatenate(ps,1),ga,NN)
        dk=dk+dot(jnp.concatenate(dss,1),qa,NN)
        dq_ref[rows,:]=(jnp.concatenate(dqs,0).T*0.125).astype(BF)
    dk_ref[...]=dk.astype(BF); dv_ref[...]=dv.astype(BF)

def col(rows): return pl.BlockSpec((rows,128),lambda p,*_:(0,p))
LSPEC=pl.BlockSpec((1,2,None),lambda p,*_:(p,0,0))
def params(): return pltpu.CompilerParams(vmem_limit_bytes=40*1024*1024)
def self_fwd(core,q,k,v):
    seq,cols=q.shape; pairs=cols//128
    return pl.pallas_call(lambda *r: self_fwd_kernel(*r,seq=seq),
        grid_spec=pltpu.PrefetchScalarGridSpec(num_scalar_prefetch=1,grid=(pairs,),in_specs=[col(seq)]*3,
            out_specs=[col(seq),pl.BlockSpec((1,2,seq),lambda p,*_:(p,0,0))],scratch_shapes=[pltpu.VMEM((seq,128),BF)]*3),
        out_shape=[jax.ShapeDtypeStruct((seq,cols),BF),jax.ShapeDtypeStruct((pairs,2,seq),F32)],
        compiler_params=params(),
        cost_estimate=pl.CostEstimate(flops=8*seq*seq*cols*2,bytes_accessed=4*seq*cols*2,transcendentals=seq*seq*pairs),name="self_forward")(core,q,k,v)
def self_bwd(core,q,k,v,g,l):
    seq,cols=q.shape; pairs=cols//128
    return pl.pallas_call(lambda *r: self_bwd_kernel(*r,seq=seq),
        grid_spec=pltpu.PrefetchScalarGridSpec(num_scalar_prefetch=1,grid=(pairs,),in_specs=[col(seq)]*4+[pl.BlockSpec((1,2,seq),lambda p,*_:(p,0,0))],
            out_specs=[col(seq)]*3,scratch_shapes=[pltpu.VMEM((seq,128),BF)]*4+[pltpu.VMEM((seq,128),F32)]*2),
        out_shape=[jax.ShapeDtypeStruct((seq,cols),BF)]*3,
        compiler_params=params(),
        cost_estimate=pl.CostEstimate(flops=20*seq*seq*cols*2,bytes_accessed=8*seq*cols*2,transcendentals=seq*seq*pairs),name="self_backward")(core,q,k,v,g,l)
def cross_fwd(mask,q,k,v):
    seq,cols=q.shape; text=k.shape[0]; pairs=cols//128
    return pl.pallas_call(lambda *r: cross_fwd_kernel(*r,seq=seq),grid=(pairs,),
        in_specs=[pl.BlockSpec((text,128),lambda p:(0,0)),col(seq),col(text),col(text)],
        out_specs=[col(seq),pl.BlockSpec((1,2,seq),lambda p:(p,0,0))],
        out_shape=[jax.ShapeDtypeStruct((seq,cols),BF),jax.ShapeDtypeStruct((pairs,2,seq),F32)],
        compiler_params=params(),
        cost_estimate=pl.CostEstimate(flops=8*seq*text*cols*2,bytes_accessed=3*seq*cols*2,transcendentals=seq*text*pairs*2),name="cross_forward")(mask,q,k,v)
def cross_bwd(mask,q,k,v,g,l):
    seq,cols=q.shape; text=k.shape[0]; pairs=cols//128
    return pl.pallas_call(lambda *r: cross_bwd_kernel(*r,seq=seq),grid=(pairs,),
        in_specs=[pl.BlockSpec((text,128),lambda p:(0,0)),col(seq),col(text),col(text),col(seq),pl.BlockSpec((1,2,seq),lambda p:(p,0,0))],
        out_specs=[col(seq),col(text),col(text)],
        out_shape=[jax.ShapeDtypeStruct((seq,cols),BF),jax.ShapeDtypeStruct((text,cols),BF),jax.ShapeDtypeStruct((text,cols),BF)],
        compiler_params=params(),
        cost_estimate=pl.CostEstimate(flops=20*seq*text*cols*2,bytes_accessed=5*seq*cols*2,transcendentals=seq*text*pairs*2),name="cross_backward")(mask,q,k,v,g,l)


from jax.sharding import PartitionSpec as P

STEP=10
NORM_EPSILON = 1e-05
BETA_FIRST = 0.9
BETA_SECOND = 0.95
LEARN_RATE = 0.1
GAIN_RATE = 0.5
WEIGHT_DECAY = 0.1
ADAM_EPSILON = 1e-08
CLIP_LIMIT = 1.0
GELU_SCALE = 0.7978845608028654
GELU_CUBIC = 0.044715

PAIR = [(0, 1), (1, 0), (2, 3), (3, 2)]
MIDDLE = [(1, 2), (2, 1)]
OUTWARD = [(1, 0), (2, 3)]
INWARD = [(0, 1), (3, 2)]
ACROSS = [(0, 2), (1, 3), (2, 0), (3, 1)]


def swap_dp(value, size, bit):
    return lax.ppermute(value, "dp", [(i, i ^ bit) for i in range(size)])


def move_mp(value, pairs):
    return lax.ppermute(value, "mp", pairs)


def adam_update(master, gradient, momentum, variance, factor, rate, decay_rate):
    clipped = gradient * factor
    moment = BETA_FIRST * momentum + (1.0 - BETA_FIRST) * clipped
    square = BETA_SECOND * variance + (1.0 - BETA_SECOND) * clipped * clipped
    step_ratio = (
        moment
        / (1.0 - BETA_FIRST**STEP)
        / (jnp.sqrt(square / (1.0 - BETA_SECOND**STEP)) + ADAM_EPSILON)
    )
    return (master - rate * (step_ratio + decay_rate * master), moment, square)


def norm_parts(values):
    center = values - jnp.mean(values, axis=-1, keepdims=True)
    spread = jnp.mean(center * center, axis=-1, keepdims=True)
    scale = lax.rsqrt(spread + NORM_EPSILON)
    return center * scale, scale


def norm_back(values, grad, gain_row):
    unit, scale = norm_parts(values)
    scaled = grad * gain_row
    back = scale * (
        scaled
        - jnp.mean(scaled, axis=-1, keepdims=True)
        - unit * jnp.mean(scaled * unit, axis=-1, keepdims=True)
    )
    return back, jnp.sum(grad * unit, axis=0), jnp.sum(grad, axis=0)


def per_device(
    image_states, text_states, text_mask, cotangent,
    input_weights, output_weights, hidden_weights, norm_gains,
    input_momentum, output_momentum, hidden_momentum, gains_momentum,
    input_variance, output_variance, hidden_variance, gains_variance,
):
    size = lax.axis_size("dp")
    lines = lax.axis_size("mp")
    dp = lax.axis_index("dp")
    mp = lax.axis_index("mp")
    core = dp % 2
    chip = dp // 2
    chips = size // 2
    middle = (mp == 1) | (mp == 2)
    bits = []
    bit = 2
    while bit < size:
        bits.append(bit)
        bit *= 2
    width = image_states.shape[-1]
    block = width // chips
    part = width // size

    def pick(first, second):
        return jnp.where(core == 0, first, second)

    def swap_core(value):
        return swap_dp(value, size, 1)

    def reorder(value):
        return jnp.concatenate(
            [lax.dynamic_slice_in_dim(value, (chip ^ p) * block, block, value.ndim - 1) for p in range(chips)], -1
        )

    def own_half(stack):
        half = stack.shape[-1] // 2
        keep = lax.dynamic_slice_in_dim(stack, core * half, half, 2)
        send = lax.dynamic_slice_in_dim(stack, (1 - core) * half, half, 2)
        recv = swap_core(send)
        return jnp.stack([pick(keep, recv), pick(recv, keep)], 1)

    def gather_line(own):
        beside = move_mp(own, PAIR)
        near = jnp.concatenate([own, beside], -1)
        far = move_mp(near, MIDDLE)
        outer = move_mp(far, OUTWARD)
        return jnp.concatenate([near, jnp.where(middle, far, outer)], -1)

    def gather_chips(own, order):
        found = {0: own}
        for b in order:
            codes = sorted(found)
            sent = found[codes[0]] if len(codes) == 1 else jnp.concatenate([found[c] for c in codes], 1)
            got = swap_dp(sent, size, b)
            rows = own.shape[1]
            for i, c in enumerate(codes):
                found[c ^ b] = lax.slice_in_dim(got, i * rows, (i + 1) * rows, axis=1)
        return found

    def gather_group(own):
        line = gather_line(own)
        first = gather_chips(line[:, 0], bits[::-1])
        second = gather_chips(line[:, 1], bits)
        pieces = []
        for p in range(chips):
            pieces += [first[2 * p], second[2 * p]]
        return jnp.concatenate(pieces, 1)

    def scatter_chips(found, order):
        for b in reversed(order):
            codes = sorted(c for c in found if not c & b)
            sent = jnp.concatenate([found[c ^ b] for c in codes], 1)
            got = swap_dp(sent, size, b)
            found = {
                c: found[c] + lax.slice_in_dim(got, i * part, (i + 1) * part, axis=1) for i, c in enumerate(codes)
            }
        return found[0]

    def scatter_line(total):
        half = total.shape[-1] // 2
        near, away = total[..., :half], total[..., half:]
        away = away + move_mp(away, INWARD)
        near = near + move_mp(away, MIDDLE)
        quarter = half // 2
        return near[..., :quarter] + move_mp(near[..., quarter:], PAIR)

    def scatter_group(grad):
        pieces = {}
        for p in range(chips):
            for h in range(2):
                pieces[2 * p, h] = lax.slice_in_dim(grad, (2 * p + h) * part, (2 * p + h + 1) * part, axis=1)
        first = scatter_chips({2 * p: pieces[2 * p, 0] for p in range(chips)}, bits[::-1])
        second = scatter_chips({2 * p: pieces[2 * p, 1] for p in range(chips)}, bits)
        mine = scatter_line(jnp.stack([first, second], 1))
        keep = pick(mine[:, 0], mine[:, 1])
        recv = swap_core(pick(mine[:, 1], mine[:, 0]))
        return jnp.concatenate([pick(keep, recv), pick(recv, keep)], -1).astype(F32)

    items = image_states.shape[0]
    run = image_states.shape[1] // 2

    def bring(value):
        blocks = value.reshape(items, 2, run, width)
        keep = pick(blocks[:, 0], blocks[:, 1])
        recv = swap_core(pick(blocks[:, 1], blocks[:, 0]))
        whole = jnp.concatenate([pick(keep, recv), pick(recv, keep)], 0)
        return reorder(lax.all_to_all(whole, "mp", 0, 0, tiled=True).reshape(lines * run, width))

    def give(value, rows):
        whole = lax.all_to_all(reorder(value).reshape(lines, rows, width), "mp", 0, 0, tiled=True)
        low, high = whole[:items], whole[items:]
        keep = pick(low, high)
        recv = swap_core(pick(high, low))
        return jnp.stack([pick(keep, recv), pick(recv, keep)], 1).reshape(items, 2 * rows, width).astype(F32)

    def both(value):
        return jnp.concatenate([value, swap_core(value)], 0)

    def joined(left, right, dims):
        half = left.shape[0] // 2
        other = dot(left[half:], right, dims).astype(BF)
        return dot(left[:half], right, dims) + swap_core(other).astype(F32)

    low_inout = own_half(jnp.concatenate([input_weights[:3], output_weights[:1], input_weights[3:], output_weights[1:]], 0).astype(BF))
    low_hidden = own_half(hidden_weights.astype(BF))

    gains_all = lax.dynamic_update_slice(
        jnp.zeros((6, width), F32), norm_gains, (0, (dp * lines + mp) * norm_gains.shape[1])
    )

    def sum_all(value):
        bit = 1
        while bit < size:
            value = value + swap_dp(value, size, bit)
            bit *= 2
        value = value + move_mp(value, PAIR)
        return value + move_mp(value, ACROSS)

    gain_rows = reorder(sum_all(gains_all))
    image_own = bring(image_states).astype(F32)

    weights_self = gather_group(low_inout[:4])
    weights_cross = gather_group(low_inout[4:])
    weights_up = gather_group(low_hidden[:1])[0]
    weights_down = gather_group(low_hidden[1:])[0]

    cot_own = bring(cotangent)

    which = mp % items
    mine = lax.dynamic_index_in_dim(text_states, which, 0, keepdims=False)
    mine_mask = lax.dynamic_index_in_dim(text_mask, which, 0, keepdims=False).astype(F32)
    here = (mp // items) == core
    text = reorder(jnp.where(here, mine, swap_core(mine)))
    valid = jnp.where(here, mine_mask, swap_core(mine_mask))
    valid = jnp.broadcast_to(valid[:, None], (valid.shape[0], 128))

    core_index = core.astype(jnp.int32).reshape(1)

    unit, _ = norm_parts(image_own)
    h1 = both((unit * gain_rows[0] + gain_rows[1]).astype(BF))
    q1, k1, v1 = (dot(h1, weights_self[j], NN).astype(BF) for j in range(3))
    o1, l1 = self_fwd(core_index, q1, k1, v1)
    r1 = image_own + joined(o1, weights_self[3], NT)
    unit, _ = norm_parts(r1)
    h2 = both((unit * gain_rows[2] + gain_rows[3]).astype(BF))
    q2 = dot(h2, weights_cross[0], NN).astype(BF)
    k2, v2 = (dot(text, weights_cross[j], NN).astype(BF) for j in (1, 2))
    o2, l2 = cross_fwd(valid, q2, k2, v2)
    r2 = r1 + joined(o2, weights_cross[3], NT)
    unit, _ = norm_parts(r2)
    h3 = both((unit * gain_rows[4] + gain_rows[5]).astype(BF))
    u = dot(h3, weights_up, NN)
    bend = jnp.tanh(GELU_SCALE * (u + GELU_CUBIC * u * u * u))
    e = (0.5 * u * (1.0 + bend)).astype(BF)
    slope = (
        0.5 * (1.0 + bend) + 0.5 * u * (1.0 - bend * bend) * GELU_SCALE * (1.0 + 3.0 * GELU_CUBIC * u * u)
    ).astype(BF)
    layer_own = r2 + joined(e, weights_down, NT)
    layer_out = give(layer_own.astype(BF), run)

    cot = both(cot_own)
    cot_float = cot_own.astype(F32)
    grad_down = dot(cot, e, TN).astype(BF)
    shard_down = scatter_group(grad_down[None])
    du = (dot(cot, weights_down, NN) * slope.astype(F32)).astype(BF)
    grad_up = dot(h3, du, TN).astype(BF)
    shard_up = scatter_group(grad_up[None])
    dh3 = joined(du, weights_up, NT)
    back, gain_five, shift_six = norm_back(r2, dh3, gain_rows[4])
    dr2 = cot_float + back
    z2 = both(dr2.astype(BF))
    do2 = dot(z2, weights_cross[3], NN).astype(BF)
    go1 = dot(z2, o2, TN).astype(BF)
    dq2, dk2, dv2 = cross_bwd(valid, q2, k2, v2, do2, l2)
    dh2 = joined(dq2, weights_cross[0], NT)
    gi3 = dot(h2, dq2, TN).astype(BF)
    gi4 = dot(text, dk2, TN).astype(BF)
    gi5 = dot(text, dv2, TN).astype(BF)
    shard_cross = scatter_group(jnp.stack([gi3, gi4, gi5, go1]))
    text_part = dot(dk2, weights_cross[1], NT) + dot(dv2, weights_cross[2], NT)
    share = text.shape[0] // (2 * lines)
    text_part = text_part.reshape(lines, 2, share, width)
    text_own = pick(text_part[:, 0], text_part[:, 1]) + swap_core(
        pick(text_part[:, 1], text_part[:, 0]).astype(BF)
    ).astype(F32)
    text_gradient = give(text_own.astype(BF).reshape(lines * share, width), share)
    back, gain_three, shift_four = norm_back(r1, dh2, gain_rows[2])
    dr1 = dr2 + back
    z1 = both(dr1.astype(BF))
    do1 = dot(z1, weights_self[3], NN).astype(BF)
    go0 = dot(z1, o1, TN).astype(BF)
    dq1, dk1, dv1 = self_bwd(core_index, q1, k1, v1, do1, l1)
    gi0, gi1, gi2 = (dot(h1, g, TN).astype(BF) for g in (dq1, dk1, dv1))
    shard_self = scatter_group(jnp.stack([gi0, gi1, gi2, go0]))
    half = dq1.shape[0] // 2

    def three(at):
        return (
            dot(dq1[at], weights_self[0], NT) + dot(dk1[at], weights_self[1], NT) + dot(dv1[at], weights_self[2], NT)
        )

    dh1 = three(slice(0, half)) + swap_core(three(slice(half, None)).astype(BF)).astype(F32)
    back, gain_one, shift_two = norm_back(image_own, dh1, gain_rows[0])
    image_gradient = give((dr1 + back).astype(BF), run)

    gains_total = sum_all(reorder(jnp.stack([gain_one, shift_two, gain_three, shift_four, gain_five, shift_six])))
    gains_shard = lax.dynamic_slice_in_dim(
        gains_total, (dp * lines + mp) * norm_gains.shape[1], norm_gains.shape[1], 1
    )

    input_shard = jnp.concatenate([shard_self[:3], shard_cross[:3]], 0)
    output_shard = jnp.concatenate([shard_self[3:], shard_cross[3:]], 0)
    hidden_shard = jnp.concatenate([shard_up, shard_down], 0)
    square_total = jnp.sum(input_shard * input_shard) + jnp.sum(output_shard * output_shard)
    square_total = square_total + jnp.sum(hidden_shard * hidden_shard) + jnp.sum(gains_shard * gains_shard)
    global_norm = jnp.sqrt(sum_all(jnp.full((8, 128), square_total)))[0, 0]
    factor = jnp.minimum(1.0, CLIP_LIMIT / (global_norm + 1e-06))
    input_updated, input_moment, input_square = adam_update(
        input_weights, input_shard, input_momentum, input_variance, factor, LEARN_RATE, WEIGHT_DECAY
    )
    output_updated, output_moment, output_square = adam_update(
        output_weights, output_shard, output_momentum, output_variance, factor, LEARN_RATE, WEIGHT_DECAY
    )
    hidden_updated, hidden_moment, hidden_square = adam_update(
        hidden_weights, hidden_shard, hidden_momentum, hidden_variance, factor, LEARN_RATE, WEIGHT_DECAY
    )
    gains_updated, gains_moment, gains_square = adam_update(
        norm_gains, gains_shard, gains_momentum, gains_variance, factor, GAIN_RATE, 0.0
    )
    return (
        layer_out, image_gradient, text_gradient, global_norm,
        input_updated, output_updated, hidden_updated, gains_updated,
        input_moment, output_moment, hidden_moment, gains_moment,
        input_square, output_square, hidden_square, gains_square,
    )


def solution(mesh):
    rows, weight, gains = P("dp", "mp", None), P(None, "dp", "mp"), P(None, ("dp", "mp"))
    return jax.shard_map(
        per_device,
        mesh=mesh,
        in_specs=(rows, P("dp", None, None), P("dp", None), rows) + (weight, weight, weight, gains) * 3,
        out_specs=(rows, rows, rows, P()) + (weight, weight, weight, gains) * 3,
        check_vma=False,
    )
```

time: 2110 us -> 755 us (0.36)
  waiting for transfers between devices: 1540 us -> 306 us
  starting transfers between devices: 2.65 us -> 156 us
  blocking collectives: 109 us -> 0 us
  matrix products: 191 us -> 96.8 us
  local copies, waits for them, and re-layouts: 121 us -> 49.1 us
  Pallas kernels: 0 us -> 50.1 us
    reduce_scatter x10 -> x0, waiting for transfers between devices: 921 us -> none  [the longest x3 429 us: collect_rows(): lax.psum_scatter(partial_value, 'mp', scatter_dimension=1, tiled=True)]
    all_gather x9 -> x0, waiting for transfers between devices: 486 us -> none  [the longest x3 238 us: spread_rows(): return lax.all_gather(normed, 'mp', axis=1, tiled=True)]
    ppermute x0 -> x97, waiting for transfers between devices: none -> 284 us  [the longest x67 200 us: swap_dp(): return lax.ppermute(value, 'dp', [(i, i ^ bit) for i in range(size)])]
    unnamed x21 -> x0, waiting for transfers between devices: 134 us -> none
    ppermute x0 -> x97, starting transfers between devices: none -> 115 us  [the longest x30 67.5 us: move_mp(): return lax.ppermute(value, 'mp', pairs)]
    dot_general x77 -> x38, matrix products: 191 us -> 96.8 us  [dot(): return lax.dot_general(a, b, dims, preferred_element_type=F32)]
    all_gather x1 -> x0, blocking collectives: 71 us -> none  [per_device(): gain_rows = lax.all_gather(norm_gains, ('dp', 'mp'), axis=1, tiled=True)]
    pallas_call x0 -> x4, Pallas kernels: none -> 50.1 us  [the longest x1 17.3 us: self_bwd(): pl.pallas_call(lambda *r: self_bwd_kernel(*r, seq=seq), grid_spec=pltpu.P...]
  transfers between devices with their start and end apart: 20 -> 102, of which waited for: 16 -> 39; matrix products, arithmetic and copies ran while one was open for 13% -> 25% of each run, Pallas kernels for 0% -> 7%
where the time goes in v1:
time: 755 us; the launch traced here: 747 us
  waiting for transfers between devices  306 us (41%)
  starting transfers between devices  156 us (21%)
  matrix products  96.8 us (13%)
  other arithmetic  83.1 us (11%)
  Pallas kernels  50.1 us (7%)
  local copies, waits for them, and re-layouts  49.1 us (7%)
    ppermute x67, waiting for transfers between devices, swap_dp(): return lax.ppermute(value, 'dp', [(i, i ^ bit) for i in range(size)])  200 us
    dot_general x38, matrix products, dot(): return lax.dot_general(a, b, dims, preferred_element_type=F32)  96.8 us
    ppermute x30, waiting for transfers between devices, move_mp(): return lax.ppermute(value, 'mp', pairs)  83.8 us
    ppermute x30, starting transfers between devices, move_mp(): return lax.ppermute(value, 'mp', pairs)  67.5 us
    ppermute x67, starting transfers between devices, swap_dp(): return lax.ppermute(value, 'dp', [(i, i ^ bit) for i in range(size)])  47.8 us
    all_to_all x2, starting transfers between devices, bring(): lax.all_to_all(whole, 'mp', 0, 0, tiled=True).reshape(lines * run, width)  27 us
    unnamed x236, local copies, waits for them, and re-layouts  27 us
    all_to_all x2, waiting for transfers between devices, bring(): lax.all_to_all(whole, 'mp', 0, 0, tiled=True).reshape(lines * run, width)  18.3 us
  transfers between devices with their start and end apart: 102, of which 39 were waited for; matrix products, arithmetic and copies ran while one was open for 25% of the time, Pallas kernels for 7%

profile of v1, /device:TPU:0, one launch (start us, length us, event | category | flops | bytes accessed | tf_op | source)
XLA Modules:
  0.0 747.3 jit_solution(15890111916162996949)
XLA Ops:
  35.8 9.0 %collective-permute-done.29 = bf16[1,2,128,512]{3,2,0,1:T(8,128)(2,1)S(1)} collective-permute-done((bf16[1,2,128,512]{3,2,0,1:T(8,128)(2,1)S(1)}, bf16[1,2,128,512]{3,2,0,1:T(8,128)(2,1)S(1)}, u32[]{:S(2)}, u32[]{:S(2)}) %collective-permute-start.29) | collective-permute-done | bytes 262176 | tf_op jit(solution)/shard_map/ppermute | solution.py:195
  63.3 22.5 %all-to-all-start = ((bf16[4,128,1024]{2,1,0:T(8,128)(2,1)}), bf16[4,128,1024]{2,1,0:T(8,128)(2,1)S(1)}, u32[]{:S(2)}, u32[]{:S(2)}) async-start(bf16[4,128,1024]{2,1,0:T(8,128)(2,1)} %pad_maximum_fusion.16), calls=%async_computation | async-start | bytes 2097152 | tf_op jit(solution)/shard_map/all_to_all | solution.py:334
  90.7 9.6 %collective-permute-done.38 = bf16[1,2,128,1024]{3,2,0,1:T(8,128)(2,1)} collective-permute-done((bf16[1,2,128,1024]{3,2,0,1:T(8,128)(2,1)}, bf16[1,2,128,1024]{3,2,0,1:T(8,128)(2,1)}, u32[]{:S(2)}, u32[]{:S(2)}) %collective-permute-start.38) | collective-permute-done | bytes 524320 | tf_op jit(solution)/shard_map/ppermute | solution.py:195
  103.6 10.1 %collective-permute-done.20 = bf16[4,2,128,256]{3,2,0,1:T(8,128)(2,1)S(1)} collective-permute-done((bf16[4,2,128,256]{3,2,0,1:T(8,128)(2,1)}, bf16[4,2,128,256]{3,2,0,1:T(8,128)(2,1)S(1)}, u32[]{:S(2)}, u32[]{:S(2)}) %collective-permute-start.20) | collective-permute-done | bytes 524320 | tf_op jit(solution)/shard_map/ppermute | solution.py:195
  113.7 16.9 %collective-permute-done.10 = bf16[4,2,128,256]{3,2,0,1:T(8,128)(2,1)S(1)} collective-permute-done((bf16[4,2,128,256]{3,2,0,1:T(8,128)(2,1)}, bf16[4,2,128,256]{3,2,0,1:T(8,128)(2,1)S(1)}, u32[]{:S(2)}, u32[]{:S(2)}) %collective-permute-start.10) | collective-permute-done | bytes 524320 | tf_op jit(solution)/shard_map/ppermute | solution.py:195
  153.8 18.3 %all-to-all-done.2 = bf16[4,128,1024]{2,1,0:T(8,128)(2,1)} async-done(((bf16[4,128,1024]{2,1,0:T(8,128)(2,1)}), bf16[4,128,1024]{2,1,0:T(8,128)(2,1)}, u32[]{:S(2)}, u32[]{:S(2)}) %all-to-all-start.2) | async-done | bytes 1048608 | tf_op jit(solution)/shard_map/all_to_all | solution.py:334
  182.9 5.4 collective-permute-done.23
  194.5 5.1 collective-permute-done.34
  201.7 40.1 %collective-permute-done.12 = bf16[4,256,512]{2,1,0:T(8,128)(2,1)S(1)} collective-permute-done((bf16[4,256,512]{2,1,0:T(8,128)(2,1)S(1)}, bf16[4,256,512]{2,1,0:T(8,128)(2,1)S(1)}, u32[]{:S(2)}, u32[]{:S(2)}) %collective-permute-start.12) | collective-permute-done | bytes 1048608 | tf_op jit(solution)/shard_map/ppermute | solution.py:191
  245.7 19.4 %collective-permute-done.33 = bf16[1,256,2048]{2,1,0:T(8,128)(2,1)S(1)} collective-permute-done((bf16[1,256,2048]{2,1,0:T(8,128)(2,1)S(1)}, bf16[1,256,2048]{2,1,0:T(8,128)(2,1)S(1)}, u32[]{:S(2)}, u32[]{:S(2)}) %collective-permute-start.33) | collective-permute-done | bytes 1048608 | tf_op jit(solution)/shard_map/ppermute | solution.py:191
  273.1 17.2 %self_forward.1 = (bf16[1024,512]{1,0:T(8,128)(2,1)S(1)}, f32[4,2,1024]{2,1,0:T(2,128)S(1)}) custom-call(s32[1]{0:T(128)} %bitcast.4.r_0_, bf16[1024,512]{1,0:T(8,128)(2,1)S(1)} %convolution_convert_fusion.13.r_1_, bf16[1024,512]{1,0:T(8,128)(2,1)S(1)} %convolution_convert_fusion.12.r_2_, bf16[1024,512]{1,0:T(8,128)(2,1)S(1)} %convolution_convert_fusion.11.r_3_), custom_call_target="tpu_custom_call" | custom-call | flops 8589934592 | bytes 4194304 | tf_op jit(solution)/shard_map/self_forward/pallas_call | solution.py:137
  304.9 6.3 cross_forward.1
  321.5 12.6 %multiply_convert_fusion.1 = (bf16[1024,2048]{1,0:T(8,128)(2,1)}, f32[1024,2048]{1,0:T(8,128)}) fusion(bf16[1,1024,2048]{2,1,0:T(8,128)(2,1)} %slice_dynamic-update-slice_fusion.4, bf16[512,1024]{1,0:T(8,128)(2,1)S(1)} %collective-permute-done.27, bf16[512,1024]{1,0:T(8,128)(2,1)S(1)} %add_convert_fusion.2), kind=kOutput, calls=%fused_computation.9 | convolution fusion | flops 4318035968 | bytes 18874368 | tf_op jit(solution)/shard_map/dot_general | solution.py:9
  334.1 16.8 %multiply_convert_fusion = bf16[1024,2048]{1,0:T(8,128)(2,1)} fusion(f32[1024,2048]{1,0:T(8,128)} %get-tuple-element.175, bf16[1,1024,2048]{2,1,0:T(8,128)(2,1)S(1)} %slice_dynamic-update-slice_fusion, bf16[512,1024]{1,0:T(8,128)(2,1)} %collective-permute-done.46, bf16[512,256]{1,0:T(8,128)(2,1)S(1)} %get-tuple-element.107, ...), kind=kOutput, calls=%fused_computation.8 | convolution fusion | flops 4349493248 | bytes 18874368 | tf_op jit(solution)/shard_map/dot_general | solution.py:9
  350.9 5.3 fusion.44
  358.7 7.1 convert_bitcast_fusion
  367.8 7.4 convert_bitcast_fusion.1
  376.0 7.3 multiply_reduce_fusion
  385.8 28.3 %collective-permute-done.71 = bf16[1,256,2048]{2,1,0:T(8,128)(2,1)S(1)} collective-permute-done((bf16[1,256,2048]{2,1,0:T(8,128)(2,1)S(1)}, bf16[1,256,2048]{2,1,0:T(8,128)(2,1)S(1)}, u32[]{:S(2)}, u32[]{:S(2)}) %collective-permute-start.71) | collective-permute-done | bytes 1048608 | tf_op jit(solution)/shard_map/ppermute | solution.py:191
  428.8 9.3 %cross_backward.1 = (bf16[1024,512]{1,0:T(8,128)(2,1)S(1)}, bf16[128,512]{1,0:T(8,128)(2,1)S(1)}, bf16[128,512]{1,0:T(8,128)(2,1)S(1)}) custom-call(f32[128,128]{1,0:T(8,128)S(1)} %broadcast_in_dim.11.r_0_, bf16[1024,512]{1,0:T(8,128)(2,1)S(1)} %convolution_convert_fusion.10.r_1_, bf16[128,512]{1,0:T(8,128)(2,1)S(1)} %convolution_convert_fusion.18.r_2_, ...), custom_call_target="tpu_custom_call" | custom-call | flops 2684354560 | bytes 5242880 | tf_op jit(solution)/shard_map/cross_backward/pallas_call | solution.py:161
  465.9 19.3 %collective-permute-done.81 = bf16[1,256,2048]{2,1,0:T(8,128)(2,1)} collective-permute-done((bf16[1,256,2048]{2,1,0:T(8,128)(2,1)}, bf16[1,256,2048]{2,1,0:T(8,128)(2,1)}, u32[]{:S(2)}, u32[]{:S(2)}) %collective-permute-start.81) | collective-permute-done | bytes 1048608 | tf_op jit(solution)/shard_map/ppermute | solution.py:191
  494.3 6.5 collective-permute-done.82
  510.4 7.2 collective-permute-done.83
  530.4 6.3 collective-permute-start.85
  536.8 5.2 collective-permute-done.85
  546.9 17.3 %self_backward.1 = (bf16[1024,512]{1,0:T(8,128)(2,1)S(1)}, bf16[1024,512]{1,0:T(8,128)(2,1)S(1)}, bf16[1024,512]{1,0:T(8,128)(2,1)S(1)}) custom-call(s32[1]{0:T(128)} %bitcast.4.r_0_, bf16[1024,512]{1,0:T(8,128)(2,1)S(1)} %copy-done.3, bf16[1024,512]{1,0:T(8,128)(2,1)S(1)} %convolution_convert_fusion.12.r_2_, ...), custom_call_target="tpu_custom_call" | custom-call | flops 21474836480 | bytes 8388608 | tf_op jit(solution)/shard_map/self_backward/pallas_call | solution.py:145
  577.7 29.2 %collective-permute-done.66 = bf16[4,128,512]{2,1,0:T(8,128)(2,1)S(1)} collective-permute-done((bf16[4,128,512]{2,1,0:T(8,128)(2,1)S(1)}, bf16[4,128,512]{2,1,0:T(8,128)(2,1)S(1)}, u32[]{:S(2)}, u32[]{:S(2)}) %collective-permute-start.66) | collective-permute-done | bytes 524320 | tf_op jit(solution)/shard_map/ppermute | solution.py:191
  620.6 8.3 %collective-permute-done.56 = bf16[4,128,512]{2,1,0:T(8,128)(2,1)} collective-permute-done((bf16[4,128,512]{2,1,0:T(8,128)(2,1)}, bf16[4,128,512]{2,1,0:T(8,128)(2,1)}, u32[]{:S(2)}, u32[]{:S(2)}) %collective-permute-start.56) | collective-permute-done | bytes 524320 | tf_op jit(solution)/shard_map/ppermute | solution.py:191
  628.9 20.5 %collective-permute-done.57 = bf16[4,256,512]{2,1,0:T(8,128)(2,1)} collective-permute-done((bf16[4,256,512]{2,1,0:T(8,128)(2,1)}, bf16[4,256,512]{2,1,0:T(8,128)(2,1)}, u32[]{:S(2)}, u32[]{:S(2)}) %collective-permute-start.57) | collective-permute-done | bytes 1048608 | tf_op jit(solution)/shard_map/ppermute | solution.py:191
  655.6 8.0 %collective-permute-done.58 = bf16[4,128,512]{2,1,0:T(8,128)(2,1)S(1)} collective-permute-done((bf16[4,128,512]{2,1,0:T(8,128)(2,1)S(1)}, bf16[4,128,512]{2,1,0:T(8,128)(2,1)S(1)}, u32[]{:S(2)}, u32[]{:S(2)}) %collective-permute-start.58) | collective-permute-done | bytes 524320 | tf_op jit(solution)/shard_map/ppermute | solution.py:191
  681.3 5.6 all-to-all-start.3
  692.9 16.3 %collective-permute-start.61 = (bf16[4,2,128,128]{3,2,0,1:T(8,128)(2,1)S(1)}, bf16[4,2,128,128]{3,2,0,1:T(8,128)(2,1)S(1)}, u32[]{:S(2)}, u32[]{:S(2)}) collective-permute-start(bf16[4,2,128,128]{3,2,0,1:T(8,128)(2,1)S(1)} %slice.707), channel_id=1, source_target_pairs={{0,1},{1,0},{2,3},{3,2},{4,5},{5,4},{6,7},{7,6},{8,9},{9,8},{10,11... | collective-permute-start | bytes 786440 | tf_op jit(solution)/shard_map/ppermute | solution.py:195
  (640 shorter events, 316.8 us)
Async XLA Ops:
  22.9 62.8 %collective-permute-start.45 = (bf16[2,128,1024]{2,1,0:T(8,128)(2,1)}, bf16[2,128,1024]{2,1,0:T(8,128)(2,1)}, u32[]{:S(2)}, u32[]{:S(2)}) collective-permute-start(bf16[2,128,1024]{2,1,0:T(8,128)(2,1)} %select_bitcast_fusion.2), channel_id=1, source_target_pairs={{0,4},{4,0},{8,12},{12,8},{16,20},{20,16},{24,28},{28,24},{1,5},{5... | collective-permute-start | bytes 1572872 | tf_op jit(solution)/shard_map/ppermute | solution.py:191
  60.9 39.4 %collective-permute-start.38 = (bf16[1,2,128,1024]{3,2,0,1:T(8,128)(2,1)}, bf16[1,2,128,1024]{3,2,0,1:T(8,128)(2,1)}, u32[]{:S(2)}, u32[]{:S(2)}) collective-permute-start(bf16[1,2,128,1024]{3,2,0,1:T(8,128)(2,1)} %collective-permute-done.37), channel_id=1, source_target_pairs={{1,0},{2,3},{5,4},{6,7},{9,8},{10,11},{13,12},{14,15},{17,16},{18,... | collective-permute-start | bytes 1572872 | tf_op jit(solution)/shard_map/ppermute | solution.py:195
  63.3 82.3 %all-to-all-start = ((bf16[4,128,1024]{2,1,0:T(8,128)(2,1)}), bf16[4,128,1024]{2,1,0:T(8,128)(2,1)S(1)}, u32[]{:S(2)}, u32[]{:S(2)}) async-start(bf16[4,128,1024]{2,1,0:T(8,128)(2,1)} %pad_maximum_fusion.16), calls=%async_computation | async-start | bytes 2097152 | tf_op jit(solution)/shard_map/all_to_all | solution.py:334
  89.4 41.1 %collective-permute-start.10 = (bf16[4,2,128,256]{3,2,0,1:T(8,128)(2,1)}, bf16[4,2,128,256]{3,2,0,1:T(8,128)(2,1)S(1)}, u32[]{:S(2)}, u32[]{:S(2)}) collective-permute-start(bf16[4,2,128,256]{3,2,0,1:T(8,128)(2,1)} %collective-permute-done.9), channel_id=1, source_target_pairs={{1,0},{2,3},{5,4},{6,7},{9,8},{10,11},{13,12},{14,15},{17,16},{18,... | collective-permute-start | bytes 1572872 | tf_op jit(solution)/shard_map/ppermute | solution.py:195
  136.6 36.8 %collective-permute-start.39 = (bf16[1,128,2048]{2,1,0:T(8,128)(2,1)}, bf16[1,128,2048]{2,1,0:T(8,128)(2,1)}, u32[]{:S(2)}, u32[]{:S(2)}) collective-permute-start(bf16[1,128,2048]{2,1,0:T(8,128)(2,1)} %slice_bitcast_fusion.33), channel_id=1, source_target_pairs={{0,16},{4,20},{8,24},{12,28},{16,0},{20,4},{24,8},{28,12},{1,17},{... | collective-permute-start | bytes 1572872 | tf_op jit(solution)/shard_map/ppermute | solution.py:191
  138.1 41.9 %collective-permute-start.41 = (bf16[1,128,2048]{2,1,0:T(8,128)(2,1)}, bf16[1,128,2048]{2,1,0:T(8,128)(2,1)}, u32[]{:S(2)}, u32[]{:S(2)}) collective-permute-start(bf16[1,128,2048]{2,1,0:T(8,128)(2,1)} %slice_bitcast_fusion.32), channel_id=1, source_target_pairs={{0,8},{4,12},{8,0},{12,4},{16,24},{20,28},{24,16},{28,20},{1,9},{5... | collective-permute-start | bytes 1572872 | tf_op jit(solution)/shard_map/ppermute | solution.py:191
  139.6 51.3 %collective-permute-start.13 = (bf16[4,128,512]{2,1,0:T(8,128)(2,1)}, bf16[4,128,512]{2,1,0:T(8,128)(2,1)}, u32[]{:S(2)}, u32[]{:S(2)}) collective-permute-start(bf16[4,128,512]{2,1,0:T(8,128)(2,1)} %get-tuple-element.124), channel_id=1, source_target_pairs={{0,8},{4,12},{8,0},{12,4},{16,24},{20,28},{24,16},{28,20},{1,9},{5... | collective-permute-start | bytes 1572872 | tf_op jit(solution)/shard_map/ppermute | solution.py:191
  140.7 37.5 %collective-permute-start.21 = (bf16[4,128,512]{2,1,0:T(8,128)(2,1)}, bf16[4,128,512]{2,1,0:T(8,128)(2,1)}, u32[]{:S(2)}, u32[]{:S(2)}) collective-permute-start(bf16[4,128,512]{2,1,0:T(8,128)(2,1)} %get-tuple-element.119), channel_id=1, source_target_pairs={{0,16},{4,20},{8,24},{12,28},{16,0},{20,4},{24,8},{28,12},{1,17},{... | collective-permute-start | bytes 1572872 | tf_op jit(solution)/shard_map/ppermute | solution.py:191
  180.1 92.0 %collective-permute-start.22 = (bf16[4,256,512]{2,1,0:T(8,128)(2,1)S(1)}, bf16[4,256,512]{2,1,0:T(8,128)(2,1)S(1)}, u32[]{:S(2)}, u32[]{:S(2)}) collective-permute-start(bf16[4,256,512]{2,1,0:T(8,128)(2,1)S(1)} %pad_maximum_fusion.22), channel_id=1, source_target_pairs={{0,8},{4,12},{8,0},{12,4},{16,24},{20,28},{24,16},{28,20},{1,9},{5... | collective-permute-start | bytes 3145736 | tf_op jit(solution)/shard_map/ppermute | solution.py:191
  188.4 53.4 %collective-permute-start.12 = (bf16[4,256,512]{2,1,0:T(8,128)(2,1)S(1)}, bf16[4,256,512]{2,1,0:T(8,128)(2,1)S(1)}, u32[]{:S(2)}, u32[]{:S(2)}) collective-permute-start(bf16[4,256,512]{2,1,0:T(8,128)(2,1)S(1)} %pad_maximum_fusion.19), channel_id=1, source_target_pairs={{0,8},{4,12},{8,0},{12,4},{16,24},{20,28},{24,16},{28,20},{1,9},{5... | collective-permute-start | bytes 3145736 | tf_op jit(solution)/shard_map/ppermute | solution.py:191
  190.9 101.4 %collective-permute-start.24 = (bf16[4,256,512]{2,1,0:T(8,128)(2,1)}, bf16[4,256,512]{2,1,0:T(8,128)(2,1)}, u32[]{:S(2)}, u32[]{:S(2)}) collective-permute-start(bf16[4,256,512]{2,1,0:T(8,128)(2,1)} %pad_maximum_fusion.23), channel_id=1, source_target_pairs={{0,16},{4,20},{8,24},{12,28},{16,0},{20,4},{24,8},{28,12},{1,17},{... | collective-permute-start | bytes 3145736 | tf_op jit(solution)/shard_map/ppermute | solution.py:191
  192.7 52.8 %collective-permute-start.14 = (bf16[4,256,512]{2,1,0:T(8,128)(2,1)S(1)}, bf16[4,256,512]{2,1,0:T(8,128)(2,1)S(1)}, u32[]{:S(2)}, u32[]{:S(2)}) collective-permute-start(bf16[4,256,512]{2,1,0:T(8,128)(2,1)S(1)} %pad_maximum_fusion.20), channel_id=1, source_target_pairs={{0,16},{4,20},{8,24},{12,28},{16,0},{20,4},{24,8},{28,12},{1,17},{... | collective-permute-start | bytes 3145736 | tf_op jit(solution)/shard_map/ppermute | solution.py:191
  199.6 119.2 %collective-permute-start.42 = (bf16[1,256,2048]{2,1,0:T(8,128)(2,1)S(1)}, bf16[1,256,2048]{2,1,0:T(8,128)(2,1)S(1)}, u32[]{:S(2)}, u32[]{:S(2)}) collective-permute-start(bf16[1,256,2048]{2,1,0:T(8,128)(2,1)S(1)} %pad_maximum_fusion.29), channel_id=1, source_target_pairs={{0,16},{4,20},{8,24},{12,28},{16,0},{20,4},{24,8},{28,12},{1,17},{... | collective-permute-start | bytes 3145736 | tf_op jit(solution)/shard_map/ppermute | solution.py:191
  268.3 65.7 %collective-permute-start.46 = (bf16[512,1024]{1,0:T(8,128)(2,1)S(1)}, bf16[512,1024]{1,0:T(8,128)(2,1)}, u32[]{:S(2)}, u32[]{:S(2)}) collective-permute-start(bf16[512,1024]{1,0:T(8,128)(2,1)S(1)} %pad_maximum_fusion.32), channel_id=1, source_target_pairs={{0,4},{4,0},{8,12},{12,8},{16,20},{20,16},{24,28},{28,24},{1,5},{5... | collective-permute-start | bytes 3145736 | tf_op jit(solution)/shard_map/ppermute | solution.py:191
  358.6 62.5 %collective-permute-start.43 = (bf16[512,1024]{1,0:T(8,128)(2,1)S(1)}, bf16[512,1024]{1,0:T(8,128)(2,1)S(1)}, u32[]{:S(2)}, u32[]{:S(2)}) collective-permute-start(bf16[512,1024]{1,0:T(8,128)(2,1)S(1)} %fusion.49), channel_id=1, source_target_pairs={{0,4},{4,0},{8,12},{12,8},{16,20},{20,16},{24,28},{28,24},{1,5},{5... | collective-permute-start | bytes 3145736 | tf_op jit(solution)/shard_map/ppermute | solution.py:191
  366.0 52.2 %collective-permute-start.79 = (bf16[1,256,2048]{2,1,0:T(8,128)(2,1)S(1)}, bf16[1,256,2048]{2,1,0:T(8,128)(2,1)S(1)}, u32[]{:S(2)}, u32[]{:S(2)}) collective-permute-start(bf16[1,256,2048]{2,1,0:T(8,128)(2,1)S(1)} %pad_maximum_fusion.40), channel_id=1, source_target_pairs={{0,8},{4,12},{8,0},{12,4},{16,24},{20,28},{24,16},{28,20},{1,9},{5... | collective-permute-start | bytes 3145736 | tf_op jit(solution)/shard_map/ppermute | solution.py:191
  375.4 38.7 %collective-permute-start.71 = (bf16[1,256,2048]{2,1,0:T(8,128)(2,1)S(1)}, bf16[1,256,2048]{2,1,0:T(8,128)(2,1)S(1)}, u32[]{:S(2)}, u32[]{:S(2)}) collective-permute-start(bf16[1,256,2048]{2,1,0:T(8,128)(2,1)S(1)} %pad_maximum_fusion.38), channel_id=1, source_target_pairs={{0,8},{4,12},{8,0},{12,4},{16,24},{20,28},{24,16},{28,20},{1,9},{5... | collective-permute-start | bytes 3145736 | tf_op jit(solution)/shard_map/ppermute | solution.py:191
  385.3 42.2 %collective-permute-start.48 = (bf16[512,1024]{1,0:T(8,128)(2,1)S(1)}, bf16[512,1024]{1,0:T(8,128)(2,1)S(1)}, u32[]{:S(2)}, u32[]{:S(2)}) collective-permute-start(bf16[512,1024]{1,0:T(8,128)(2,1)S(1)} %get-tuple-element.64), channel_id=1, source_target_pairs={{0,4},{4,0},{8,12},{12,8},{16,20},{20,16},{24,28},{28,24},{1,5},{5... | collective-permute-start | bytes 3145736 | tf_op jit(solution)/shard_map/ppermute | solution.py:191
  415.2 46.1 %collective-permute-start.72 = (bf16[1,128,2048]{2,1,0:T(8,128)(2,1)}, bf16[1,128,2048]{2,1,0:T(8,128)(2,1)}, u32[]{:S(2)}, u32[]{:S(2)}) collective-permute-start(bf16[1,128,2048]{2,1,0:T(8,128)(2,1)} %get-tuple-element.68), channel_id=1, source_target_pairs={{0,16},{4,20},{8,24},{12,28},{16,0},{20,4},{24,8},{28,12},{1,17},{... | collective-permute-start | bytes 1572872 | tf_op jit(solution)/shard_map/ppermute | solution.py:191
  417.2 44.2 %collective-permute-start.73 = (bf16[1,256,2048]{2,1,0:T(8,128)(2,1)}, bf16[1,256,2048]{2,1,0:T(8,128)(2,1)}, u32[]{:S(2)}, u32[]{:S(2)}) collective-permute-start(bf16[1,256,2048]{2,1,0:T(8,128)(2,1)} %pad_maximum_fusion.39), channel_id=1, source_target_pairs={{0,16},{4,20},{8,24},{12,28},{16,0},{20,4},{24,8},{28,12},{1,17},{... | collective-permute-start | bytes 3145736 | tf_op jit(solution)/shard_map/ppermute | solution.py:191
  419.2 46.5 %collective-permute-start.80 = (bf16[1,128,2048]{2,1,0:T(8,128)(2,1)}, bf16[1,128,2048]{2,1,0:T(8,128)(2,1)}, u32[]{:S(2)}, u32[]{:S(2)}) collective-permute-start(bf16[1,128,2048]{2,1,0:T(8,128)(2,1)} %get-tuple-element.75), channel_id=1, source_target_pairs={{0,16},{4,20},{8,24},{12,28},{16,0},{20,4},{24,8},{28,12},{1,17},{... | collective-permute-start | bytes 1572872 | tf_op jit(solution)/shard_map/ppermute | solution.py:191
  421.2 64.0 %collective-permute-start.81 = (bf16[1,256,2048]{2,1,0:T(8,128)(2,1)}, bf16[1,256,2048]{2,1,0:T(8,128)(2,1)}, u32[]{:S(2)}, u32[]{:S(2)}) collective-permute-start(bf16[1,256,2048]{2,1,0:T(8,128)(2,1)} %pad_maximum_fusion.41), channel_id=1, source_target_pairs={{0,16},{4,20},{8,24},{12,28},{16,0},{20,4},{24,8},{28,12},{1,17},{... | collective-permute-start | bytes 3145736 | tf_op jit(solution)/shard_map/ppermute | solution.py:191
  445.9 72.6 %collective-permute-start.63 = (bf16[4,256,512]{2,1,0:T(8,128)(2,1)}, bf16[4,256,512]{2,1,0:T(8,128)(2,1)}, u32[]{:S(2)}, u32[]{:S(2)}) collective-permute-start(bf16[4,256,512]{2,1,0:T(8,128)(2,1)} %pad_maximum_fusion.36), channel_id=1, source_target_pairs={{0,8},{4,12},{8,0},{12,4},{16,24},{20,28},{24,16},{28,20},{1,9},{5... | collective-permute-start | bytes 3145736 | tf_op jit(solution)/shard_map/ppermute | solution.py:191
  461.2 42.6 %collective-permute-start.49 = (bf16[512,1024]{1,0:T(8,128)(2,1)}, bf16[512,1024]{1,0:T(8,128)(2,1)}, u32[]{:S(2)}, u32[]{:S(2)}) collective-permute-start(bf16[512,1024]{1,0:T(8,128)(2,1)} %convolution_convert_fusion.14), channel_id=1, source_target_pairs={{0,4},{4,0},{8,12},{12,8},{16,20},{20,16},{24,28},{28,24},{1,5},{5... | collective-permute-start | bytes 3145736 | tf_op jit(solution)/shard_map/ppermute | solution.py:191
  491.3 233.4 %collective-permute-start.44 = (bf16[2,128,1024]{2,1,0:T(8,128)(2,1)}, bf16[2,128,1024]{2,1,0:T(8,128)(2,1)}, u32[]{:S(2)}, u32[]{:S(2)}) collective-permute-start(bf16[2,128,1024]{2,1,0:T(8,128)(2,1)} %broadcast_select_fusion.8), channel_id=1, source_target_pairs={{0,4},{4,0},{8,12},{12,8},{16,20},{20,16},{24,28},{28,24},{1,5},{5... | collective-permute-start | bytes 1572872 | tf_op jit(solution)/shard_map/ppermute | solution.py:191
  509.4 36.3 %collective-permute-start.50 = (bf16[512,1024]{1,0:T(8,128)(2,1)S(1)}, bf16[512,1024]{1,0:T(8,128)(2,1)S(1)}, u32[]{:S(2)}, u32[]{:S(2)}) collective-permute-start(bf16[512,1024]{1,0:T(8,128)(2,1)S(1)} %get-tuple-element.62), channel_id=1, source_target_pairs={{0,4},{4,0},{8,12},{12,8},{16,20},{20,16},{24,28},{28,24},{1,5},{5... | collective-permute-start | bytes 3145736 | tf_op jit(solution)/shard_map/ppermute | solution.py:191
  519.7 53.7 %collective-permute-start.64 = (bf16[4,128,512]{2,1,0:T(8,128)(2,1)S(1)}, bf16[4,128,512]{2,1,0:T(8,128)(2,1)S(1)}, u32[]{:S(2)}, u32[]{:S(2)}) collective-permute-start(bf16[4,128,512]{2,1,0:T(8,128)(2,1)S(1)} %get-tuple-element.89), channel_id=1, source_target_pairs={{0,16},{4,20},{8,24},{12,28},{16,0},{20,4},{24,8},{28,12},{1,17},{... | collective-permute-start | bytes 1572872 | tf_op jit(solution)/shard_map/ppermute | solution.py:191
  525.9 47.5 %collective-permute-start.65 = (bf16[4,256,512]{2,1,0:T(8,128)(2,1)}, bf16[4,256,512]{2,1,0:T(8,128)(2,1)}, u32[]{:S(2)}, u32[]{:S(2)}) collective-permute-start(bf16[4,256,512]{2,1,0:T(8,128)(2,1)} %pad_maximum_fusion.37), channel_id=1, source_target_pairs={{0,16},{4,20},{8,24},{12,28},{16,0},{20,4},{24,8},{28,12},{1,17},{... | collective-permute-start | bytes 3145736 | tf_op jit(solution)/shard_map/ppermute | solution.py:191
  570.3 42.4 %collective-permute-start.55 = (bf16[4,256,512]{2,1,0:T(8,128)(2,1)S(1)}, bf16[4,256,512]{2,1,0:T(8,128)(2,1)S(1)}, u32[]{:S(2)}, u32[]{:S(2)}) collective-permute-start(bf16[4,256,512]{2,1,0:T(8,128)(2,1)S(1)} %pad_maximum_fusion.34), channel_id=1, source_target_pairs={{0,8},{4,12},{8,0},{12,4},{16,24},{20,28},{24,16},{28,20},{1,9},{5... | collective-permute-start | bytes 3145736 | tf_op jit(solution)/shard_map/ppermute | solution.py:191
  576.1 40.8 %collective-permute-start.51 = (bf16[512,1024]{1,0:T(8,128)(2,1)S(1)}, bf16[512,1024]{1,0:T(8,128)(2,1)S(1)}, u32[]{:S(2)}, u32[]{:S(2)}) collective-permute-start(bf16[512,1024]{1,0:T(8,128)(2,1)S(1)} %add_convert_fusion), channel_id=1, source_target_pairs={{0,4},{4,0},{8,12},{12,8},{16,20},{20,16},{24,28},{28,24},{1,5},{5... | collective-permute-start | bytes 3145736 | tf_op jit(solution)/shard_map/ppermute | solution.py:191
  608.1 44.7 %collective-permute-start.67 = (bf16[4,2,128,256]{3,2,0,1:T(8,128)(2,1)S(1)}, bf16[4,2,128,256]{3,2,0,1:T(8,128)(2,1)}, u32[]{:S(2)}, u32[]{:S(2)}) collective-permute-start(bf16[4,2,128,256]{3,2,0,1:T(8,128)(2,1)S(1)} %pad_maximum_fusion.45), channel_id=1, source_target_pairs={{0,1},{3,2},{4,5},{7,6},{8,9},{11,10},{12,13},{15,14},{16,17},{19,... | collective-permute-start | bytes 1572872 | tf_op jit(solution)/shard_map/ppermute | solution.py:195
  681.3 40.8 %all-to-all-start.3 = ((bf16[4,128,1024]{2,1,0:T(8,128)(2,1)}), bf16[4,128,1024]{2,1,0:T(8,128)(2,1)S(1)}, u32[]{:S(2)}, u32[]{:S(2)}) async-start(bf16[4,128,1024]{2,1,0:T(8,128)(2,1)} %bitcast.45), calls=%async_computation.3 | async-start | bytes 2097152 | tf_op jit(solution)/shard_map/all_to_all | solution.py:337
  (174 other events, 3073.4 us)

commit v2 on v1

--- a/solution.py
+++ b/solution.py
@@ -6,6 +6,7 @@
 BF=jnp.bfloat16; F32=jnp.float32
 HEAD_DIM=64; MASKED=-1e30; BQ=256
 NT=(((1,),(1,)),((),())); NN=(((1,),(0,)),((),())); TN=(((0,),(0,)),((),()))
+TINY=pl.CostEstimate(flops=1,bytes_accessed=1,transcendentals=0)
 def dot(a,b,dims): return lax.dot_general(a,b,dims,preferred_element_type=F32)
 
 def place_of(block, core, half):
@@ -139,7 +140,7 @@
             out_specs=[col(seq),pl.BlockSpec((1,2,seq),lambda p,*_:(p,0,0))],scratch_shapes=[pltpu.VMEM((seq,128),BF)]*3),
         out_shape=[jax.ShapeDtypeStruct((seq,cols),BF),jax.ShapeDtypeStruct((pairs,2,seq),F32)],
         compiler_params=params(),
-        cost_estimate=pl.CostEstimate(flops=8*seq*seq*cols*2,bytes_accessed=4*seq*cols*2,transcendentals=seq*seq*pairs),name="self_forward")(core,q,k,v)
+        cost_estimate=TINY,name="self_forward")(core,q,k,v)
 def self_bwd(core,q,k,v,g,l):
     seq,cols=q.shape; pairs=cols//128
     return pl.pallas_call(lambda *r: self_bwd_kernel(*r,seq=seq),
@@ -147,7 +148,7 @@
             out_specs=[col(seq)]*3,scratch_shapes=[pltpu.VMEM((seq,128),BF)]*4+[pltpu.VMEM((seq,128),F32)]*2),
         out_shape=[jax.ShapeDtypeStruct((seq,cols),BF)]*3,
         compiler_params=params(),
-        cost_estimate=pl.CostEstimate(flops=20*seq*seq*cols*2,bytes_accessed=8*seq*cols*2,transcendentals=seq*seq*pairs),name="self_backward")(core,q,k,v,g,l)
+        cost_estimate=TINY,name="self_backward")(core,q,k,v,g,l)
 def cross_fwd(mask,q,k,v):
     seq,cols=q.shape; text=k.shape[0]; pairs=cols//128
     return pl.pallas_call(lambda *r: cross_fwd_kernel(*r,seq=seq),grid=(pairs,),
@@ -155,7 +156,7 @@
         out_specs=[col(seq),pl.BlockSpec((1,2,seq),lambda p:(p,0,0))],
         out_shape=[jax.ShapeDtypeStruct((seq,cols),BF),jax.ShapeDtypeStruct((pairs,2,seq),F32)],
         compiler_params=params(),
-        cost_estimate=pl.CostEstimate(flops=8*seq*text*cols*2,bytes_accessed=3*seq*cols*2,transcendentals=seq*text*pairs*2),name="cross_forward")(mask,q,k,v)
+        cost_estimate=TINY,name="cross_forward")(mask,q,k,v)
 def cross_bwd(mask,q,k,v,g,l):
     seq,cols=q.shape; text=k.shape[0]; pairs=cols//128
     return pl.pallas_call(lambda *r: cross_bwd_kernel(*r,seq=seq),grid=(pairs,),
@@ -163,7 +164,89 @@
         out_specs=[col(seq),col(text),col(text)],
         out_shape=[jax.ShapeDtypeStruct((seq,cols),BF),jax.ShapeDtypeStruct((text,cols),BF),jax.ShapeDtypeStruct((text,cols),BF)],
         compiler_params=params(),
-        cost_estimate=pl.CostEstimate(flops=20*seq*text*cols*2,bytes_accessed=5*seq*cols*2,transcendentals=seq*text*pairs*2),name="cross_backward")(mask,q,k,v,g,l)
+        cost_estimate=TINY,name="cross_backward")(mask,q,k,v,g,l)
+
+def split_halves(a,b):
+    half,m,rows,cols=a.shape[0]//2,*a.shape[1:]
+    def body(a_ref,b_ref,x_ref,y_ref):
+        x_ref[...]=a_ref[...]
+        y_ref[...]=b_ref[...]
+    block=(half,1,rows,cols)
+    out=jax.ShapeDtypeStruct((half,m,rows,cols),a.dtype)
+    return pl.pallas_call(body,grid=(m,),
+        in_specs=[pl.BlockSpec(block,lambda i:(0,i,0,0)),pl.BlockSpec(block,lambda i:(1,i,0,0))],
+        out_specs=[pl.BlockSpec(block,lambda i:(0,i,0,0))]*2,out_shape=[out,out],compiler_params=params(),
+        cost_estimate=TINY,name="split_halves")(a,b)
+
+def place_pieces(groups,rows):
+    first=groups[0][0]
+    _,m,_,cols=first.shape
+    width=sum(v.shape[0] for v in groups[0])*cols
+    flat=[v for g in groups for v in g]
+    shapes=[[v.shape[0] for v in g] for g in groups]
+    def body(*refs):
+        ins,out=refs[:len(flat)],refs[len(flat)]
+        at=0
+        for p,s in enumerate(shapes):
+            def fill(at=at,s=s):
+                z=0
+                for i,k in enumerate(s):
+                    for j in range(k):
+                        out[:,:,z*cols:(z+1)*cols]=ins[at+i][j,:,0:rows,:]; z+=1
+            pl.when(pl.program_id(0)==p)(fill)
+            at+=len(s)
+    return pl.pallas_call(body,grid=(len(groups),),
+        in_specs=[pl.BlockSpec(v.shape,lambda p:(0,0,0,0),pipeline_mode=pl.Buffered(1)) for v in flat],
+        out_specs=pl.BlockSpec((m,rows,width),lambda p:(0,p,0)),
+        out_shape=jax.ShapeDtypeStruct((m,rows*len(groups),width),first.dtype),compiler_params=params(),
+        cost_estimate=TINY,name="place_pieces")(*flat)
+
+def hidden_up_kernel(h_ref, w_ref, e_ref, s_ref):
+    w=w_ref[0]
+    for i in range(h_ref.shape[0]//256):
+        rows=slice(i*256,(i+1)*256)
+        u=dot(h_ref[rows,:],w,NN)
+        uu=u*u
+        t=jnp.tanh(u*(0.7978845608028654+(0.7978845608028654*0.044715)*uu))
+        p=0.5+0.5*t
+        e_ref[rows,:]=(u*p).astype(BF)
+        s_ref[rows,:]=(p+u*(p*(1.0-t))*(0.7978845608028654+(3.0*0.7978845608028654*0.044715)*uu)).astype(BF)
+
+def hidden_up(h,w):
+    rows,depth=h.shape; parts,_,cols=w.shape; blk=256; per=cols//blk
+    out=pl.BlockSpec((rows,blk),lambda j:(0,j))
+    return pl.pallas_call(hidden_up_kernel,grid=(parts*per,),
+        in_specs=[pl.BlockSpec((rows,depth),lambda j:(0,0)),pl.BlockSpec((1,depth,blk),lambda j:(j//per,0,j%per))],
+        out_specs=[out,out],out_shape=[jax.ShapeDtypeStruct((rows,parts*cols),BF)]*2,compiler_params=params(),
+        cost_estimate=TINY,name="hidden_up")(h,w)
+
+def hidden_slope_kernel(g_ref, w_ref, s_ref, d_ref):
+    w=w_ref[0]
+    for i in range(g_ref.shape[0]//256):
+        rows=slice(i*256,(i+1)*256)
+        d_ref[rows,:]=(dot(g_ref[rows,:],w,NN)*s_ref[rows,:].astype(F32)).astype(BF)
+
+def hidden_slope(g,w,s):
+    rows,depth=g.shape; parts,_,cols=w.shape; blk=256; per=cols//blk
+    out=pl.BlockSpec((rows,blk),lambda j:(0,j))
+    return pl.pallas_call(hidden_slope_kernel,grid=(parts*per,),
+        in_specs=[pl.BlockSpec((rows,depth),lambda j:(0,0)),pl.BlockSpec((1,depth,blk),lambda j:(j//per,0,j%per)),out],
+        out_specs=out,out_shape=jax.ShapeDtypeStruct((rows,parts*cols),BF),compiler_params=params(),
+        cost_estimate=TINY,name="hidden_slope")(g,w,s)
+
+def hidden_down_kernel(a_ref, w_ref, y_ref):
+    cols=w_ref.shape[2]
+    total=dot(a_ref[:,0:cols],w_ref[0],NT)
+    for z in range(1,w_ref.shape[0]):
+        total=total+dot(a_ref[:,z*cols:(z+1)*cols],w_ref[z],NT)
+    y_ref[...]=total.astype(y_ref.dtype)
+
+def hidden_down(a,w,half,kind):
+    rows=a.shape[0]//2; parts,depth,cols=w.shape; blk=256
+    return pl.pallas_call(hidden_down_kernel,grid=(depth//blk,),
+        in_specs=[pl.BlockSpec((rows,parts*cols),lambda j:(half,0)),pl.BlockSpec((parts,blk,cols),lambda j:(0,j,0))],
+        out_specs=pl.BlockSpec((rows,blk),lambda j:(0,j)),out_shape=jax.ShapeDtypeStruct((rows,depth),kind),compiler_params=params(),
+        cost_estimate=TINY,name="hidden_down")(a,w)
 
 
 from jax.sharding import PartitionSpec as P
@@ -185,6 +268,10 @@
 OUTWARD = [(1, 0), (2, 3)]
 INWARD = [(0, 1), (3, 2)]
 ACROSS = [(0, 2), (1, 3), (2, 0), (3, 1)]
+
+
+def tie(*values):
+    return lax.optimization_barrier(values)
 
 
 def swap_dp(value, size, bit):
@@ -264,80 +351,148 @@
         keep = lax.dynamic_slice_in_dim(stack, core * half, half, 2)
         send = lax.dynamic_slice_in_dim(stack, (1 - core) * half, half, 2)
         recv = swap_core(send)
-        return jnp.stack([pick(keep, recv), pick(recv, keep)], 1)
-
-    def gather_line(own):
-        beside = move_mp(own, PAIR)
-        near = jnp.concatenate([own, beside], -1)
-        far = move_mp(near, MIDDLE)
-        outer = move_mp(far, OUTWARD)
-        return jnp.concatenate([near, jnp.where(middle, far, outer)], -1)
-
-    def gather_chips(own, order):
-        found = {0: own}
-        for b in order:
-            codes = sorted(found)
-            sent = found[codes[0]] if len(codes) == 1 else jnp.concatenate([found[c] for c in codes], 1)
-            got = swap_dp(sent, size, b)
-            rows = own.shape[1]
-            for i, c in enumerate(codes):
-                found[c ^ b] = lax.slice_in_dim(got, i * rows, (i + 1) * rows, axis=1)
+        return jnp.concatenate([pick(keep, recv), pick(recv, keep)], 1)
+
+    pairs = [bits[i : i + 2] for i in range(0, len(bits), 2)]
+
+    near = pairs[0] if pairs else []
+
+    def phase_low(low):
+        return {b: swap_dp(low, size, b) for b in near}
+
+    def phase_on(low, high, lows, highs):
+        found = {0: (low, high)}
+        for b in near:
+            found[b] = (lows[b], highs[b])
+        if len(near) == 2:
+            a, b = near
+            found[a ^ b] = (swap_dp(lows[b], size, a), swap_dp(highs[a], size, b))
+        for bit in bits[2:]:
+            for c in sorted(found):
+                found[c ^ bit] = tuple(swap_dp(v, size, bit) for v in found[c])
         return found
 
-    def gather_group(own):
-        line = gather_line(own)
-        first = gather_chips(line[:, 0], bits[::-1])
-        second = gather_chips(line[:, 1], bits)
-        pieces = []
+    def whole_on(line, wholes):
+        found = {0: (line,)}
+        for b in near:
+            found[b] = (wholes[b],)
+        if len(near) == 2:
+            a, b = near
+            low, high = split_halves(wholes[b], wholes[a])
+            found[a ^ b] = (swap_dp(low, size, a), swap_dp(high, size, b))
+        for bit in bits[2:]:
+            for c in sorted(found):
+                found[c ^ bit] = tuple(swap_dp(v, size, bit) for v in found[c])
+        return found
+
+    def assemble(found):
+        return place_pieces([found[2 * p] for p in range(chips)], 2 * part)
+
+    def assemble_gains(found):
+        per = norm_gains.shape[1]
+        count = 2 * 2 * 6 * per
+        rows = []
         for p in range(chips):
-            pieces += [first[2 * p], second[2 * p]]
-        return jnp.concatenate(pieces, 1)
-
-    def scatter_chips(found, order):
-        for b in reversed(order):
-            codes = sorted(c for c in found if not c & b)
-            sent = jnp.concatenate([found[c ^ b] for c in codes], 1)
-            got = swap_dp(sent, size, b)
+            pieces = [v[z, 0, 2 * part :].reshape(-1)[:count] for v in found[2 * p] for z in range(v.shape[0])]
+            rows.append(jnp.stack(pieces, 0).reshape(lines, 2, 2, 6, per).astype(F32))
+        stacked = jnp.stack(rows, 0)
+        stacked = jnp.stack(
+            [lax.dynamic_index_in_dim(stacked, (z - mp) % lines, 1, keepdims=False) for z in range(lines)], 2
+        )
+        total = stacked[:, :, :, 0] + stacked[:, :, :, 1]
+        return total.transpose(3, 0, 1, 2, 4).reshape(6, width)
+
+    def slices(grad):
+        half = grad.shape[-1] // 2
+        found = {}
+        for p in range(chips):
+            rows = lax.slice_in_dim(grad, p * 2 * part, (p + 1) * 2 * part, axis=1)
+            found[2 * p] = (rows[..., :half], rows[..., half:])
+        for bit in reversed(bits[2:]):
             found = {
-                c: found[c] + lax.slice_in_dim(got, i * part, (i + 1) * part, axis=1) for i, c in enumerate(codes)
+                c: tuple(u + swap_dp(v, size, bit) for u, v in zip(found[c], found[c ^ bit])) for c in found if not c & bit
             }
-        return found[0]
-
-    def scatter_line(total):
-        half = total.shape[-1] // 2
-        near, away = total[..., :half], total[..., half:]
-        away = away + move_mp(away, INWARD)
-        near = near + move_mp(away, MIDDLE)
-        quarter = half // 2
-        return near[..., :quarter] + move_mp(near[..., quarter:], PAIR)
-
-    def scatter_group(grad):
-        pieces = {}
-        for p in range(chips):
-            for h in range(2):
-                pieces[2 * p, h] = lax.slice_in_dim(grad, (2 * p + h) * part, (2 * p + h + 1) * part, axis=1)
-        first = scatter_chips({2 * p: pieces[2 * p, 0] for p in range(chips)}, bits[::-1])
-        second = scatter_chips({2 * p: pieces[2 * p, 1] for p in range(chips)}, bits)
-        mine = scatter_line(jnp.stack([first, second], 1))
-        keep = pick(mine[:, 0], mine[:, 1])
-        recv = swap_core(pick(mine[:, 1], mine[:, 0]))
+        return found
+
+    def back_far(found):
+        if len(near) < 2:
+            return {}
+        a, b = near
+        return {"low": swap_dp(found[a ^ b][0], size, a), "high": swap_dp(found[a ^ b][1], size, b)}
+
+    def back_plain(found):
+        if len(near) < 2:
+            return {}
+        a, b = near
+        return {"low": swap_dp(found[a][0], size, a), "high": swap_dp(found[b][1], size, b)}
+
+    def back_summed(found, far):
+        if not near:
+            return {}
+        if len(near) < 2:
+            return {"low": swap_dp(found[near[0]][0], size, near[0]), "high": swap_dp(found[near[0]][1], size, near[0])}
+        a, b = near
+        return {
+            "low": swap_dp(found[b][0] + far["low"], size, b),
+            "high": swap_dp(found[a][1] + far["high"], size, a),
+        }
+
+    def back_total(found, plain, summed):
+        low, high = found[0]
+        for got in (plain, summed):
+            if got:
+                low, high = low + got["low"], high + got["high"]
+        return jnp.concatenate([low, high], -1)
+
+    def lay(total):
+        quarter = total.shape[-1] // lines
+        return [total[..., z * quarter : (z + 1) * quarter] for z in range(lines)]
+
+    def lay_hidden(total):
+        group = 128 * lines
+        count = total.shape[-1] // group
+        return [
+            jnp.concatenate([total[..., j * group + z * 128 : j * group + (z + 1) * 128] for j in range(count)], -1)
+            for z in range(lines)
+        ]
+
+    def scatter_line(pieces):
+        return lax.psum_scatter(jnp.stack(pieces, 0), "mp", scatter_dimension=0, tiled=True)[0]
+
+    def scatter_shift(pieces):
+        total = pieces[0].astype(F32)
+        for k in range(1, lines):
+            total = total + move_mp(pieces[k], [(i, (i + k) % lines) for i in range(lines)]).astype(F32)
+        return total.astype(BF)
+
+    def scatter_core(mine):
+        keep = pick(mine[:, :part], mine[:, part:])
+        recv = swap_core(pick(mine[:, part:], mine[:, :part]))
         return jnp.concatenate([pick(keep, recv), pick(recv, keep)], -1).astype(F32)
 
     items = image_states.shape[0]
     run = image_states.shape[1] // 2
 
-    def bring(value):
+    def bring_core(value):
         blocks = value.reshape(items, 2, run, width)
         keep = pick(blocks[:, 0], blocks[:, 1])
         recv = swap_core(pick(blocks[:, 1], blocks[:, 0]))
-        whole = jnp.concatenate([pick(keep, recv), pick(recv, keep)], 0)
-        return reorder(lax.all_to_all(whole, "mp", 0, 0, tiled=True).reshape(lines * run, width))
-
-    def give(value, rows):
-        whole = lax.all_to_all(reorder(value).reshape(lines, rows, width), "mp", 0, 0, tiled=True)
+        return jnp.concatenate([pick(keep, recv), pick(recv, keep)], 0)
+
+    def bring_line(whole):
+        return lax.all_to_all(whole, "mp", 0, 0, tiled=True)
+
+    def bring_last(whole):
+        return reorder(whole.reshape(lines * run, width))
+
+    def give_line(value, rows):
+        return lax.all_to_all(reorder(value).reshape(lines, rows, width), "mp", 0, 0, tiled=True)
+
+    def give_core(whole):
         low, high = whole[:items], whole[items:]
         keep = pick(low, high)
         recv = swap_core(pick(high, low))
+        rows = whole.shape[1]
         return jnp.stack([pick(keep, recv), pick(recv, keep)], 1).reshape(items, 2 * rows, width).astype(F32)
 
     def both(value):
@@ -347,13 +502,6 @@
         half = left.shape[0] // 2
         other = dot(left[half:], right, dims).astype(BF)
         return dot(left[:half], right, dims) + swap_core(other).astype(F32)
-
-    low_inout = own_half(jnp.concatenate([input_weights[:3], output_weights[:1], input_weights[3:], output_weights[1:]], 0).astype(BF))
-    low_hidden = own_half(hidden_weights.astype(BF))
-
-    gains_all = lax.dynamic_update_slice(
-        jnp.zeros((6, width), F32), norm_gains, (0, (dp * lines + mp) * norm_gains.shape[1])
-    )
 
     def sum_all(value):
         bit = 1
@@ -363,15 +511,53 @@
         value = value + move_mp(value, PAIR)
         return value + move_mp(value, ACROSS)
 
-    gain_rows = reorder(sum_all(gains_all))
-    image_own = bring(image_states).astype(F32)
-
-    weights_self = gather_group(low_inout[:4])
-    weights_cross = gather_group(low_inout[4:])
-    weights_up = gather_group(low_hidden[:1])[0]
-    weights_down = gather_group(low_hidden[1:])[0]
-
-    cot_own = bring(cotangent)
+    def sum_fast(value):
+        value = value + swap_core(value)
+        for i in range(0, len(bits), 2):
+            pair = bits[i : i + 2]
+            others = pair + [sum(pair)] if len(pair) == 2 else pair
+            value = value + sum(swap_dp(value, size, b) for b in others)
+        shifts = [[(i, (i + k) % lines) for i in range(lines)] for k in range(1, lines)]
+        return value + sum(move_mp(value, pairs) for pairs in shifts)
+
+    low = jnp.concatenate([input_weights[:3], output_weights[:1], input_weights[3:], output_weights[1:]], 0).astype(BF)
+    own_inout = own_half(low)
+    own_hidden = own_half(hidden_weights.astype(BF))
+    blocks = own_hidden.shape[-1] // 128
+
+    def in_blocks(shard):
+        return jnp.stack([shard[:, j * 128 : (j + 1) * 128] for j in range(blocks)], 0)
+
+    rest = jnp.concatenate([own_inout[4:], in_blocks(own_hidden[0]), in_blocks(own_hidden[1])], 0)
+
+    gains_high = norm_gains.astype(BF)
+    gains_low = (norm_gains - gains_high.astype(F32)).astype(BF)
+    gains_own = jnp.stack([gains_high, gains_low], 0)
+    gains_recv = swap_core(gains_own)
+    gains_chip = jnp.stack([pick(gains_own, gains_recv), pick(gains_recv, gains_own)], 0)
+    extra = -(-gains_chip.size // 1024) * 8
+    gains_rows = jnp.pad(gains_chip.reshape(-1), (0, extra * 128 - gains_chip.size)).reshape(1, extra, 128)
+    gains_rows = jnp.pad(gains_rows, ((0, 3), (0, 0), (0, 0)))
+    own_self = jnp.concatenate([own_inout[:4], gains_rows], 1)
+
+    def shift(value, step):
+        return move_mp(value, [(i, (i - step) % lines) for i in range(lines)])
+
+    moved = [own_self] + [shift(own_self, k) for k in range(1, lines)]
+    image_core = bring_core(image_states)
+    mid = lines // 2
+    moved, image_core, rest = tie(moved, image_core, rest)
+    self_line = jnp.stack(moved, 0)
+    self_whole = phase_low(self_line)
+    image_line = bring_line(image_core)
+    self_whole, rest, image_line = tie(self_whole, rest, image_line)
+    line_cross = lax.all_gather(rest[:4], "mp", axis=0)
+    found_self = whole_on(self_line, self_whole)
+    image_all = both(bring_last(image_line))
+    line_cross, rest_hidden = tie(line_cross, rest[4:])
+    line_hidden = lax.all_gather(rest_hidden, "mp", axis=0)
+    cot_core = bring_core(cotangent)
+    line_hidden, cot_core = tie(line_hidden, cot_core)
 
     which = mp % items
     mine = lax.dynamic_index_in_dim(text_states, which, 0, keepdims=False)
@@ -383,63 +569,116 @@
 
     core_index = core.astype(jnp.int32).reshape(1)
 
-    unit, _ = norm_parts(image_own)
-    h1 = both((unit * gain_rows[0] + gain_rows[1]).astype(BF))
+    half = image_all.shape[0] // 2
+    found_self, image_all = tie(found_self, image_all)
+    weights_self = assemble(found_self)
+    gain_rows = assemble_gains(found_self)
+    cross_low, cross_high = line_cross[:mid], line_cross[mid:]
+    cross_lows = phase_low(cross_low)
+    image_float = image_all.astype(F32)
+    image_own = image_float[:half]
+    unit, _ = norm_parts(image_float)
+    h1 = (unit * gain_rows[0] + gain_rows[1]).astype(BF)
     q1, k1, v1 = (dot(h1, weights_self[j], NN).astype(BF) for j in range(3))
+    q1, k1, v1, cross_lows = tie(q1, k1, v1, cross_lows)
+    cross_highs = phase_low(cross_high)
     o1, l1 = self_fwd(core_index, q1, k1, v1)
+    o1, cross_lows, cross_highs, line_hidden = tie(o1, cross_lows, cross_highs, line_hidden)
+    found_cross = phase_on(cross_low, cross_high, cross_lows, cross_highs)
+    up_low, up_high = line_hidden[:mid, :blocks], line_hidden[mid:, :blocks]
+    down_low, down_high = line_hidden[:mid, blocks:], line_hidden[mid:, blocks:]
+    up_lows = phase_low(up_low)
     r1 = image_own + joined(o1, weights_self[3], NT)
     unit, _ = norm_parts(r1)
     h2 = both((unit * gain_rows[2] + gain_rows[3]).astype(BF))
+    h2, found_cross, up_lows = tie(h2, found_cross, up_lows)
+    weights_cross = assemble(found_cross)
+    up_highs = phase_low(up_high)
     q2 = dot(h2, weights_cross[0], NN).astype(BF)
     k2, v2 = (dot(text, weights_cross[j], NN).astype(BF) for j in (1, 2))
     o2, l2 = cross_fwd(valid, q2, k2, v2)
+    o2, up_lows, up_highs = tie(o2, up_lows, up_highs)
+    found_up = phase_on(up_low, up_high, up_lows, up_highs)
+    down_lows = phase_low(down_low)
+    cot_line = bring_line(cot_core)
     r2 = r1 + joined(o2, weights_cross[3], NT)
     unit, _ = norm_parts(r2)
     h3 = both((unit * gain_rows[4] + gain_rows[5]).astype(BF))
-    u = dot(h3, weights_up, NN)
-    bend = jnp.tanh(GELU_SCALE * (u + GELU_CUBIC * u * u * u))
-    e = (0.5 * u * (1.0 + bend)).astype(BF)
-    slope = (
-        0.5 * (1.0 + bend) + 0.5 * u * (1.0 - bend * bend) * GELU_SCALE * (1.0 + 3.0 * GELU_CUBIC * u * u)
-    ).astype(BF)
-    layer_own = r2 + joined(e, weights_down, NT)
-    layer_out = give(layer_own.astype(BF), run)
-
+    h3, found_up, down_lows = tie(h3, found_up, down_lows)
+    weights_up = assemble(found_up)
+    down_highs = phase_low(down_high)
+    e, slope = hidden_up(h3, weights_up)
+    e, down_lows, down_highs, cot_line = tie(e, down_lows, down_highs, cot_line)
+    found_down = phase_on(down_low, down_high, down_lows, down_highs)
+    cot_own = bring_last(cot_line)
     cot = both(cot_own)
     cot_float = cot_own.astype(F32)
     grad_down = dot(cot, e, TN).astype(BF)
-    shard_down = scatter_group(grad_down[None])
-    du = (dot(cot, weights_down, NN) * slope.astype(F32)).astype(BF)
+    e, slope, found_down, grad_down = tie(e, slope, found_down, grad_down)
+    weights_down = assemble(found_down)
+
+    def joined_hidden(value, weights):
+        other = hidden_down(value, weights, 1, BF)
+        return hidden_down(value, weights, 0, F32) + swap_core(other).astype(F32)
+
+    send_down = slices(grad_down[None])
+    far_down = back_far(send_down)
+    du = hidden_slope(cot, weights_down, slope)
+    du, far_down = tie(du, far_down)
+    plain_down = back_plain(send_down)
     grad_up = dot(h3, du, TN).astype(BF)
-    shard_up = scatter_group(grad_up[None])
-    dh3 = joined(du, weights_up, NT)
+    grad_up, far_down, plain_down = tie(grad_up, far_down, plain_down)
+    summed_down = back_summed(send_down, far_down)
+    send_up = slices(grad_up[None])
+    far_up = back_far(send_up)
+    dh3 = joined_hidden(du, weights_up)
     back, gain_five, shift_six = norm_back(r2, dh3, gain_rows[4])
     dr2 = cot_float + back
     z2 = both(dr2.astype(BF))
+    z2, summed_down, far_up = tie(z2, summed_down, far_up)
+    plain_up = back_plain(send_up)
+    near_down = scatter_line(lay_hidden(back_total(send_down, plain_down, summed_down)))
+    layer_own = r2 + joined_hidden(e, weights_down)
     do2 = dot(z2, weights_cross[3], NN).astype(BF)
     go1 = dot(z2, o2, TN).astype(BF)
     dq2, dk2, dv2 = cross_bwd(valid, q2, k2, v2, do2, l2)
+    dq2, dk2, dv2, plain_up, far_up, layer_own = tie(dq2, dk2, dv2, plain_up, far_up, layer_own)
+    layer_line = give_line(layer_own.astype(BF), run)
+    summed_up = back_summed(send_up, far_up)
     dh2 = joined(dq2, weights_cross[0], NT)
     gi3 = dot(h2, dq2, TN).astype(BF)
     gi4 = dot(text, dk2, TN).astype(BF)
     gi5 = dot(text, dv2, TN).astype(BF)
-    shard_cross = scatter_group(jnp.stack([gi3, gi4, gi5, go1]))
+    back, gain_three, shift_four = norm_back(r1, dh2, gain_rows[2])
+    dr1 = dr2 + back
+    z1 = both(dr1.astype(BF))
+    z1, summed_up, gi3, gi4, gi5, go1 = tie(z1, summed_up, gi3, gi4, gi5, go1)
+    send_cross = slices(jnp.stack([gi3, gi4, gi5, go1]))
+    far_cross = back_far(send_cross)
+    near_up = scatter_line(lay_hidden(back_total(send_up, plain_up, summed_up)))
     text_part = dot(dk2, weights_cross[1], NT) + dot(dv2, weights_cross[2], NT)
     share = text.shape[0] // (2 * lines)
     text_part = text_part.reshape(lines, 2, share, width)
     text_own = pick(text_part[:, 0], text_part[:, 1]) + swap_core(
         pick(text_part[:, 1], text_part[:, 0]).astype(BF)
     ).astype(F32)
-    text_gradient = give(text_own.astype(BF).reshape(lines * share, width), share)
-    back, gain_three, shift_four = norm_back(r1, dh2, gain_rows[2])
-    dr1 = dr2 + back
-    z1 = both(dr1.astype(BF))
+    text_line = give_line(text_own.astype(BF).reshape(lines * share, width), share)
     do1 = dot(z1, weights_self[3], NN).astype(BF)
     go0 = dot(z1, o1, TN).astype(BF)
+    do1, go0, far_cross, layer_line = tie(do1, go0, far_cross, layer_line)
+    plain_cross = back_plain(send_cross)
+    summed_cross = back_summed(send_cross, far_cross)
     dq1, dk1, dv1 = self_bwd(core_index, q1, k1, v1, do1, l1)
+    dq1, dk1, dv1, plain_cross, summed_cross, text_line = tie(dq1, dk1, dv1, plain_cross, summed_cross, text_line)
     gi0, gi1, gi2 = (dot(h1, g, TN).astype(BF) for g in (dq1, dk1, dv1))
-    shard_self = scatter_group(jnp.stack([gi0, gi1, gi2, go0]))
-    half = dq1.shape[0] // 2
+    grad_self = jnp.stack([gi0, gi1, gi2, go0])
+    send_self = slices(grad_self)
+    far_self = back_far(send_self)
+    plain_self = back_plain(send_self)
+    send_self, dq1, dk1, dv1, plain_cross, summed_cross, near_up, near_down = tie(
+        send_self, dq1, dk1, dv1, plain_cross, summed_cross, near_up, near_down
+    )
+    near_cross = scatter_line(lay(back_total(send_cross, plain_cross, summed_cross)))
 
     def three(at):
         return (
@@ -447,10 +686,23 @@
         )
 
     dh1 = three(slice(0, half)) + swap_core(three(slice(half, None)).astype(BF)).astype(F32)
+    dh1, far_self, plain_self = tie(dh1, far_self, plain_self)
+    summed_self = back_summed(send_self, far_self)
     back, gain_one, shift_two = norm_back(image_own, dh1, gain_rows[0])
-    image_gradient = give((dr1 + back).astype(BF), run)
-
-    gains_total = sum_all(reorder(jnp.stack([gain_one, shift_two, gain_three, shift_four, gain_five, shift_six])))
+    image_own_grad = (dr1 + back).astype(BF)
+    gains_total = reorder(jnp.stack([gain_one, shift_two, gain_three, shift_four, gain_five, shift_six]))
+    image_line = give_line(image_own_grad, run)
+    summed_self, gains_total = tie(summed_self, gains_total)
+    gains_total = sum_all(gains_total)
+    near_self = scatter_shift(lay(back_total(send_self, plain_self, summed_self)))
+    near_self, image_line, near_cross, near_up, near_down = tie(near_self, image_line, near_cross, near_up, near_down)
+    shard_down = scatter_core(near_down)
+    shard_up = scatter_core(near_up)
+    shard_cross = scatter_core(near_cross)
+    shard_self = scatter_core(near_self)
+    layer_out = give_core(layer_line)
+    image_gradient = give_core(image_line)
+    text_gradient = give_core(text_line)
     gains_shard = lax.dynamic_slice_in_dim(
         gains_total, (dp * lines + mp) * norm_gains.shape[1], norm_gains.shape[1], 1
     )
@@ -460,7 +712,7 @@
     hidden_shard = jnp.concatenate([shard_up, shard_down], 0)
     square_total = jnp.sum(input_shard * input_shard) + jnp.sum(output_shard * output_shard)
     square_total = square_total + jnp.sum(hidden_shard * hidden_shard) + jnp.sum(gains_shard * gains_shard)
-    global_norm = jnp.sqrt(sum_all(jnp.full((8, 128), square_total)))[0, 0]
+    global_norm = jnp.sqrt(sum_fast(jnp.full((8, 128), square_total)))[0, 0]
     factor = jnp.minimum(1.0, CLIP_LIMIT / (global_norm + 1e-06))
     input_updated, input_moment, input_square = adam_update(
         input_weights, input_shard, input_momentum, input_variance, factor, LEARN_RATE, WEIGHT_DECAY

time: 755 us -> 618 us (0.82)
  waiting for transfers between devices: 306 us -> 179 us
  starting transfers between devices: 156 us -> 101 us
  Pallas kernels: 50.1 us -> 96.3 us
  matrix products: 96.8 us -> 71.7 us
  between operations: 6.64 us -> 20.3 us
  other arithmetic: 83.1 us -> 95.6 us
    ppermute x67 -> x80, waiting for transfers between devices: 200 us -> 114 us  [swap_dp(): return lax.ppermute(value, 'dp', [(i, i ^ bit) for i in range(size)])]
    ppermute x30 -> x11, starting transfers between devices: 67.5 us -> 19 us  [move_mp(): return lax.ppermute(value, 'mp', pairs)]
    pallas_call x0 -> x11, Pallas kernels: none -> 46.7 us  [the longest x4 15.6 us: hidden_down(): pl.pallas_call(hidden_down_kernel, grid=(depth // blk,), in_specs=[pl.Blo...]
    ppermute x30 -> x11, waiting for transfers between devices: 83.8 us -> 51.3 us  [move_mp(): return lax.ppermute(value, 'mp', pairs)]
    dot_general x38 -> x32, matrix products: 96.8 us -> 71.7 us  [dot(): return lax.dot_general(a, b, dims, preferred_element_type=F32)]
    all_to_all x5, starting transfers between devices: 40.2 us -> 22 us  [the longest x3 13.3 us: give_line(): lax.all_to_all(reorder(value).reshape(lines, rows, width), 'mp', 0, 0, ti...]
    all_to_all x5, waiting for transfers between devices: 21.8 us -> 4.9 us  [the longest x3 4.9 us: give_line(): lax.all_to_all(reorder(value).reshape(lines, rows, width), 'mp', 0, 0, ti...]
    slice x9 -> x19, local copies, waits for them, and re-layouts: 1.66 us -> 13.2 us  [the longest x4 3.54 us: slices(): found[2 * p] = (rows[..., :half], rows[..., half:])]
  transfers between devices with their start and end apart: 102 -> 101, of which waited for: 39 -> 33; matrix products, arithmetic and copies ran while one was open for 25% -> 27% of each run, Pallas kernels for 7% -> 15%
where the time goes in v2:
time: 618 us; the launch traced here: 613 us
  waiting for transfers between devices  179 us (29%)
  starting transfers between devices  101 us (16%)
  Pallas kernels  96.3 us (16%)
  other arithmetic  95.6 us (15%)
  matrix products  71.7 us (12%)
  local copies, waits for them, and re-layouts  49.8 us (8%)
  between operations  20.3 us (3%)
    ppermute x80, waiting for transfers between devices, swap_dp(): return lax.ppermute(value, 'dp', [(i, i ^ bit) for i in range(size)])  114 us
    dot_general x32, matrix products, dot(): return lax.dot_general(a, b, dims, preferred_element_type=F32)  71.7 us
    ppermute x80, starting transfers between devices, swap_dp(): return lax.ppermute(value, 'dp', [(i, i ^ bit) for i in range(size)])  58.8 us
    ppermute x11, waiting for transfers between devices, move_mp(): return lax.ppermute(value, 'mp', pairs)  51.3 us
    unnamed x319, local copies, waits for them, and re-layouts  25.2 us
    ppermute x11, starting transfers between devices, move_mp(): return lax.ppermute(value, 'mp', pairs)  19 us
    pallas_call x1, Pallas kernels, self_bwd(): pl.pallas_call(lambda *r: self_bwd_kernel(*r, seq=seq), grid_spec=pltpu.P...  17.1 us
    pallas_call x1, Pallas kernels, self_fwd(): pl.pallas_call(lambda *r: self_fwd_kernel(*r, seq=seq), grid_spec=pltpu.P...  16.9 us
  transfers between devices with their start and end apart: 101, of which 33 were waited for; matrix products, arithmetic and copies ran while one was open for 27% of the time, Pallas kernels for 15%

profile of v2, /device:TPU:0, one launch (start us, length us, event | category | flops | bytes accessed | tf_op | source)
XLA Modules:
  0.0 613.4 jit_solution(16887889871909881067)
XLA Ops:
  14.2 5.1 collective-permute-start.2
  26.2 16.3 %collective-permute-done.3 = bf16[4,264,128]{2,1,0:T(8,128)(2,1)S(1)} collective-permute-done((bf16[4,264,128]{2,1,0:T(8,128)(2,1)S(1)}, bf16[4,264,128]{2,1,0:T(8,128)(2,1)S(1)}, u32[]{:S(2)}, u32[]{:S(2)}) %collective-permute-start.3) | collective-permute-done | bytes 270368 | tf_op jit(solution)/shard_map/ppermute | solution.py:282
  42.5 4.2 all-to-all-start
  51.0 21.9 %collective-permute-done.7.b_ref.refs_1_ = bf16[4,4,264,128]{3,2,1,0:T(8,128)(2,1)S(1)} collective-permute-done((bf16[4,4,264,128]{3,2,1,0:T(8,128)(2,1)S(1)}, bf16[4,4,264,128]{3,2,1,0:T(8,128)(2,1)S(1)}, u32[]{:S(2)}, u32[]{:S(2)}) %collective-permute-start.7) | collective-permute-done | bytes 1081376 | tf_op jit(solution)/shard_map/ppermute | solution.py:278
  90.3 6.4 %collective-permute-done.9.refs_3_ = bf16[2,4,264,128]{3,2,1,0:T(8,128)(2,1)} collective-permute-done((bf16[2,4,264,128]{3,2,1,0:T(8,128)(2,1)}, bf16[2,4,264,128]{3,2,1,0:T(8,128)(2,1)}, u32[]{:S(2)}, u32[]{:S(2)}) %collective-permute-start.9) | collective-permute-done | bytes 540704 | tf_op jit(solution)/shard_map/ppermute | solution.py:278
  99.9 8.1 %all-gather.5.cloned.1.call-done = bf16[16,256,128]{2,1,0:T(8,128)(2,1)} async-done(((bf16[4,256,128]{2,1,0:T(8,128)(2,1)}), bf16[16,256,128]{2,1,0:T(8,128)(2,1)}) %all-gather.5.cloned.1.call-update) | async-done | bytes 1048592 | tf_op jit(solution)/shard_map/all_gather | solution.py:554
  127.2 8.3 %collective-permute-done.12.refs_2_ = bf16[2,4,256,128]{3,2,1,0:T(8,128)(2,1)S(1)} collective-permute-done((bf16[2,4,256,128]{3,2,1,0:T(8,128)(2,1)S(1)}, bf16[2,4,256,128]{3,2,1,0:T(8,128)(2,1)S(1)}, u32[]{:S(2)}, u32[]{:S(2)}) %collective-permute-start.12) | collective-permute-done | bytes 524320 | tf_op jit(solution)/shard_map/ppermute | solution.py:278
  137.0 16.9 %self_forward.1 = (bf16[1024,512]{1,0:T(8,128)(2,1)S(1)}, f32[4,2,1024]{2,1,0:T(2,128)S(1)}) custom-call(s32[1]{0:T(128)} %bitcast.23.r_0_, bf16[1024,512]{1,0:T(8,128)(2,1)S(1)} %convolution_convert_fusion.15.r_1_, bf16[1024,512]{1,0:T(8,128)(2,1)S(1)} %convolution_convert_fusion.14.r_2_, bf16[1024,512]{1,0:T(8,128)(2,1)S(1)} %convolution_convert_fusion.13.r_3_), custom_call_target="tpu_custom_call" | custom-call | flops 1 | bytes 1 | tf_op jit(solution)/shard_map/self_forward/pallas_call | solution.py:138
  159.1 4.1 convert_element_type.239
  178.7 19.1 %collective-permute-done.20.refs_6_ = bf16[2,4,256,128]{3,2,1,0:T(8,128)(2,1)S(1)} collective-permute-done((bf16[2,4,256,128]{3,2,1,0:T(8,128)(2,1)S(1)}, bf16[2,4,256,128]{3,2,1,0:T(8,128)(2,1)S(1)}, u32[]{:S(2)}, u32[]{:S(2)}) %collective-permute-start.20) | collective-permute-done | bytes 524320 | tf_op jit(solution)/shard_map/ppermute | solution.py:278
  204.4 6.3 %cross_forward.1 = (bf16[1024,512]{1,0:T(8,128)(2,1)S(1)}, f32[4,2,1024]{2,1,0:T(2,128)S(1)}) custom-call(f32[128,128]{1,0:T(8,128)S(1)} %broadcast_in_dim.8.r_0_, bf16[1024,512]{1,0:T(8,128)(2,1)S(1)} %convolution_convert_fusion.12.r_1_, bf16[128,512]{1,0:T(8,128)(2,1)S(1)} %convolution_convert_fusion.20.r_2_, ...), custom_call_target="tpu_custom_call" | custom-call | flops 1 | bytes 1 | tf_op jit(solution)/shard_map/cross_forward/pallas_call | solution.py:154
  219.5 4.5 all-to-all-start.1
  228.2 10.9 %collective-permute-done.31.refs_2_ = bf16[2,4,256,128]{3,2,1,0:T(8,128)(2,1)S(1)} collective-permute-done((bf16[2,4,256,128]{3,2,1,0:T(8,128)(2,1)}, bf16[2,4,256,128]{3,2,1,0:T(8,128)(2,1)S(1)}, u32[]{:S(2)}, u32[]{:S(2)}) %collective-permute-start.31) | collective-permute-done | bytes 524320 | tf_op jit(solution)/shard_map/ppermute | solution.py:278
  244.5 5.8 collective-permute-done.29.refs_6_
  255.8 11.5 %hidden_up.1 = (bf16[1024,2048]{1,0:T(8,128)(2,1)S(1)}, bf16[1024,2048]{1,0:T(8,128)(2,1)S(1)}) custom-call(bf16[1024,1024]{1,0:T(8,128)(2,1)S(1)} %pad_maximum_fusion.4.h_ref, bf16[4,1024,512]{2,1,0:T(8,128)(2,1)} %copy-done.2), custom_call_target="tpu_custom_call" | custom-call | flops 1 | bytes 1 | tf_op jit(solution)/shard_map/hidden_up/pallas_call | solution.py:218
  276.3 10.2 %convolution_convert_fusion.1 = bf16[1024,2048]{1,0:T(8,128)(2,1)S(1)} fusion(bf16[1024,2048]{1,0:T(8,128)(2,1)S(1)} %copy-done.11, bf16[512,1024]{1,0:T(8,128)(2,1)S(1)} %collective-permute-done.35, bf16[512,256]{1,0:T(8,128)(2,1)S(1)} %get-tuple-element.423, bf16[512,256]{1,0:T(8,128)(2,1)S(1)} %get-tuple-element.424, ...), kind=kOutput, calls=%fused_computation.5 | convolution fusion | flops 4307550208 | bytes 10485760 | tf_op jit(solution)/shard_map/dot_general | solution.py:10
  296.5 8.5 %hidden_slope.1.a_ref = bf16[1024,2048]{1,0:T(8,128)(2,1)S(1)} custom-call(bf16[1024,1024]{1,0:T(8,128)(2,1)S(1)} %pad_maximum_fusion.5.g_ref, bf16[4,1024,512]{2,1,0:T(8,128)(2,1)S(1)} %place_pieces.7.w_ref, bf16[1024,2048]{1,0:T(8,128)(2,1)} %copy-done.16), custom_call_target="tpu_custom_call" | custom-call | flops 1 | bytes 1 | tf_op jit(solution)/shard_map/hidden_slope/pallas_call | solution.py:232
  305.1 4.4 hidden_down.5
  319.7 4.4 hidden_down.7
  336.3 4.8 convolution_convert_fusion
  348.3 9.8 %collective-permute-done.44 = bf16[1,256,1024]{2,1,0:T(8,128)(2,1)S(1)} collective-permute-done((bf16[1,256,1024]{2,1,0:T(8,128)(2,1)S(1)}, bf16[1,256,1024]{2,1,0:T(8,128)(2,1)S(1)}, u32[]{:S(2)}, u32[]{:S(2)}) %collective-permute-start.44) | collective-permute-done | bytes 524320 | tf_op jit(solution)/shard_map/ppermute | solution.py:278
  360.3 10.3 %collective-permute-done.46 = bf16[1,256,1024]{2,1,0:T(8,128)(2,1)S(1)} collective-permute-done((bf16[1,256,1024]{2,1,0:T(8,128)(2,1)S(1)}, bf16[1,256,1024]{2,1,0:T(8,128)(2,1)S(1)}, u32[]{:S(2)}, u32[]{:S(2)}) %collective-permute-start.46) | collective-permute-done | bytes 524320 | tf_op jit(solution)/shard_map/ppermute | solution.py:278
  371.8 9.3 %cross_backward.1 = (bf16[1024,512]{1,0:T(8,128)(2,1)S(1)}, bf16[128,512]{1,0:T(8,128)(2,1)S(1)}, bf16[128,512]{1,0:T(8,128)(2,1)S(1)}) custom-call(f32[128,128]{1,0:T(8,128)S(1)} %broadcast_in_dim.8.r_0_, bf16[1024,512]{1,0:T(8,128)(2,1)S(1)} %copy-done.22, bf16[128,512]{1,0:T(8,128)(2,1)S(1)} %convolution_convert_fusion.20.r_2_, ...), custom_call_target="tpu_custom_call" | custom-call | flops 1 | bytes 1 | tf_op jit(solution)/shard_map/cross_backward/pallas_call | solution.py:162
  386.8 5.1 all-to-all-start.2
  426.8 4.9 all-to-all-done.2
  446.1 17.1 %self_backward.1 = (bf16[1024,512]{1,0:T(8,128)(2,1)S(1)}, bf16[1024,512]{1,0:T(8,128)(2,1)S(1)}, bf16[1024,512]{1,0:T(8,128)(2,1)S(1)}) custom-call(s32[1]{0:T(128)} %bitcast.23.r_0_, bf16[1024,512]{1,0:T(8,128)(2,1)S(1)} %convolution_convert_fusion.15.r_1_, bf16[1024,512]{1,0:T(8,128)(2,1)S(1)} %copy-done.18, bf16[1024,512]{1,0:T(8,128)(2,1)S(1)} %copy-done.20, ...), custom_call_target="tpu_custom_call" | custom-call | flops 1 | bytes 1 | tf_op jit(solution)/shard_map/self_backward/pallas_call | solution.py:146
  510.8 4.9 all-to-all-start.4
  527.3 3.7 collective-permute-start.72
  534.5 13.8 %collective-permute-done.82 = f32[6,1024]{1,0:T(8,128)S(1)} collective-permute-done((f32[6,1024]{1,0:T(8,128)S(1)}, f32[6,1024]{1,0:T(8,128)S(1)}, u32[]{:S(2)}, u32[]{:S(2)}) %collective-permute-start.82) | collective-permute-done | bytes 24608 | tf_op jit(solution)/shard_map/ppermute | solution.py:282
  548.3 4.6 collective-permute-start.83
  552.9 15.2 %collective-permute-done.83 = f32[6,1024]{1,0:T(8,128)S(1)} collective-permute-done((f32[6,1024]{1,0:T(8,128)S(1)}, f32[6,1024]{1,0:T(8,128)S(1)}, u32[]{:S(2)}, u32[]{:S(2)}) %collective-permute-start.83) | collective-permute-done | bytes 24608 | tf_op jit(solution)/shard_map/ppermute | solution.py:282
  591.7 3.5 collective-permute-done.88
  (743 shorter events, 309.3 us)
Async XLA Ops:
  42.5 31.6 %all-to-all-start = ((bf16[4,128,1024]{2,1,0:T(8,128)(2,1)}), bf16[4,128,1024]{2,1,0:T(8,128)(2,1)}, u32[]{:S(2)}, u32[]{:S(2)}) async-start(bf16[4,128,1024]{2,1,0:T(8,128)(2,1)} %pad_maximum_fusion.9), calls=%async_computation | async-start | bytes 2097152 | tf_op jit(solution)/shard_map/all_to_all | solution.py:483
  46.7 61.3 %all-gather.5.cloned.1.call-start = ((), (), s32[]{:S(2)}) async-start(), calls=%async_computation.11 | async-start | bytes 1310720 | tf_op jit(solution)/shard_map/all_gather | solution.py:554
  47.9 25.0 %collective-permute-start.7 = (bf16[4,4,264,128]{3,2,1,0:T(8,128)(2,1)S(1)}, bf16[4,4,264,128]{3,2,1,0:T(8,128)(2,1)S(1)}, u32[]{:S(2)}, u32[]{:S(2)}) collective-permute-start(bf16[4,4,264,128]{3,2,1,0:T(8,128)(2,1)S(1)} %pad_maximum_fusion.8.refs_0_), channel_id=1, source_target_pairs={{0,8},{4,12},{8,0},{12,4},{16,24},{20,28},{24,16},{28,20},{1,9},{5... | collective-permute-start | bytes 3244040 | tf_op jit(solution)/shard_map/ppermute | solution.py:278
  49.4 24.7 %collective-permute-start.8 = (bf16[4,4,264,128]{3,2,1,0:T(8,128)(2,1)S(1)}, bf16[4,4,264,128]{3,2,1,0:T(8,128)(2,1)S(1)}, u32[]{:S(2)}, u32[]{:S(2)}) collective-permute-start(bf16[4,4,264,128]{3,2,1,0:T(8,128)(2,1)S(1)} %pad_maximum_fusion.8.refs_0_), channel_id=1, source_target_pairs={{0,16},{4,20},{8,24},{12,28},{16,0},{20,4},{24,8},{28,12},{1,17},{... | collective-permute-start | bytes 3244040 | tf_op jit(solution)/shard_map/ppermute | solution.py:278
  79.8 76.1 %all-gather.7.cloned.1.call-start = ((), (), s32[]{:S(2)}) async-start(), calls=%async_computation.12 | async-start | bytes 2621440 | tf_op jit(solution)/shard_map/all_gather | solution.py:558
  123.6 32.3 %collective-permute-start.14 = (bf16[2,4,256,128]{3,2,1,0:T(8,128)(2,1)S(1)}, bf16[2,4,256,128]{3,2,1,0:T(8,128)(2,1)}, u32[]{:S(2)}, u32[]{:S(2)}) collective-permute-start(bf16[2,4,256,128]{3,2,1,0:T(8,128)(2,1)S(1)} %get-tuple-element.207.refs_1_), channel_id=1, source_target_pairs={{0,8},{4,12},{8,0},{12,4},{16,24},{20,28},{24,16},{28,20},{1,9},{5... | collective-permute-start | bytes 1572872 | tf_op jit(solution)/shard_map/ppermute | solution.py:278
  124.2 31.7 %collective-permute-start.15 = (bf16[2,4,256,128]{3,2,1,0:T(8,128)(2,1)S(1)}, bf16[2,4,256,128]{3,2,1,0:T(8,128)(2,1)}, u32[]{:S(2)}, u32[]{:S(2)}) collective-permute-start(bf16[2,4,256,128]{3,2,1,0:T(8,128)(2,1)S(1)} %get-tuple-element.207.refs_1_), channel_id=1, source_target_pairs={{0,16},{4,20},{8,24},{12,28},{16,0},{20,4},{24,8},{28,12},{1,17},{... | collective-permute-start | bytes 1572872 | tf_op jit(solution)/shard_map/ppermute | solution.py:278
  171.7 27.6 %collective-permute-start.22 = (bf16[2,4,256,128]{3,2,1,0:T(8,128)(2,1)S(1)}, bf16[2,4,256,128]{3,2,1,0:T(8,128)(2,1)S(1)}, u32[]{:S(2)}, u32[]{:S(2)}) collective-permute-start(bf16[2,4,256,128]{3,2,1,0:T(8,128)(2,1)S(1)} %get-tuple-element.223.refs_0_), channel_id=1, source_target_pairs={{0,8},{4,12},{8,0},{12,4},{16,24},{20,28},{24,16},{28,20},{1,9},{5... | collective-permute-start | bytes 1572872 | tf_op jit(solution)/shard_map/ppermute | solution.py:278
  173.0 27.1 %collective-permute-start.23 = (bf16[2,4,256,128]{3,2,1,0:T(8,128)(2,1)S(1)}, bf16[2,4,256,128]{3,2,1,0:T(8,128)(2,1)}, u32[]{:S(2)}, u32[]{:S(2)}) collective-permute-start(bf16[2,4,256,128]{3,2,1,0:T(8,128)(2,1)S(1)} %get-tuple-element.223.refs_0_), channel_id=1, source_target_pairs={{0,16},{4,20},{8,24},{12,28},{16,0},{20,4},{24,8},{28,12},{1,17},{... | collective-permute-start | bytes 1572872 | tf_op jit(solution)/shard_map/ppermute | solution.py:278
  176.0 34.7 %collective-permute-start.25 = (bf16[2,4,256,128]{3,2,1,0:T(8,128)(2,1)S(1)}, bf16[2,4,256,128]{3,2,1,0:T(8,128)(2,1)}, u32[]{:S(2)}, u32[]{:S(2)}) collective-permute-start(bf16[2,4,256,128]{3,2,1,0:T(8,128)(2,1)S(1)} %get-tuple-element.224.refs_1_), channel_id=1, source_target_pairs={{0,8},{4,12},{8,0},{12,4},{16,24},{20,28},{24,16},{28,20},{1,9},{5... | collective-permute-start | bytes 1572872 | tf_op jit(solution)/shard_map/ppermute | solution.py:278
  219.5 52.5 %all-to-all-start.1 = ((bf16[4,128,1024]{2,1,0:T(8,128)(2,1)}), bf16[4,128,1024]{2,1,0:T(8,128)(2,1)}, u32[]{:S(2)}, u32[]{:S(2)}) async-start(bf16[4,128,1024]{2,1,0:T(8,128)(2,1)} %pad_maximum_fusion.11), calls=%async_computation.1 | async-start | bytes 2097152 | tf_op jit(solution)/shard_map/all_to_all | solution.py:483
  226.8 24.7 %collective-permute-start.30 = (bf16[2,4,256,128]{3,2,1,0:T(8,128)(2,1)}, bf16[2,4,256,128]{3,2,1,0:T(8,128)(2,1)S(1)}, u32[]{:S(2)}, u32[]{:S(2)}) collective-permute-start(bf16[2,4,256,128]{3,2,1,0:T(8,128)(2,1)} %collective-permute-done.25.refs_3_), channel_id=1, source_target_pairs={{0,16},{4,20},{8,24},{12,28},{16,0},{20,4},{24,8},{28,12},{1,17},{... | collective-permute-start | bytes 1572872 | tf_op jit(solution)/shard_map/ppermute | solution.py:278
  239.9 31.3 %collective-permute-start.33 = (bf16[2,4,256,128]{3,2,1,0:T(8,128)(2,1)}, bf16[2,4,256,128]{3,2,1,0:T(8,128)(2,1)}, u32[]{:S(2)}, u32[]{:S(2)}) collective-permute-start(bf16[2,4,256,128]{3,2,1,0:T(8,128)(2,1)} %get-tuple-element.243.refs_1_), channel_id=1, source_target_pairs={{0,8},{4,12},{8,0},{12,4},{16,24},{20,28},{24,16},{28,20},{1,9},{5... | collective-permute-start | bytes 1572872 | tf_op jit(solution)/shard_map/ppermute | solution.py:278
  242.1 29.1 %collective-permute-start.34 = (bf16[2,4,256,128]{3,2,1,0:T(8,128)(2,1)}, bf16[2,4,256,128]{3,2,1,0:T(8,128)(2,1)S(1)}, u32[]{:S(2)}, u32[]{:S(2)}) collective-permute-start(bf16[2,4,256,128]{3,2,1,0:T(8,128)(2,1)} %get-tuple-element.243.refs_1_), channel_id=1, source_target_pairs={{0,16},{4,20},{8,24},{12,28},{16,0},{20,4},{24,8},{28,12},{1,17},{... | collective-permute-start | bytes 1572872 | tf_op jit(solution)/shard_map/ppermute | solution.py:278
  345.4 25.1 %collective-permute-start.46 = (bf16[1,256,1024]{2,1,0:T(8,128)(2,1)S(1)}, bf16[1,256,1024]{2,1,0:T(8,128)(2,1)S(1)}, u32[]{:S(2)}, u32[]{:S(2)}) collective-permute-start(bf16[1,256,1024]{2,1,0:T(8,128)(2,1)S(1)} %get-tuple-element.383), channel_id=1, source_target_pairs={{0,16},{4,20},{8,24},{12,28},{16,0},{20,4},{24,8},{28,12},{1,17},{... | collective-permute-start | bytes 1572872 | tf_op jit(solution)/shard_map/ppermute | solution.py:278
  384.0 29.0 %collective-permute-start.53 = (bf16[1,256,1024]{2,1,0:T(8,128)(2,1)}, bf16[1,256,1024]{2,1,0:T(8,128)(2,1)}, u32[]{:S(2)}, u32[]{:S(2)}) collective-permute-start(bf16[1,256,1024]{2,1,0:T(8,128)(2,1)} %get-tuple-element.379), channel_id=1, source_target_pairs={{0,8},{4,12},{8,0},{12,4},{16,24},{20,28},{24,16},{28,20},{1,9},{5... | collective-permute-start | bytes 1572872 | tf_op jit(solution)/shard_map/ppermute | solution.py:278
  384.9 28.2 %collective-permute-start.54 = (bf16[1,256,1024]{2,1,0:T(8,128)(2,1)}, bf16[1,256,1024]{2,1,0:T(8,128)(2,1)}, u32[]{:S(2)}, u32[]{:S(2)}) collective-permute-start(bf16[1,256,1024]{2,1,0:T(8,128)(2,1)} %get-tuple-element.378), channel_id=1, source_target_pairs={{0,16},{4,20},{8,24},{12,28},{16,0},{20,4},{24,8},{28,12},{1,17},{... | collective-permute-start | bytes 1572872 | tf_op jit(solution)/shard_map/ppermute | solution.py:278
  386.8 45.0 %all-to-all-start.2 = ((bf16[4,128,1024]{2,1,0:T(8,128)(2,1)}), bf16[4,128,1024]{2,1,0:T(8,128)(2,1)}, u32[]{:S(2)}, u32[]{:S(2)}) async-start(bf16[4,128,1024]{2,1,0:T(8,128)(2,1)} %bitcast.318), calls=%async_computation.2 | async-start | bytes 2097152 | tf_op jit(solution)/shard_map/all_to_all | solution.py:489
  391.9 89.6 %reduce-scatter.6.cloned.1.call-start = ((), (), s32[]{:S(2)}) async-start(), calls=%async_computation.9 | async-start | bytes 1310720 | tf_op jit(solution)/shard_map/reduce_scatter | solution.py:460
  431.7 34.3 %all-to-all-start.3 = ((bf16[4,16,1024]{2,1,0:T(8,128)(2,1)}), bf16[4,16,1024]{2,1,0:T(8,128)(2,1)S(1)}, u32[]{:S(2)}, u32[]{:S(2)}) async-start(bf16[4,16,1024]{2,1,0:T(8,128)(2,1)} %bitcast.64), calls=%async_computation.3 | async-start | bytes 262144 | tf_op jit(solution)/shard_map/all_to_all | solution.py:489
  435.1 46.4 %reduce-scatter.4.cloned.1.call-start = ((), (), s32[]{:S(2)}) async-start(), calls=%async_computation.8 | async-start | bytes 1310720 | tf_op jit(solution)/shard_map/reduce_scatter | solution.py:460
  438.3 27.8 %collective-permute-start.58 = (bf16[4,256,256]{2,1,0:T(8,128)(2,1)}, bf16[4,256,256]{2,1,0:T(8,128)(2,1)}, u32[]{:S(2)}, u32[]{:S(2)}) collective-permute-start(bf16[4,256,256]{2,1,0:T(8,128)(2,1)} %get-tuple-element.375), channel_id=1, source_target_pairs={{0,16},{4,20},{8,24},{12,28},{16,0},{20,4},{24,8},{28,12},{1,17},{... | collective-permute-start | bytes 1572872 | tf_op jit(solution)/shard_map/ppermute | solution.py:278
  439.6 26.4 %collective-permute-start.59 = (bf16[4,256,256]{2,1,0:T(8,128)(2,1)}, bf16[4,256,256]{2,1,0:T(8,128)(2,1)}, u32[]{:S(2)}, u32[]{:S(2)}) collective-permute-start(bf16[4,256,256]{2,1,0:T(8,128)(2,1)} %get-tuple-element.374), channel_id=1, source_target_pairs={{0,8},{4,12},{8,0},{12,4},{16,24},{20,28},{24,16},{28,20},{1,9},{5... | collective-permute-start | bytes 1572872 | tf_op jit(solution)/shard_map/ppermute | solution.py:278
  440.8 25.2 %collective-permute-start.60 = (bf16[4,256,256]{2,1,0:T(8,128)(2,1)}, bf16[4,256,256]{2,1,0:T(8,128)(2,1)}, u32[]{:S(2)}, u32[]{:S(2)}) collective-permute-start(bf16[4,256,256]{2,1,0:T(8,128)(2,1)} %get-tuple-element.373), channel_id=1, source_target_pairs={{0,8},{4,12},{8,0},{12,4},{16,24},{20,28},{24,16},{28,20},{1,9},{5... | collective-permute-start | bytes 1572872 | tf_op jit(solution)/shard_map/ppermute | solution.py:278
  441.7 24.4 %collective-permute-start.61 = (bf16[4,256,256]{2,1,0:T(8,128)(2,1)}, bf16[4,256,256]{2,1,0:T(8,128)(2,1)}, u32[]{:S(2)}, u32[]{:S(2)}) collective-permute-start(bf16[4,256,256]{2,1,0:T(8,128)(2,1)} %get-tuple-element.372), channel_id=1, source_target_pairs={{0,16},{4,20},{8,24},{12,28},{16,0},{20,4},{24,8},{28,12},{1,17},{... | collective-permute-start | bytes 1572872 | tf_op jit(solution)/shard_map/ppermute | solution.py:278
  443.6 125.4 %reduce-scatter.8.cloned.1.call-start = ((), (), s32[]{:S(2)}) async-start(), calls=%async_computation.10 | async-start | bytes 1310720 | tf_op jit(solution)/shard_map/reduce_scatter | solution.py:460
  446.1 33.0 %collective-permute-start.57 = (bf16[2,128,1024]{2,1,0:T(8,128)(2,1)}, bf16[2,128,1024]{2,1,0:T(8,128)(2,1)}, u32[]{:S(2)}, u32[]{:S(2)}) collective-permute-start(bf16[2,128,1024]{2,1,0:T(8,128)(2,1)} %broadcast_select_fusion.4), channel_id=1, source_target_pairs={{0,4},{4,0},{8,12},{12,8},{16,20},{20,16},{24,28},{28,24},{1,5},{5... | collective-permute-start | bytes 1572872 | tf_op jit(solution)/shard_map/ppermute | solution.py:278
  510.8 58.2 %all-to-all-start.4 = ((bf16[4,128,1024]{2,1,0:T(8,128)(2,1)}), bf16[4,128,1024]{2,1,0:T(8,128)(2,1)S(1)}, u32[]{:S(2)}, u32[]{:S(2)}) async-start(bf16[4,128,1024]{2,1,0:T(8,128)(2,1)} %bitcast.85), calls=%async_computation.6 | async-start | bytes 2097152 | tf_op jit(solution)/shard_map/all_to_all | solution.py:489
  522.0 30.9 %collective-permute-start.74 = (bf16[2,16,1024]{2,1,0:T(8,128)(2,1)S(1)}, bf16[2,16,1024]{2,1,0:T(8,128)(2,1)S(1)}, u32[]{:S(2)}, u32[]{:S(2)}) collective-permute-start(bf16[2,16,1024]{2,1,0:T(8,128)(2,1)S(1)} %broadcast_select_fusion.27), channel_id=1, source_target_pairs={{0,4},{4,0},{8,12},{12,8},{16,20},{20,16},{24,28},{28,24},{1,5},{5... | collective-permute-start | bytes 196616 | tf_op jit(solution)/shard_map/ppermute | solution.py:278
  527.3 41.5 %collective-permute-start.72 = (bf16[4,256,128]{2,1,0:T(8,128)(2,1)S(1)}, bf16[4,256,128]{2,1,0:T(8,128)(2,1)S(1)}, u32[]{:S(2)}, u32[]{:S(2)}) collective-permute-start(bf16[4,256,128]{2,1,0:T(8,128)(2,1)S(1)} %get-tuple-element.445), channel_id=1, source_target_pairs={{0,3},{1,0},{2,1},{3,2},{4,7},{5,4},{6,5},{7,6},{8,11},{9,8},{10,9... | collective-permute-start | bytes 786440 | tf_op jit(solution)/shard_map/ppermute | solution.py:282
  531.0 37.8 %collective-permute-start.71 = (bf16[4,256,128]{2,1,0:T(8,128)(2,1)S(1)}, bf16[4,256,128]{2,1,0:T(8,128)(2,1)S(1)}, u32[]{:S(2)}, u32[]{:S(2)}) collective-permute-start(bf16[4,256,128]{2,1,0:T(8,128)(2,1)S(1)} %get-tuple-element.444), channel_id=1, source_target_pairs={{0,2},{1,3},{2,0},{3,1},{4,6},{5,7},{6,4},{7,5},{8,10},{9,11},{10,... | collective-permute-start | bytes 786440 | tf_op jit(solution)/shard_map/ppermute | solution.py:282
  533.7 35.2 %collective-permute-start.70 = (bf16[4,256,128]{2,1,0:T(8,128)(2,1)S(1)}, bf16[4,256,128]{2,1,0:T(8,128)(2,1)S(1)}, u32[]{:S(2)}, u32[]{:S(2)}) collective-permute-start(bf16[4,256,128]{2,1,0:T(8,128)(2,1)S(1)} %slice.900), channel_id=1, source_target_pairs={{0,1},{1,2},{2,3},{3,0},{4,5},{5,6},{6,7},{7,4},{8,9},{9,10},{10,1... | collective-permute-start | bytes 786440 | tf_op jit(solution)/shard_map/ppermute | solution.py:282
  (225 other events, 1982.7 us)
Sparse Core Ops, SparseCore 0:
  79.9 28.0 all-gather.4
  110.2 45.4 all-gather.6
  399.4 36.2 reduce-scatter.5
  443.8 28.0 reduce-scatter.3
  495.0 30.4 reduce-scatter.7

commit v3 on v2

--- a/solution.py
+++ b/solution.py
@@ -132,7 +132,7 @@
 
 def col(rows): return pl.BlockSpec((rows,128),lambda p,*_:(0,p))
 LSPEC=pl.BlockSpec((1,2,None),lambda p,*_:(p,0,0))
-def params(): return pltpu.CompilerParams(vmem_limit_bytes=40*1024*1024)
+def params(): return pltpu.CompilerParams(vmem_limit_bytes=48*1024*1024)
 def self_fwd(core,q,k,v):
     seq,cols=q.shape; pairs=cols//128
     return pl.pallas_call(lambda *r: self_fwd_kernel(*r,seq=seq),
@@ -178,13 +178,13 @@
         out_specs=[pl.BlockSpec(block,lambda i:(0,i,0,0))]*2,out_shape=[out,out],compiler_params=params(),
         cost_estimate=TINY,name="split_halves")(a,b)
 
-def place_pieces(groups,rows):
+def place_pieces(groups,chip,rows):
     first=groups[0][0]
     _,m,_,cols=first.shape
     width=sum(v.shape[0] for v in groups[0])*cols
     flat=[v for g in groups for v in g]
     shapes=[[v.shape[0] for v in g] for g in groups]
-    def body(*refs):
+    def body(chip_ref,*refs):
         ins,out=refs[:len(flat)],refs[len(flat)]
         at=0
         for p,s in enumerate(shapes):
@@ -195,11 +195,12 @@
                         out[:,:,z*cols:(z+1)*cols]=ins[at+i][j,:,0:rows,:]; z+=1
             pl.when(pl.program_id(0)==p)(fill)
             at+=len(s)
-    return pl.pallas_call(body,grid=(len(groups),),
-        in_specs=[pl.BlockSpec(v.shape,lambda p:(0,0,0,0),pipeline_mode=pl.Buffered(1)) for v in flat],
-        out_specs=pl.BlockSpec((m,rows,width),lambda p:(0,p,0)),
+    return pl.pallas_call(body,
+        grid_spec=pltpu.PrefetchScalarGridSpec(num_scalar_prefetch=1,grid=(len(groups),),
+            in_specs=[pl.BlockSpec(v.shape,lambda p,c:(0,0,0,0),pipeline_mode=pl.Buffered(1)) for v in flat],
+            out_specs=pl.BlockSpec((m,rows,width),lambda p,c:(0,p^c[0],0))),
         out_shape=jax.ShapeDtypeStruct((m,rows*len(groups),width),first.dtype),compiler_params=params(),
-        cost_estimate=TINY,name="place_pieces")(*flat)
+        cost_estimate=TINY,name="place_pieces")(chip,*flat)
 
 def hidden_up_kernel(h_ref, w_ref, e_ref, s_ref):
     w=w_ref[0]
@@ -247,6 +248,68 @@
         in_specs=[pl.BlockSpec((rows,parts*cols),lambda j:(half,0)),pl.BlockSpec((parts,blk,cols),lambda j:(0,j,0))],
         out_specs=pl.BlockSpec((rows,blk),lambda j:(0,j)),out_shape=jax.ShapeDtypeStruct((rows,depth),kind),compiler_params=params(),
         cost_estimate=TINY,name="hidden_down")(a,w)
+
+
+def place_hidden(groups,chip,rows):
+    first=groups[0][0]
+    cols=first.shape[3]
+    parts=sum(v.shape[0] for v in groups[0])
+    flat=[v for g in groups for v in g]
+    shapes=[[v.shape[0] for v in g] for g in groups]
+    def body(chip_ref,*refs):
+        ins,out=refs[:len(flat)],refs[len(flat)]
+        at=0
+        for p,s in enumerate(shapes):
+            def fill(at=at,s=s):
+                z=0
+                for i,k in enumerate(s):
+                    out[z:z+k]=ins[at+i][:,0]; z+=k
+            pl.when(pl.program_id(0)==p)(fill)
+            at+=len(s)
+    return pl.pallas_call(body,
+        grid_spec=pltpu.PrefetchScalarGridSpec(num_scalar_prefetch=1,grid=(len(groups),),
+            in_specs=[pl.BlockSpec(v.shape,lambda p,c:(0,0,0,0),pipeline_mode=pl.Buffered(1)) for v in flat],
+            out_specs=pl.BlockSpec((parts,rows,cols),lambda p,c:(0,p^c[0],0))),
+        out_shape=jax.ShapeDtypeStruct((parts,rows*len(groups),cols),first.dtype),compiler_params=params(),
+        cost_estimate=TINY,name="place_hidden")(chip,*flat)
+
+def piece_grads(chip,lefts,rights,chips):
+    tokens,depth=lefts[0].shape
+    rows=depth//chips; m=len(rights); cols=rights[0][2]
+    arrays=[]
+    for _,v,_,_ in rights:
+        if not any(v is w for w in arrays): arrays.append(v)
+    where=[next(i for i,w in enumerate(arrays) if w is v) for _,v,_,_ in rights]
+    nl,na=len(lefts),len(arrays)
+    def body(chip_ref,*refs):
+        ls,rs,outs=refs[:nl],refs[nl:nl+na],refs[nl+na:]
+        turned=[l[...].T for l in ls]
+        got=[]
+        for j,(left,_,_,at) in enumerate(rights):
+            r=rs[where[j]][:,at*cols:(at+1)*cols]
+            got.append(dot(turned[left],r,NN).astype(BF))
+        for p in range(chips):
+            def fill(p=p):
+                for j in range(m): outs[p][j]=got[j]
+            pl.when(pl.program_id(0)==p)(fill)
+    shape=jax.ShapeDtypeStruct((m,rows,cols),BF)
+    return pl.pallas_call(body,
+        grid_spec=pltpu.PrefetchScalarGridSpec(num_scalar_prefetch=1,grid=(chips,),
+            in_specs=[pl.BlockSpec((tokens,rows),lambda p,c:(0,p^c[0])) for _ in lefts]
+                +[pl.BlockSpec(v.shape,lambda p,c:(0,0),pipeline_mode=pl.Buffered(1)) for v in arrays],
+            out_specs=[pl.BlockSpec((m,rows,cols),lambda p,c:(0,0,0))]*chips),
+        out_shape=[shape]*chips,compiler_params=params(),cost_estimate=TINY,name="piece_grads")(chip,*lefts,*arrays)
+
+def token_grad(a,b,parts):
+    rows,depth=a.shape; cols=b.shape[1]//parts; blk=256
+    def body(a_ref,b_ref,g_ref):
+        turned=a_ref[...].T
+        for z in range(parts):
+            g_ref[z]=dot(turned,b_ref[:,z*cols:(z+1)*cols],NN).astype(BF)
+    return pl.pallas_call(body,grid=(depth//blk,),
+        in_specs=[pl.BlockSpec((rows,blk),lambda j:(0,j)),pl.BlockSpec(b.shape,lambda j:(0,0),pipeline_mode=pl.Buffered(1))],
+        out_specs=pl.BlockSpec((parts,blk,cols),lambda j:(0,j,0)),out_shape=jax.ShapeDtypeStruct((parts,depth,cols),BF),compiler_params=params(),
+        cost_estimate=TINY,name="token_grad")(a,b)
 
 
 from jax.sharding import PartitionSpec as P
@@ -341,10 +404,8 @@
     def swap_core(value):
         return swap_dp(value, size, 1)
 
-    def reorder(value):
-        return jnp.concatenate(
-            [lax.dynamic_slice_in_dim(value, (chip ^ p) * block, block, value.ndim - 1) for p in range(chips)], -1
-        )
+    chip_index = chip.astype(jnp.int32).reshape(1)
+    groups = [[d * lines + m for m in range(lines) for d in range(c, size, 2)] for c in range(2)]
 
     def own_half(stack):
         half = stack.shape[-1] // 2
@@ -357,20 +418,8 @@
 
     near = pairs[0] if pairs else []
 
-    def phase_low(low):
-        return {b: swap_dp(low, size, b) for b in near}
-
-    def phase_on(low, high, lows, highs):
-        found = {0: (low, high)}
-        for b in near:
-            found[b] = (lows[b], highs[b])
-        if len(near) == 2:
-            a, b = near
-            found[a ^ b] = (swap_dp(lows[b], size, a), swap_dp(highs[a], size, b))
-        for bit in bits[2:]:
-            for c in sorted(found):
-                found[c ^ bit] = tuple(swap_dp(v, size, bit) for v in found[c])
-        return found
+    def phase_first(line):
+        return {b: swap_dp(line, size, b) for b in near}
 
     def whole_on(line, wholes):
         found = {0: (line,)}
@@ -385,8 +434,34 @@
                 found[c ^ bit] = tuple(swap_dp(v, size, bit) for v in found[c])
         return found
 
+    def gather_column(own):
+        found = {0: own}
+        if len(near) == 2:
+            a, b = near
+            found[a], found[b] = swap_dp(own, size, a), swap_dp(own, size, b)
+            found[a ^ b] = jnp.concatenate([swap_dp(found[b][:part], size, a), swap_dp(found[a][part:], size, b)], 0)
+        else:
+            for a in near:
+                found[a] = swap_dp(own, size, a)
+        for bit in bits[2:]:
+            for c in sorted(found):
+                found[c ^ bit] = swap_dp(found[c], size, bit)
+        stacked = jnp.stack([found[2 * p] for p in range(chips)], 0)
+        return jnp.concatenate(
+            [lax.dynamic_index_in_dim(stacked, chip ^ p, 0, keepdims=False) for p in range(chips)], 0
+        )
+
+    def scatter_column(total):
+        found = {
+            2 * p: lax.dynamic_slice_in_dim(total, (chip ^ p) * 2 * part, 2 * part, axis=0)[None] for p in range(chips)
+        }
+        for bit in reversed(bits[2:]):
+            found = {c: found[c] + swap_dp(found[c ^ bit], size, bit) for c in found if not c & bit}
+        far = back_far(found, cut_columns)
+        return back_sum(back_total(found, far, cut_columns, glue_columns))
+
     def assemble(found):
-        return place_pieces([found[2 * p] for p in range(chips)], 2 * part)
+        return place_pieces([found[2 * p] for p in range(chips)], chip_index, 2 * part)
 
     def assemble_gains(found):
         per = norm_gains.shape[1]
@@ -396,68 +471,67 @@
             pieces = [v[z, 0, 2 * part :].reshape(-1)[:count] for v in found[2 * p] for z in range(v.shape[0])]
             rows.append(jnp.stack(pieces, 0).reshape(lines, 2, 2, 6, per).astype(F32))
         stacked = jnp.stack(rows, 0)
+        stacked = jnp.stack([lax.dynamic_index_in_dim(stacked, chip ^ p, 0, keepdims=False) for p in range(chips)], 0)
         stacked = jnp.stack(
             [lax.dynamic_index_in_dim(stacked, (z - mp) % lines, 1, keepdims=False) for z in range(lines)], 2
         )
         total = stacked[:, :, :, 0] + stacked[:, :, :, 1]
         return total.transpose(3, 0, 1, 2, 4).reshape(6, width)
 
-    def slices(grad):
-        half = grad.shape[-1] // 2
-        found = {}
-        for p in range(chips):
-            rows = lax.slice_in_dim(grad, p * 2 * part, (p + 1) * 2 * part, axis=1)
-            found[2 * p] = (rows[..., :half], rows[..., half:])
+    def pieces(lefts, rights):
+        if (2 * part) % 128 == 0:
+            found = piece_grads(chip_index, lefts, rights, chips)
+            found = {2 * p: found[p] for p in range(chips)}
+        else:
+            grad = jnp.stack([dot(lefts[i], v[:, at * n : (at + 1) * n], TN).astype(BF) for i, v, n, at in rights])
+            found = {
+                2 * p: lax.dynamic_slice_in_dim(grad, (chip ^ p) * 2 * part, 2 * part, axis=1) for p in range(chips)
+            }
         for bit in reversed(bits[2:]):
-            found = {
-                c: tuple(u + swap_dp(v, size, bit) for u, v in zip(found[c], found[c ^ bit])) for c in found if not c & bit
-            }
+            found = {c: found[c] + swap_dp(found[c ^ bit], size, bit) for c in found if not c & bit}
         return found
 
-    def back_far(found):
+    def back_far(found, cut):
         if len(near) < 2:
             return {}
         a, b = near
-        return {"low": swap_dp(found[a ^ b][0], size, a), "high": swap_dp(found[a ^ b][1], size, b)}
-
-    def back_plain(found):
+        low, high = cut(found[a ^ b])
+        return {"low": swap_dp(low, size, a), "high": swap_dp(high, size, b)}
+
+    def back_total(found, far, cut, glue):
+        total = found[0]
         if len(near) < 2:
-            return {}
+            return total + swap_dp(found[near[0]], size, near[0]) if near else total
         a, b = near
-        return {"low": swap_dp(found[a][0], size, a), "high": swap_dp(found[b][1], size, b)}
-
-    def back_summed(found, far):
-        if not near:
-            return {}
-        if len(near) < 2:
-            return {"low": swap_dp(found[near[0]][0], size, near[0]), "high": swap_dp(found[near[0]][1], size, near[0])}
-        a, b = near
-        return {
-            "low": swap_dp(found[b][0] + far["low"], size, b),
-            "high": swap_dp(found[a][1] + far["high"], size, a),
-        }
-
-    def back_total(found, plain, summed):
-        low, high = found[0]
-        for got in (plain, summed):
-            if got:
-                low, high = low + got["low"], high + got["high"]
+        low, high = cut(found[b])
+        to_b = glue(low + far["low"], high)
+        low, high = cut(found[a])
+        to_a = glue(low, high + far["high"])
+        return {"own": total, "a": swap_dp(to_a, size, a), "b": swap_dp(to_b, size, b)}
+
+    def back_sum(got):
+        return got["own"] + got["a"] + got["b"] if isinstance(got, dict) else got
+
+    def cut_columns(value):
+        half = value.shape[-1] // 2
+        return value[..., :half], value[..., half:]
+
+    def glue_columns(low, high):
         return jnp.concatenate([low, high], -1)
+
+    def cut_blocks(value):
+        half = value.shape[0] // 2
+        return value[:half], value[half:]
+
+    def glue_blocks(low, high):
+        return jnp.concatenate([low, high], 0)
 
     def lay(total):
         quarter = total.shape[-1] // lines
         return [total[..., z * quarter : (z + 1) * quarter] for z in range(lines)]
 
-    def lay_hidden(total):
-        group = 128 * lines
-        count = total.shape[-1] // group
-        return [
-            jnp.concatenate([total[..., j * group + z * 128 : j * group + (z + 1) * 128] for j in range(count)], -1)
-            for z in range(lines)
-        ]
-
-    def scatter_line(pieces):
-        return lax.psum_scatter(jnp.stack(pieces, 0), "mp", scatter_dimension=0, tiled=True)[0]
+    def scatter_line(laid):
+        return lax.psum_scatter(laid, "mp", scatter_dimension=0, tiled=True)[0]
 
     def scatter_shift(pieces):
         total = pieces[0].astype(F32)
@@ -483,10 +557,10 @@
         return lax.all_to_all(whole, "mp", 0, 0, tiled=True)
 
     def bring_last(whole):
-        return reorder(whole.reshape(lines * run, width))
+        return whole.reshape(lines * run, width)
 
     def give_line(value, rows):
-        return lax.all_to_all(reorder(value).reshape(lines, rows, width), "mp", 0, 0, tiled=True)
+        return lax.all_to_all(value.reshape(lines, rows, width), "mp", 0, 0, tiled=True)
 
     def give_core(whole):
         low, high = whole[:items], whole[items:]
@@ -523,13 +597,6 @@
     low = jnp.concatenate([input_weights[:3], output_weights[:1], input_weights[3:], output_weights[1:]], 0).astype(BF)
     own_inout = own_half(low)
     own_hidden = own_half(hidden_weights.astype(BF))
-    blocks = own_hidden.shape[-1] // 128
-
-    def in_blocks(shard):
-        return jnp.stack([shard[:, j * 128 : (j + 1) * 128] for j in range(blocks)], 0)
-
-    rest = jnp.concatenate([own_inout[4:], in_blocks(own_hidden[0]), in_blocks(own_hidden[1])], 0)
-
     gains_high = norm_gains.astype(BF)
     gains_low = (norm_gains - gains_high.astype(F32)).astype(BF)
     gains_own = jnp.stack([gains_high, gains_low], 0)
@@ -545,25 +612,27 @@
 
     moved = [own_self] + [shift(own_self, k) for k in range(1, lines)]
     image_core = bring_core(image_states)
-    mid = lines // 2
-    moved, image_core, rest = tie(moved, image_core, rest)
+    column_down = gather_column(own_hidden[1])
+    moved, image_core, own_cross, column_down = tie(moved, image_core, own_inout[4:], column_down)
     self_line = jnp.stack(moved, 0)
-    self_whole = phase_low(self_line)
+    self_whole = phase_first(self_line)
     image_line = bring_line(image_core)
-    self_whole, rest, image_line = tie(self_whole, rest, image_line)
-    line_cross = lax.all_gather(rest[:4], "mp", axis=0)
+    self_whole, own_cross, image_line = tie(self_whole, own_cross, image_line)
+    cross_line = lax.all_gather(own_cross, "mp", axis=0)
     found_self = whole_on(self_line, self_whole)
     image_all = both(bring_last(image_line))
-    line_cross, rest_hidden = tie(line_cross, rest[4:])
-    line_hidden = lax.all_gather(rest_hidden, "mp", axis=0)
+    cross_line, own_up = tie(cross_line, own_hidden[:1])
+    up_line = lax.all_gather(own_up, "mp", axis=0)
     cot_core = bring_core(cotangent)
-    line_hidden, cot_core = tie(line_hidden, cot_core)
+    up_line, column_down, cot_core = tie(up_line, column_down, cot_core)
+    weights_down = lax.all_gather(column_down, "mp", axis=0)
+    cot_line = bring_line(cot_core)
 
     which = mp % items
     mine = lax.dynamic_index_in_dim(text_states, which, 0, keepdims=False)
     mine_mask = lax.dynamic_index_in_dim(text_mask, which, 0, keepdims=False).astype(F32)
     here = (mp // items) == core
-    text = reorder(jnp.where(here, mine, swap_core(mine)))
+    text = jnp.where(here, mine, swap_core(mine))
     valid = jnp.where(here, mine_mask, swap_core(mine_mask))
     valid = jnp.broadcast_to(valid[:, None], (valid.shape[0], 128))
 
@@ -573,89 +642,79 @@
     found_self, image_all = tie(found_self, image_all)
     weights_self = assemble(found_self)
     gain_rows = assemble_gains(found_self)
-    cross_low, cross_high = line_cross[:mid], line_cross[mid:]
-    cross_lows = phase_low(cross_low)
     image_float = image_all.astype(F32)
     image_own = image_float[:half]
     unit, _ = norm_parts(image_float)
     h1 = (unit * gain_rows[0] + gain_rows[1]).astype(BF)
+    h1, cross_line = tie(h1, cross_line)
+    cross_whole = phase_first(cross_line)
     q1, k1, v1 = (dot(h1, weights_self[j], NN).astype(BF) for j in range(3))
-    q1, k1, v1, cross_lows = tie(q1, k1, v1, cross_lows)
-    cross_highs = phase_low(cross_high)
     o1, l1 = self_fwd(core_index, q1, k1, v1)
-    o1, cross_lows, cross_highs, line_hidden = tie(o1, cross_lows, cross_highs, line_hidden)
-    found_cross = phase_on(cross_low, cross_high, cross_lows, cross_highs)
-    up_low, up_high = line_hidden[:mid, :blocks], line_hidden[mid:, :blocks]
-    down_low, down_high = line_hidden[:mid, blocks:], line_hidden[mid:, blocks:]
-    up_lows = phase_low(up_low)
+    o1, cross_whole = tie(o1, cross_whole)
+    found_cross = whole_on(cross_line, cross_whole)
     r1 = image_own + joined(o1, weights_self[3], NT)
     unit, _ = norm_parts(r1)
     h2 = both((unit * gain_rows[2] + gain_rows[3]).astype(BF))
-    h2, found_cross, up_lows = tie(h2, found_cross, up_lows)
+    h2, found_cross, up_line = tie(h2, found_cross, up_line)
+    up_whole = phase_first(up_line)
     weights_cross = assemble(found_cross)
-    up_highs = phase_low(up_high)
     q2 = dot(h2, weights_cross[0], NN).astype(BF)
     k2, v2 = (dot(text, weights_cross[j], NN).astype(BF) for j in (1, 2))
     o2, l2 = cross_fwd(valid, q2, k2, v2)
-    o2, up_lows, up_highs = tie(o2, up_lows, up_highs)
-    found_up = phase_on(up_low, up_high, up_lows, up_highs)
-    down_lows = phase_low(down_low)
-    cot_line = bring_line(cot_core)
+    o2, up_whole = tie(o2, up_whole)
+    found_up = whole_on(up_line, up_whole)
     r2 = r1 + joined(o2, weights_cross[3], NT)
     unit, _ = norm_parts(r2)
     h3 = both((unit * gain_rows[4] + gain_rows[5]).astype(BF))
-    h3, found_up, down_lows = tie(h3, found_up, down_lows)
-    weights_up = assemble(found_up)
-    down_highs = phase_low(down_high)
+    h3, found_up = tie(h3, found_up)
+    weights_up = place_hidden([found_up[2 * p] for p in range(chips)], chip_index, 2 * part)
     e, slope = hidden_up(h3, weights_up)
-    e, down_lows, down_highs, cot_line = tie(e, down_lows, down_highs, cot_line)
-    found_down = phase_on(down_low, down_high, down_lows, down_highs)
+    e, slope, cot_line = tie(e, slope, cot_line)
     cot_own = bring_last(cot_line)
     cot = both(cot_own)
     cot_float = cot_own.astype(F32)
-    grad_down = dot(cot, e, TN).astype(BF)
-    e, slope, found_down, grad_down = tie(e, slope, found_down, grad_down)
-    weights_down = assemble(found_down)
+    grad_down = token_grad(cot, e, lines)
+    e, slope, weights_down, grad_down = tie(e, slope, weights_down, grad_down)
 
     def joined_hidden(value, weights):
         other = hidden_down(value, weights, 1, BF)
         return hidden_down(value, weights, 0, F32) + swap_core(other).astype(F32)
 
-    send_down = slices(grad_down[None])
-    far_down = back_far(send_down)
+    line_down = lax.psum_scatter(grad_down, "mp", scatter_dimension=0)
     du = hidden_slope(cot, weights_down, slope)
-    du, far_down = tie(du, far_down)
-    plain_down = back_plain(send_down)
-    grad_up = dot(h3, du, TN).astype(BF)
-    grad_up, far_down, plain_down = tie(grad_up, far_down, plain_down)
-    summed_down = back_summed(send_down, far_down)
-    send_up = slices(grad_up[None])
-    far_up = back_far(send_up)
+    send_up = pieces([h3], [(0, du, du.shape[1] // lines, z) for z in range(lines)])
+    far_up = back_far(send_up, cut_blocks)
     dh3 = joined_hidden(du, weights_up)
     back, gain_five, shift_six = norm_back(r2, dh3, gain_rows[4])
     dr2 = cot_float + back
     z2 = both(dr2.astype(BF))
-    z2, summed_down, far_up = tie(z2, summed_down, far_up)
-    plain_up = back_plain(send_up)
-    near_down = scatter_line(lay_hidden(back_total(send_down, plain_down, summed_down)))
+    z2, far_up = tie(z2, far_up)
+    total_up = back_total(send_up, far_up, cut_blocks, glue_blocks)
     layer_own = r2 + joined_hidden(e, weights_down)
     do2 = dot(z2, weights_cross[3], NN).astype(BF)
-    go1 = dot(z2, o2, TN).astype(BF)
     dq2, dk2, dv2 = cross_bwd(valid, q2, k2, v2, do2, l2)
-    dq2, dk2, dv2, plain_up, far_up, layer_own = tie(dq2, dk2, dv2, plain_up, far_up, layer_own)
+    dq2, dk2, dv2, layer_own, line_down = tie(dq2, dk2, dv2, layer_own, line_down)
+    near_down = scatter_column(line_down)
     layer_line = give_line(layer_own.astype(BF), run)
-    summed_up = back_summed(send_up, far_up)
     dh2 = joined(dq2, weights_cross[0], NT)
-    gi3 = dot(h2, dq2, TN).astype(BF)
+    send_cross = pieces([h2, z2], [(0, dq2, dq2.shape[1], 0), (1, o2, o2.shape[1], 0)])
     gi4 = dot(text, dk2, TN).astype(BF)
     gi5 = dot(text, dv2, TN).astype(BF)
+    send_text = {
+        2 * p: jnp.stack(
+            [lax.dynamic_slice_in_dim(v, (chip ^ p) * 2 * part, 2 * part, axis=0) for v in (gi4, gi5)]
+        )
+        for p in range(chips)
+    }
+    for bit in reversed(bits[2:]):
+        send_text = {c: send_text[c] + swap_dp(send_text[c ^ bit], size, bit) for c in send_text if not c & bit}
+    send_cross = {c: jnp.concatenate([send_cross[c], send_text[c]], 0) for c in send_cross}
     back, gain_three, shift_four = norm_back(r1, dh2, gain_rows[2])
     dr1 = dr2 + back
     z1 = both(dr1.astype(BF))
-    z1, summed_up, gi3, gi4, gi5, go1 = tie(z1, summed_up, gi3, gi4, gi5, go1)
-    send_cross = slices(jnp.stack([gi3, gi4, gi5, go1]))
-    far_cross = back_far(send_cross)
-    near_up = scatter_line(lay_hidden(back_total(send_up, plain_up, summed_up)))
+    z1, send_cross, total_up = tie(z1, send_cross, total_up)
+    near_up = scatter_line(back_sum(total_up))[None]
+    far_cross = back_far(send_cross, cut_columns)
     text_part = dot(dk2, weights_cross[1], NT) + dot(dv2, weights_cross[2], NT)
     share = text.shape[0] // (2 * lines)
     text_part = text_part.reshape(lines, 2, share, width)
@@ -664,21 +723,14 @@
     ).astype(F32)
     text_line = give_line(text_own.astype(BF).reshape(lines * share, width), share)
     do1 = dot(z1, weights_self[3], NN).astype(BF)
-    go0 = dot(z1, o1, TN).astype(BF)
-    do1, go0, far_cross, layer_line = tie(do1, go0, far_cross, layer_line)
-    plain_cross = back_plain(send_cross)
-    summed_cross = back_summed(send_cross, far_cross)
+    do1, far_cross = tie(do1, far_cross)
+    total_cross = back_total(send_cross, far_cross, cut_columns, glue_columns)
     dq1, dk1, dv1 = self_bwd(core_index, q1, k1, v1, do1, l1)
-    dq1, dk1, dv1, plain_cross, summed_cross, text_line = tie(dq1, dk1, dv1, plain_cross, summed_cross, text_line)
-    gi0, gi1, gi2 = (dot(h1, g, TN).astype(BF) for g in (dq1, dk1, dv1))
-    grad_self = jnp.stack([gi0, gi1, gi2, go0])
-    send_self = slices(grad_self)
-    far_self = back_far(send_self)
-    plain_self = back_plain(send_self)
-    send_self, dq1, dk1, dv1, plain_cross, summed_cross, near_up, near_down = tie(
-        send_self, dq1, dk1, dv1, plain_cross, summed_cross, near_up, near_down
-    )
-    near_cross = scatter_line(lay(back_total(send_cross, plain_cross, summed_cross)))
+    dq1, dk1, dv1, text_line, layer_line, near_down = tie(dq1, dk1, dv1, text_line, layer_line, near_down)
+    send_self = pieces([h1, z1], [(0, v, v.shape[1], 0) for v in (dq1, dk1, dv1)] + [(1, o1, o1.shape[1], 0)])
+    far_self = back_far(send_self, cut_columns)
+    send_self, dq1, dk1, dv1, total_cross = tie(send_self, dq1, dk1, dv1, total_cross)
+    near_cross = scatter_line(jnp.stack(lay(back_sum(total_cross)), 0))
 
     def three(at):
         return (
@@ -686,15 +738,15 @@
         )
 
     dh1 = three(slice(0, half)) + swap_core(three(slice(half, None)).astype(BF)).astype(F32)
-    dh1, far_self, plain_self = tie(dh1, far_self, plain_self)
-    summed_self = back_summed(send_self, far_self)
+    dh1, far_self = tie(dh1, far_self)
+    total_self = back_total(send_self, far_self, cut_columns, glue_columns)
     back, gain_one, shift_two = norm_back(image_own, dh1, gain_rows[0])
     image_own_grad = (dr1 + back).astype(BF)
-    gains_total = reorder(jnp.stack([gain_one, shift_two, gain_three, shift_four, gain_five, shift_six]))
+    gains_total = jnp.stack([gain_one, shift_two, gain_three, shift_four, gain_five, shift_six])
     image_line = give_line(image_own_grad, run)
-    summed_self, gains_total = tie(summed_self, gains_total)
+    total_self, gains_total = tie(total_self, gains_total)
     gains_total = sum_all(gains_total)
-    near_self = scatter_shift(lay(back_total(send_self, plain_self, summed_self)))
+    near_self = scatter_shift(lay(back_sum(total_self)))
     near_self, image_line, near_cross, near_up, near_down = tie(near_self, image_line, near_cross, near_up, near_down)
     shard_down = scatter_core(near_down)
     shard_up = scatter_core(near_up)
@@ -707,8 +759,8 @@
         gains_total, (dp * lines + mp) * norm_gains.shape[1], norm_gains.shape[1], 1
     )
 
-    input_shard = jnp.concatenate([shard_self[:3], shard_cross[:3]], 0)
-    output_shard = jnp.concatenate([shard_self[3:], shard_cross[3:]], 0)
+    input_shard = jnp.concatenate([shard_self[:3], shard_cross[:1], shard_cross[2:]], 0)
+    output_shard = jnp.concatenate([shard_self[3:], shard_cross[1:2]], 0)
     hidden_shard = jnp.concatenate([shard_up, shard_down], 0)
     square_total = jnp.sum(input_shard * input_shard) + jnp.sum(output_shard * output_shard)
     square_total = square_total + jnp.sum(hidden_shard * hidden_shard) + jnp.sum(gains_shard * gains_shard)

time: 618 us -> 584 us (0.945)
  Pallas kernels: 96.3 us -> 137 us
  matrix products: 71.7 us -> 43.1 us
  local copies, waits for them, and re-layouts: 49.8 us -> 30.4 us
  starting transfers between devices: 101 us -> 83.2 us
  other arithmetic: 95.6 us -> 89.4 us
    pallas_call x4 -> x7, Pallas kernels: 9.48 us -> 39.3 us  [the longest x3 21.1 us: piece_grads(): pl.pallas_call(body, grid_spec=pltpu.PrefetchScalarGridSpec(num_scalar_pr...]
    dot_general x32 -> x24, matrix products: 71.7 us -> 43.1 us  [dot(): return lax.dot_general(a, b, dims, preferred_element_type=F32)]
    all_to_all x2, waiting for transfers between devices: 0.01 us -> 19.4 us  [bring_line(): return lax.all_to_all(whole, 'mp', 0, 0, tiled=True)]
    ppermute x11, waiting for transfers between devices: 51.3 us -> 35.4 us  [move_mp(): return lax.ppermute(value, 'mp', pairs)]
    ppermute x80 -> x66, waiting for transfers between devices: 114 us -> 101 us  [swap_dp(): return lax.ppermute(value, 'dp', [(i, i ^ bit) for i in range(size)])]
    ppermute x80 -> x66, starting transfers between devices: 58.8 us -> 48.2 us  [swap_dp(): return lax.ppermute(value, 'dp', [(i, i ^ bit) for i in range(size)])]
    unnamed x319 -> x176, local copies, waits for them, and re-layouts: 25.2 us -> 15.9 us
    concatenate x6 -> x15, other arithmetic: 4.22 us -> 12.8 us  [the longest x6 5.72 us: glue_columns(): return jnp.concatenate([low, high], -1)]
  transfers between devices with their start and end apart: 101 -> 88, of which waited for: 33 -> 32; matrix products, arithmetic and copies ran while one was open for 27% -> 24% of each run, Pallas kernels for 15% -> 24%
where the time goes in v3:
time: 584 us; the launch traced here: 579 us
  waiting for transfers between devices  176 us (30%)
  Pallas kernels  137 us (23%)
  other arithmetic  89.4 us (15%)
  starting transfers between devices  83.2 us (14%)
  matrix products  43.1 us (7%)
  local copies, waits for them, and re-layouts  30.4 us (5%)
  between operations  19.5 us (3%)
    ppermute x66, waiting for transfers between devices, swap_dp(): return lax.ppermute(value, 'dp', [(i, i ^ bit) for i in range(size)])  101 us
    ppermute x66, starting transfers between devices, swap_dp(): return lax.ppermute(value, 'dp', [(i, i ^ bit) for i in range(size)])  48.2 us
    dot_general x24, matrix products, dot(): return lax.dot_general(a, b, dims, preferred_element_type=F32)  43.1 us
    ppermute x11, waiting for transfers between devices, move_mp(): return lax.ppermute(value, 'mp', pairs)  35.4 us
    pallas_call x4, Pallas kernels, hidden_down(): pl.pallas_call(hidden_down_kernel, grid=(depth // blk,), in_specs=[pl.Blo...  21.2 us
    pallas_call x3, Pallas kernels, piece_grads(): pl.pallas_call(body, grid_spec=pltpu.PrefetchScalarGridSpec(num_scalar_pr...  21.1 us
    all_to_all x2, waiting for transfers between devices, bring_line(): return lax.all_to_all(whole, 'mp', 0, 0, tiled=True)  19.4 us
    pallas_call x1, Pallas kernels, self_bwd(): pl.pallas_call(lambda *r: self_bwd_kernel(*r, seq=seq), grid_spec=pltpu.P...  17.9 us
  transfers between devices with their start and end apart: 88, of which 32 were waited for; matrix products, arithmetic and copies ran while one was open for 24% of the time, Pallas kernels for 24%

profile of v3, /device:TPU:0, one launch (start us, length us, event | category | flops | bytes accessed | tf_op | source)
XLA Modules:
  0.0 578.5 jit_solution(615437358387689266)
XLA Ops:
  33.5 13.4 %collective-permute-done.3 = bf16[4,264,128]{2,1,0:T(8,128)(2,1)S(1)} collective-permute-done((bf16[4,264,128]{2,1,0:T(8,128)(2,1)S(1)}, bf16[4,264,128]{2,1,0:T(8,128)(2,1)S(1)}, u32[]{:S(2)}, u32[]{:S(2)}) %collective-permute-start.3) | collective-permute-done | bytes 270368 | tf_op jit(solution)/shard_map/ppermute | solution.py:345
  46.9 4.3 all-to-all-start
  52.5 23.6 %collective-permute-done.11.b_ref.refs_1_ = bf16[4,4,264,128]{3,2,1,0:T(8,128)(2,1)S(1)} collective-permute-done((bf16[4,4,264,128]{3,2,1,0:T(8,128)(2,1)S(1)}, bf16[4,4,264,128]{3,2,1,0:T(8,128)(2,1)S(1)}, u32[]{:S(2)}, u32[]{:S(2)}) %collective-permute-start.11) | collective-permute-done | bytes 1081376 | tf_op jit(solution)/shard_map/ppermute | solution.py:341
  83.2 10.2 %collective-permute-done.13.refs_3_ = bf16[2,4,264,128]{3,2,1,0:T(8,128)(2,1)} collective-permute-done((bf16[2,4,264,128]{3,2,1,0:T(8,128)(2,1)}, bf16[2,4,264,128]{3,2,1,0:T(8,128)(2,1)}, u32[]{:S(2)}, u32[]{:S(2)}) %collective-permute-start.13) | collective-permute-done | bytes 540704 | tf_op jit(solution)/shard_map/ppermute | solution.py:341
  97.5 4.0 place_pieces.2
  116.8 16.7 %self_forward.1 = (bf16[1024,512]{1,0:T(8,128)(2,1)S(1)}, f32[4,2,1024]{2,1,0:T(2,128)S(1)}) custom-call(s32[1]{0:T(128)} %bitcast.r_0_, bf16[1024,512]{1,0:T(8,128)(2,1)S(1)} %convolution_convert_fusion.7.r_1_, bf16[1024,512]{1,0:T(8,128)(2,1)S(1)} %convolution_convert_fusion.6.r_2_, bf16[1024,512]{1,0:T(8,128)(2,1)S(1)} %convolution_convert_fusion.5.r_3_), custom_call_target="tpu_custom_call" | custom-call | flops 1 | bytes 1 | tf_op jit(solution)/shard_map/self_forward/pallas_call | solution.py:138
  154.2 11.8 %all-gather.9.cloned.1.call-done = bf16[4,256,512]{2,1,0:T(8,128)(2,1)} async-done(((bf16[1,256,512]{2,1,0:T(8,128)(2,1)}), bf16[4,256,512]{2,1,0:T(8,128)(2,1)}) %all-gather.9.cloned.1.call-update) | async-done | bytes 1048592 | tf_op jit(solution)/shard_map/all_gather | solution.py:625
  183.2 6.3 %cross_forward.1 = (bf16[1024,512]{1,0:T(8,128)(2,1)S(1)}, f32[4,2,1024]{2,1,0:T(2,128)S(1)}) custom-call(f32[128,128]{1,0:T(8,128)S(1)} %broadcast_in_dim.12.r_0_, bf16[1024,512]{1,0:T(8,128)(2,1)S(1)} %convolution_convert_fusion.4.r_1_, bf16[128,512]{1,0:T(8,128)(2,1)S(1)} %convolution_convert_fusion.12.r_2_, ...), custom_call_target="tpu_custom_call" | custom-call | flops 1 | bytes 1 | tf_op jit(solution)/shard_map/cross_forward/pallas_call | solution.py:154
  189.5 4.9 collective-permute-done.25.b_ref.refs_1_
  212.2 12.1 %collective-permute-done.29.refs_3_ = bf16[2,1,256,512]{3,2,1,0:T(8,128)(2,1)S(1)} collective-permute-done((bf16[2,1,256,512]{3,2,1,0:T(8,128)(2,1)S(1)}, bf16[2,1,256,512]{3,2,1,0:T(8,128)(2,1)S(1)}, u32[]{:S(2)}, u32[]{:S(2)}) %collective-permute-start.29) | collective-permute-done | bytes 524320 | tf_op jit(solution)/shard_map/ppermute | solution.py:341
  227.5 12.3 %hidden_up.1 = (bf16[1024,2048]{1,0:T(8,128)(2,1)}, bf16[1024,2048]{1,0:T(8,128)(2,1)}) custom-call(bf16[1024,1024]{1,0:T(8,128)(2,1)S(1)} %pad_maximum_fusion.2.h_ref.refs_0_, bf16[4,1024,512]{2,1,0:T(8,128)(2,1)} %place_hidden.1.w_ref), custom_call_target="tpu_custom_call" | custom-call | flops 1 | bytes 1 | tf_op jit(solution)/shard_map/hidden_up/pallas_call | solution.py:219
  239.8 19.0 %all-to-all-done.1 = bf16[4,128,1024]{2,1,0:T(8,128)(2,1)S(1)} async-done(((bf16[4,128,1024]{2,1,0:T(8,128)(2,1)}), bf16[4,128,1024]{2,1,0:T(8,128)(2,1)S(1)}, u32[]{:S(2)}, u32[]{:S(2)}) %all-to-all-start.1) | async-done | bytes 1048608 | tf_op jit(solution)/shard_map/all_to_all | solution.py:557
  262.9 8.6 %token_grad.1 = bf16[4,1024,512]{2,1,0:T(8,128)(2,1)} custom-call(bf16[1024,1024]{1,0:T(8,128)(2,1)S(1)} %pad_maximum_fusion.3.a_ref.g_ref, bf16[1024,2048]{1,0:T(8,128)(2,1)} %get-tuple-element.206.b_ref.a_ref), custom_call_target="tpu_custom_call" | custom-call | flops 1 | bytes 1 | tf_op jit(solution)/shard_map/token_grad/pallas_call | solution.py:309
  271.5 10.2 %hidden_slope.1.a_ref.refs_1_ = bf16[1024,2048]{1,0:T(8,128)(2,1)} custom-call(bf16[1024,1024]{1,0:T(8,128)(2,1)S(1)} %pad_maximum_fusion.3.a_ref.g_ref, bf16[4,1024,512]{2,1,0:T(8,128)(2,1)} %bitcast.276, bf16[1024,2048]{1,0:T(8,128)(2,1)} %get-tuple-element.199.s_ref), custom_call_target="tpu_custom_call" | custom-call | flops 1 | bytes 1 | tf_op jit(solution)/shard_map/hidden_slope/pallas_call | solution.py:233
  283.9 4.9 hidden_down.5
  290.7 5.7 hidden_down.4
  296.5 5.0 hidden_down.7
  309.6 8.0 %piece_grads.3 = (bf16[4,256,512]{2,1,0:T(8,128)(2,1)S(1)}, bf16[4,256,512]{2,1,0:T(8,128)(2,1)S(1)}, bf16[4,256,512]{2,1,0:T(8,128)(2,1)S(1)}, bf16[4,256,512]{2,1,0:T(8,128)(2,1)S(1)}) custom-call(s32[1]{0:T(128)} %bitcast.30.chip_ref, bf16[1024,1024]{1,0:T(8,128)(2,1)} %copy-done.2, bf16[1024,2048]{1,0:T(8,128)(2,1)} %hidden_slope.1.a_ref.refs_1_), custom_call_target="tpu_custom_call" | custom-call | flops 1 | bytes 1 | tf_op jit(solution)/shard_map/piece_grads/pallas_call | solution.py:296
  318.6 5.6 hidden_down.6
  328.3 10.1 %collective-permute-done.34 = bf16[2,256,512]{2,1,0:T(8,128)(2,1)S(1)} collective-permute-done((bf16[2,256,512]{2,1,0:T(8,128)(2,1)S(1)}, bf16[2,256,512]{2,1,0:T(8,128)(2,1)S(1)}, u32[]{:S(2)}, u32[]{:S(2)}) %collective-permute-start.34) | collective-permute-done | bytes 524320 | tf_op jit(solution)/shard_map/ppermute | solution.py:341
  345.8 9.5 %cross_backward.1 = (bf16[1024,512]{1,0:T(8,128)(2,1)S(1)}, bf16[128,512]{1,0:T(8,128)(2,1)S(1)}, bf16[128,512]{1,0:T(8,128)(2,1)S(1)}) custom-call(f32[128,128]{1,0:T(8,128)S(1)} %broadcast_in_dim.12.r_0_, bf16[1024,512]{1,0:T(8,128)(2,1)S(1)} %copy-done.13, bf16[128,512]{1,0:T(8,128)(2,1)S(1)} %convolution_convert_fusion.12.r_2_, ...), custom_call_target="tpu_custom_call" | custom-call | flops 1 | bytes 1 | tf_op jit(solution)/shard_map/cross_backward/pallas_call | solution.py:162
  355.4 5.1 piece_grads.4
  381.3 5.0 all-to-all-start.2
  389.8 5.7 collective-permute-done.41
  395.5 4.8 all-to-all-start.3
  411.1 17.9 %self_backward.1 = (bf16[1024,512]{1,0:T(8,128)(2,1)S(1)}, bf16[1024,512]{1,0:T(8,128)(2,1)S(1)}, bf16[1024,512]{1,0:T(8,128)(2,1)S(1)}) custom-call(s32[1]{0:T(128)} %bitcast.r_0_, bf16[1024,512]{1,0:T(8,128)(2,1)S(1)} %copy-done.9, bf16[1024,512]{1,0:T(8,128)(2,1)S(1)} %copy-done.7, bf16[1024,512]{1,0:T(8,128)(2,1)} %copy-done.5, ...), custom_call_target="tpu_custom_call" | custom-call | flops 1 | bytes 1 | tf_op jit(solution)/shard_map/self_backward/pallas_call | solution.py:146
  430.9 7.4 %all-to-all-done.3 = bf16[4,128,1024]{2,1,0:T(8,128)(2,1)} async-done(((bf16[4,128,1024]{2,1,0:T(8,128)(2,1)}), bf16[4,128,1024]{2,1,0:T(8,128)(2,1)}, u32[]{:S(2)}, u32[]{:S(2)}) %all-to-all-start.3) | async-done | bytes 1048608 | tf_op jit(solution)/shard_map/all_to_all | solution.py:563
  438.4 8.0 %piece_grads.5 = (bf16[4,256,512]{2,1,0:T(8,128)(2,1)S(1)}, bf16[4,256,512]{2,1,0:T(8,128)(2,1)S(1)}, bf16[4,256,512]{2,1,0:T(8,128)(2,1)S(1)}, bf16[4,256,512]{2,1,0:T(8,128)(2,1)S(1)}) custom-call(s32[1]{0:T(128)} %bitcast.30.chip_ref, bf16[1024,1024]{1,0:T(8,128)(2,1)} %add_convert_fusion.refs_0_, bf16[1024,1024]{1,0:T(8,128)(2,1)} %copy-done.50, ...), custom_call_target="tpu_custom_call" | custom-call | flops 1 | bytes 1 | tf_op jit(solution)/shard_map/piece_grads/pallas_call | solution.py:296
  474.3 3.9 all-to-all-start.4
  478.6 14.4 %collective-permute-done.55 = bf16[4,256,512]{2,1,0:T(8,128)(2,1)} collective-permute-done((bf16[4,256,512]{2,1,0:T(8,128)(2,1)}, bf16[4,256,512]{2,1,0:T(8,128)(2,1)}, u32[]{:S(2)}, u32[]{:S(2)}) %collective-permute-start.55) | collective-permute-done | bytes 1048608 | tf_op jit(solution)/shard_map/ppermute | solution.py:341
  509.2 15.6 %collective-permute-done.68 = f32[6,1024]{1,0:T(8,128)S(1)} collective-permute-done((f32[6,1024]{1,0:T(8,128)S(1)}, f32[6,1024]{1,0:T(8,128)S(1)}, u32[]{:S(2)}, u32[]{:S(2)}) %collective-permute-start.68) | collective-permute-done | bytes 24608 | tf_op jit(solution)/shard_map/ppermute | solution.py:345
  526.1 5.1 collective-permute-done.69
  (561 shorter events, 260.2 us)
Async XLA Ops:
  24.0 22.9 %collective-permute-start.3 = (bf16[4,264,128]{2,1,0:T(8,128)(2,1)S(1)}, bf16[4,264,128]{2,1,0:T(8,128)(2,1)S(1)}, u32[]{:S(2)}, u32[]{:S(2)}) collective-permute-start(bf16[4,264,128]{2,1,0:T(8,128)(2,1)S(1)} %fusion.24), channel_id=1, source_target_pairs={{0,2},{1,3},{2,0},{3,1},{4,6},{5,7},{6,4},{7,5},{8,10},{9,11},{10,... | collective-permute-start | bytes 811016 | tf_op jit(solution)/shard_map/ppermute | solution.py:345
  46.9 29.9 %all-to-all-start = ((bf16[4,128,1024]{2,1,0:T(8,128)(2,1)}), bf16[4,128,1024]{2,1,0:T(8,128)(2,1)}, u32[]{:S(2)}, u32[]{:S(2)}) async-start(bf16[4,128,1024]{2,1,0:T(8,128)(2,1)} %pad_maximum_fusion.7), calls=%async_computation | async-start | bytes 2097152 | tf_op jit(solution)/shard_map/all_to_all | solution.py:557
  51.2 57.1 %all-gather.7.cloned.1.call-start = ((), (), s32[]{:S(2)}) async-start(), calls=%async_computation.11 | async-start | bytes 1310720 | tf_op jit(solution)/shard_map/all_gather | solution.py:621
  51.4 24.7 %collective-permute-start.11 = (bf16[4,4,264,128]{3,2,1,0:T(8,128)(2,1)S(1)}, bf16[4,4,264,128]{3,2,1,0:T(8,128)(2,1)S(1)}, u32[]{:S(2)}, u32[]{:S(2)}) collective-permute-start(bf16[4,4,264,128]{3,2,1,0:T(8,128)(2,1)S(1)} %pad_maximum_fusion.6.refs_0_), channel_id=1, source_target_pairs={{0,8},{4,12},{8,0},{12,4},{16,24},{20,28},{24,16},{28,20},{1,9},{5... | collective-permute-start | bytes 3244040 | tf_op jit(solution)/shard_map/ppermute | solution.py:341
  52.0 24.3 %collective-permute-start.12 = (bf16[4,4,264,128]{3,2,1,0:T(8,128)(2,1)S(1)}, bf16[4,4,264,128]{3,2,1,0:T(8,128)(2,1)S(1)}, u32[]{:S(2)}, u32[]{:S(2)}) collective-permute-start(bf16[4,4,264,128]{3,2,1,0:T(8,128)(2,1)S(1)} %pad_maximum_fusion.6.refs_0_), channel_id=1, source_target_pairs={{0,16},{4,20},{8,24},{12,28},{16,0},{20,4},{24,8},{28,12},{1,17},{... | collective-permute-start | bytes 3244040 | tf_op jit(solution)/shard_map/ppermute | solution.py:341
  80.0 86.0 %all-gather.9.cloned.1.call-start = ((), (), s32[]{:S(2)}) async-start(), calls=%async_computation.12 | async-start | bytes 1310720 | tf_op jit(solution)/shard_map/all_gather | solution.py:625
  108.2 25.4 %collective-permute-start.16 = (bf16[4,4,256,128]{3,2,1,0:T(8,128)(2,1)}, bf16[4,4,256,128]{3,2,1,0:T(8,128)(2,1)S(1)}, u32[]{:S(2)}, u32[]{:S(2)}) collective-permute-start(bf16[4,4,256,128]{3,2,1,0:T(8,128)(2,1)} %bitcast.270), channel_id=1, source_target_pairs={{0,8},{4,12},{8,0},{12,4},{16,24},{20,28},{24,16},{28,20},{1,9},{5... | collective-permute-start | bytes 3145736 | tf_op jit(solution)/shard_map/ppermute | solution.py:341
  109.7 24.7 %collective-permute-start.17 = (bf16[4,4,256,128]{3,2,1,0:T(8,128)(2,1)}, bf16[4,4,256,128]{3,2,1,0:T(8,128)(2,1)S(1)}, u32[]{:S(2)}, u32[]{:S(2)}) collective-permute-start(bf16[4,4,256,128]{3,2,1,0:T(8,128)(2,1)} %bitcast.271), channel_id=1, source_target_pairs={{0,16},{4,20},{8,24},{12,28},{16,0},{20,4},{24,8},{28,12},{1,17},{... | collective-permute-start | bytes 3145736 | tf_op jit(solution)/shard_map/ppermute | solution.py:341
  138.9 132.6 %all-gather.11.cloned.1.call-start = ((), (), s32[]{:S(2)}) async-start(), calls=%async_computation.13 | async-start | bytes 5242880 | tf_op jit(solution)/shard_map/all_gather | solution.py:628
  147.8 24.7 %collective-permute-start.24 = (bf16[128,1024]{1,0:T(8,128)(2,1)S(1)}, bf16[128,1024]{1,0:T(8,128)(2,1)}, u32[]{:S(2)}, u32[]{:S(2)}) collective-permute-start(bf16[128,1024]{1,0:T(8,128)(2,1)S(1)} %dynamic-slice_bitcast_fusion.11), channel_id=1, source_target_pairs={{0,4},{4,0},{8,12},{12,8},{16,20},{20,16},{24,28},{28,24},{1,5},{5... | collective-permute-start | bytes 786440 | tf_op jit(solution)/shard_map/ppermute | solution.py:341
  169.6 24.8 %collective-permute-start.25 = (bf16[4,1,256,512]{3,2,1,0:T(8,128)(2,1)S(1)}, bf16[4,1,256,512]{3,2,1,0:T(8,128)(2,1)S(1)}, u32[]{:S(2)}, u32[]{:S(2)}) collective-permute-start(bf16[4,1,256,512]{3,2,1,0:T(8,128)(2,1)S(1)} %bitcast.273), channel_id=1, source_target_pairs={{0,8},{4,12},{8,0},{12,4},{16,24},{20,28},{24,16},{28,20},{1,9},{5... | collective-permute-start | bytes 3145736 | tf_op jit(solution)/shard_map/ppermute | solution.py:341
  171.1 24.5 %collective-permute-start.26 = (bf16[4,1,256,512]{3,2,1,0:T(8,128)(2,1)S(1)}, bf16[4,1,256,512]{3,2,1,0:T(8,128)(2,1)S(1)}, u32[]{:S(2)}, u32[]{:S(2)}) collective-permute-start(bf16[4,1,256,512]{3,2,1,0:T(8,128)(2,1)S(1)} %bitcast.274), channel_id=1, source_target_pairs={{0,16},{4,20},{8,24},{12,28},{16,0},{20,4},{24,8},{28,12},{1,17},{... | collective-permute-start | bytes 3145736 | tf_op jit(solution)/shard_map/ppermute | solution.py:341
  200.2 58.6 %all-to-all-start.1 = ((bf16[4,128,1024]{2,1,0:T(8,128)(2,1)}), bf16[4,128,1024]{2,1,0:T(8,128)(2,1)S(1)}, u32[]{:S(2)}, u32[]{:S(2)}) async-start(bf16[4,128,1024]{2,1,0:T(8,128)(2,1)} %pad_maximum_fusion.10), calls=%async_computation.1 | async-start | bytes 2097152 | tf_op jit(solution)/shard_map/all_to_all | solution.py:557
  203.8 151.6 %reduce-scatter.4.cloned.1.call-start = ((), (), s32[]{:S(2)}) async-start(), calls=%async_computation.8 | async-start | bytes 5242880 | tf_op jit(solution)/shard_map/reduce_scatter | solution.py:683
  301.5 25.0 %collective-permute-start.36 = (bf16[512,1024]{1,0:T(8,128)(2,1)S(1)}, bf16[512,1024]{1,0:T(8,128)(2,1)S(1)}, u32[]{:S(2)}, u32[]{:S(2)}) collective-permute-start(bf16[512,1024]{1,0:T(8,128)(2,1)S(1)} %hidden_down.7), channel_id=1, source_target_pairs={{0,4},{4,0},{8,12},{12,8},{16,20},{20,16},{24,28},{28,24},{1,5},{5... | collective-permute-start | bytes 3145736 | tf_op jit(solution)/shard_map/ppermute | solution.py:341
  340.8 35.9 %collective-permute-start.40 = (bf16[4,256,512]{2,1,0:T(8,128)(2,1)}, bf16[4,256,512]{2,1,0:T(8,128)(2,1)}, u32[]{:S(2)}, u32[]{:S(2)}) collective-permute-start(bf16[4,256,512]{2,1,0:T(8,128)(2,1)} %pad_maximum_fusion.16), channel_id=1, source_target_pairs={{0,16},{4,20},{8,24},{12,28},{16,0},{20,4},{24,8},{28,12},{1,17},{... | collective-permute-start | bytes 3145736 | tf_op jit(solution)/shard_map/ppermute | solution.py:341
  342.5 34.3 %collective-permute-start.39 = (bf16[4,256,512]{2,1,0:T(8,128)(2,1)}, bf16[4,256,512]{2,1,0:T(8,128)(2,1)}, u32[]{:S(2)}, u32[]{:S(2)}) collective-permute-start(bf16[4,256,512]{2,1,0:T(8,128)(2,1)} %pad_maximum_fusion.15), channel_id=1, source_target_pairs={{0,8},{4,12},{8,0},{12,4},{16,24},{20,28},{24,16},{28,20},{1,9},{5... | collective-permute-start | bytes 3145736 | tf_op jit(solution)/shard_map/ppermute | solution.py:341
  374.5 32.4 %collective-permute-start.45 = (bf16[1,256,512]{2,1,0:T(8,128)(2,1)}, bf16[1,256,512]{2,1,0:T(8,128)(2,1)}, u32[]{:S(2)}, u32[]{:S(2)}) collective-permute-start(bf16[1,256,512]{2,1,0:T(8,128)(2,1)} %pad_maximum_fusion.27), channel_id=1, source_target_pairs={{0,8},{4,12},{8,0},{12,4},{16,24},{20,28},{24,16},{28,20},{1,9},{5... | collective-permute-start | bytes 786440 | tf_op jit(solution)/shard_map/ppermute | solution.py:341
  376.0 30.9 %collective-permute-start.47 = (bf16[1,256,512]{2,1,0:T(8,128)(2,1)}, bf16[1,256,512]{2,1,0:T(8,128)(2,1)}, u32[]{:S(2)}, u32[]{:S(2)}) collective-permute-start(bf16[1,256,512]{2,1,0:T(8,128)(2,1)} %pad_maximum_fusion.28), channel_id=1, source_target_pairs={{0,16},{4,20},{8,24},{12,28},{16,0},{20,4},{24,8},{28,12},{1,17},{... | collective-permute-start | bytes 786440 | tf_op jit(solution)/shard_map/ppermute | solution.py:341
  395.5 42.9 %all-to-all-start.3 = ((bf16[4,128,1024]{2,1,0:T(8,128)(2,1)}), bf16[4,128,1024]{2,1,0:T(8,128)(2,1)}, u32[]{:S(2)}, u32[]{:S(2)}) async-start(bf16[4,128,1024]{2,1,0:T(8,128)(2,1)} %bitcast.285), calls=%async_computation.4 | async-start | bytes 2097152 | tf_op jit(solution)/shard_map/all_to_all | solution.py:563
  400.2 131.8 %reduce-scatter.8.cloned.1.call-start = ((), (), s32[]{:S(2)}) async-start(), calls=%async_computation.10 | async-start | bytes 1310720 | tf_op jit(solution)/shard_map/reduce_scatter | solution.py:534
  402.5 47.3 %collective-permute-start.50 = (bf16[4,256,512]{2,1,0:T(8,128)(2,1)}, bf16[4,256,512]{2,1,0:T(8,128)(2,1)}, u32[]{:S(2)}, u32[]{:S(2)}) collective-permute-start(bf16[4,256,512]{2,1,0:T(8,128)(2,1)} %pad_maximum_fusion.18), channel_id=1, source_target_pairs={{0,16},{4,20},{8,24},{12,28},{16,0},{20,4},{24,8},{28,12},{1,17},{... | collective-permute-start | bytes 3145736 | tf_op jit(solution)/shard_map/ppermute | solution.py:341
  405.2 44.6 %collective-permute-start.49 = (bf16[4,256,512]{2,1,0:T(8,128)(2,1)}, bf16[4,256,512]{2,1,0:T(8,128)(2,1)}, u32[]{:S(2)}, u32[]{:S(2)}) collective-permute-start(bf16[4,256,512]{2,1,0:T(8,128)(2,1)} %pad_maximum_fusion.17), channel_id=1, source_target_pairs={{0,8},{4,12},{8,0},{12,4},{16,24},{20,28},{24,16},{28,20},{1,9},{5... | collective-permute-start | bytes 3145736 | tf_op jit(solution)/shard_map/ppermute | solution.py:341
  411.1 121.0 %reduce-scatter.6.cloned.1.call-start = ((), (), s32[]{:S(2)}) async-start(), calls=%async_computation.9 | async-start | bytes 1310720 | tf_op jit(solution)/shard_map/reduce_scatter | solution.py:534
  466.8 26.2 %collective-permute-start.55 = (bf16[4,256,512]{2,1,0:T(8,128)(2,1)}, bf16[4,256,512]{2,1,0:T(8,128)(2,1)}, u32[]{:S(2)}, u32[]{:S(2)}) collective-permute-start(bf16[4,256,512]{2,1,0:T(8,128)(2,1)} %pad_maximum_fusion.20), channel_id=1, source_target_pairs={{0,16},{4,20},{8,24},{12,28},{16,0},{20,4},{24,8},{28,12},{1,17},{... | collective-permute-start | bytes 3145736 | tf_op jit(solution)/shard_map/ppermute | solution.py:341
  471.1 25.6 %collective-permute-start.54 = (bf16[4,256,512]{2,1,0:T(8,128)(2,1)}, bf16[4,256,512]{2,1,0:T(8,128)(2,1)}, u32[]{:S(2)}, u32[]{:S(2)}) collective-permute-start(bf16[4,256,512]{2,1,0:T(8,128)(2,1)} %pad_maximum_fusion.19), channel_id=1, source_target_pairs={{0,8},{4,12},{8,0},{12,4},{16,24},{20,28},{24,16},{28,20},{1,9},{5... | collective-permute-start | bytes 3145736 | tf_op jit(solution)/shard_map/ppermute | solution.py:341
  474.3 57.8 %all-to-all-start.4 = ((bf16[4,128,1024]{2,1,0:T(8,128)(2,1)}), bf16[4,128,1024]{2,1,0:T(8,128)(2,1)S(1)}, u32[]{:S(2)}, u32[]{:S(2)}) async-start(bf16[4,128,1024]{2,1,0:T(8,128)(2,1)} %bitcast.76), calls=%async_computation.5 | async-start | bytes 2097152 | tf_op jit(solution)/shard_map/all_to_all | solution.py:563
  478.2 29.5 %collective-permute-start.60 = (bf16[2,16,1024]{2,1,0:T(8,128)(2,1)S(1)}, bf16[2,16,1024]{2,1,0:T(8,128)(2,1)S(1)}, u32[]{:S(2)}, u32[]{:S(2)}) collective-permute-start(bf16[2,16,1024]{2,1,0:T(8,128)(2,1)S(1)} %broadcast_select_fusion.27), channel_id=1, source_target_pairs={{0,4},{4,0},{8,12},{12,8},{16,20},{20,16},{24,28},{28,24},{1,5},{5... | collective-permute-start | bytes 196616 | tf_op jit(solution)/shard_map/ppermute | solution.py:341
  498.7 46.5 %collective-permute-start.48 = (bf16[2,128,1024]{2,1,0:T(8,128)(2,1)}, bf16[2,128,1024]{2,1,0:T(8,128)(2,1)}, u32[]{:S(2)}, u32[]{:S(2)}) collective-permute-start(bf16[2,128,1024]{2,1,0:T(8,128)(2,1)} %broadcast_select_fusion.4), channel_id=1, source_target_pairs={{0,4},{4,0},{8,12},{12,8},{16,20},{20,16},{24,28},{28,24},{1,5},{5... | collective-permute-start | bytes 1572872 | tf_op jit(solution)/shard_map/ppermute | solution.py:341
  503.8 28.1 %collective-permute-start.56 = (bf16[4,256,128]{2,1,0:T(8,128)(2,1)S(1)}, bf16[4,256,128]{2,1,0:T(8,128)(2,1)S(1)}, u32[]{:S(2)}, u32[]{:S(2)}) collective-permute-start(bf16[4,256,128]{2,1,0:T(8,128)(2,1)S(1)} %get-tuple-element.322), channel_id=1, source_target_pairs={{0,1},{1,2},{2,3},{3,0},{4,5},{5,6},{6,7},{7,4},{8,9},{9,10},{10,1... | collective-permute-start | bytes 786440 | tf_op jit(solution)/shard_map/ppermute | solution.py:345
  503.9 28.0 %collective-permute-start.57 = (bf16[4,256,128]{2,1,0:T(8,128)(2,1)S(1)}, bf16[4,256,128]{2,1,0:T(8,128)(2,1)S(1)}, u32[]{:S(2)}, u32[]{:S(2)}) collective-permute-start(bf16[4,256,128]{2,1,0:T(8,128)(2,1)S(1)} %get-tuple-element.324), channel_id=1, source_target_pairs={{0,2},{1,3},{2,0},{3,1},{4,6},{5,7},{6,4},{7,5},{8,10},{9,11},{10,... | collective-permute-start | bytes 786440 | tf_op jit(solution)/shard_map/ppermute | solution.py:345
  507.1 24.8 %collective-permute-start.58 = (bf16[4,256,128]{2,1,0:T(8,128)(2,1)S(1)}, bf16[4,256,128]{2,1,0:T(8,128)(2,1)S(1)}, u32[]{:S(2)}, u32[]{:S(2)}) collective-permute-start(bf16[4,256,128]{2,1,0:T(8,128)(2,1)S(1)} %get-tuple-element.323), channel_id=1, source_target_pairs={{0,3},{1,0},{2,1},{3,2},{4,7},{5,4},{6,5},{7,6},{8,11},{9,8},{10,9... | collective-permute-start | bytes 786440 | tf_op jit(solution)/shard_map/ppermute | solution.py:345
  (144 other events, 915.2 us)
Sparse Core Ops, SparseCore 0:
  80.1 28.0 all-gather.6
  139.0 26.9 all-gather.8
  168.1 102.4 all-gather.10
  272.8 76.1 reduce-scatter.3
  411.2 31.3 reduce-scatter.7
  461.0 27.0 reduce-scatter.5

commit v4 on v3

--- a/solution.py
+++ b/solution.py
@@ -4,7 +4,7 @@
 from jax.experimental import pallas as pl
 from jax.experimental.pallas import tpu as pltpu
 BF=jnp.bfloat16; F32=jnp.float32
-HEAD_DIM=64; MASKED=-1e30; BQ=256
+HEAD_DIM=64; MASKED=-1e30; FORWARD_ROWS=512; BACKWARD_ROWS=256; CROSS_ROWS=1024
 NT=(((1,),(1,)),((),())); NN=(((1,),(0,)),((),())); TN=(((0,),(0,)),((),()))
 TINY=pl.CostEstimate(flops=1,bytes_accessed=1,transcendentals=0)
 def dot(a,b,dims): return lax.dot_general(a,b,dims,preferred_element_type=F32)
@@ -18,43 +18,44 @@
         at=pl.ds(place_of(b,core,half),128); to=slice(b*128,b*128+128)
         qs[to,:]=(q_ref[at,:].astype(F32)*0.125).astype(BF)
         ks[to,:]=k_ref[at,:]
-        vs[to,:]=v_ref[at,:]
+        vs[:,to]=v_ref[at,:].T
     low=lax.broadcasted_iota(jnp.int32,(1,128),1)<HEAD_DIM
-    for i in range(seq//BQ):
-        n=(i+1)*BQ
-        q=qs[i*BQ:n,:]
+    for i in range(seq//FORWARD_ROWS):
+        n=(i+1)*FORWARD_ROWS
+        q=qs[i*FORWARD_ROWS:n,:]
         outs=[]
         for h in range(2):
             keep=low if h==0 else ~low
             kh=jnp.where(keep,ks[0:n,:],jnp.zeros((),BF))
             s=dot(kh,q,NT)
-            tri=lax.broadcasted_iota(jnp.int32,(BQ,BQ),0)<=lax.broadcasted_iota(jnp.int32,(BQ,BQ),1)
-            diag=jnp.where(tri,s[n-BQ:,:],MASKED)
-            s=diag if n==BQ else jnp.concatenate([s[:n-BQ],diag],0)
+            tri=lax.broadcasted_iota(jnp.int32,(FORWARD_ROWS,FORWARD_ROWS),0)<=lax.broadcasted_iota(jnp.int32,(FORWARD_ROWS,FORWARD_ROWS),1)
+            diag=jnp.where(tri,s[n-FORWARD_ROWS:,:],MASKED)
+            s=diag if n==FORWARD_ROWS else jnp.concatenate([s[:n-FORWARD_ROWS],diag],0)
             m=jnp.max(s,axis=0,keepdims=True)
             e=jnp.exp(s-m)
             t=jnp.sum(e,axis=0,keepdims=True)
-            l_ref[0,h:h+1,i*BQ:n]=m+jnp.log(t)
-            vh=vs[0:n,h*64:h*64+64]
-            o=dot(vh,e.astype(BF),TN)
+            l_ref[0,h:h+1,i*FORWARD_ROWS:n]=m+jnp.log(t)
+            o=dot(vs[h*64:h*64+64,0:n],e.astype(BF),NN)
             outs.append(o*(1.0/t))
         o=jnp.concatenate(outs,0).T.astype(BF)
-        for j in range(BQ//128):
-            o_ref[pl.ds(place_of(i*(BQ//128)+j,core,half),128),:]=o[j*128:j*128+128]
-
-def self_bwd_kernel(core_ref, q_ref, k_ref, v_ref, g_ref, l_ref, dq_ref, dk_ref, dv_ref, qs, ks, vs, gs, dka, dva, *, seq):
+        for j in range(FORWARD_ROWS//128):
+            o_ref[pl.ds(place_of(i*(FORWARD_ROWS//128)+j,core,half),128),:]=o[j*128:j*128+128]
+
+def self_bwd_kernel(core_ref, q_ref, k_ref, v_ref, g_ref, l_ref, dq_ref, dk_ref, dv_ref, qs, ks, vs, gs, kt, dka, dva, *, seq):
     core=core_ref[0]; half=seq//2
     for b in range(seq//128):
         at=pl.ds(place_of(b,core,half),128); to=slice(b*128,b*128+128)
         qs[to,:]=(q_ref[at,:].astype(F32)*0.125).astype(BF)
-        ks[to,:]=k_ref[at,:]
+        k=k_ref[at,:]
+        ks[to,:]=k
+        kt[:,to]=k.T
         vs[to,:]=v_ref[at,:]
         gs[to,:]=g_ref[at,:]
     dka[...]=jnp.zeros_like(dka); dva[...]=jnp.zeros_like(dva)
     low=lax.broadcasted_iota(jnp.int32,(1,128),1)<HEAD_DIM
     zero=jnp.zeros((),BF)
-    for i in range(seq//BQ):
-        n=(i+1)*BQ; rows=slice(i*BQ,n)
+    for i in range(seq//BACKWARD_ROWS):
+        n=(i+1)*BACKWARD_ROWS; rows=slice(i*BACKWARD_ROWS,n)
         q=qs[rows,:]; g=gs[rows,:]
         ps=[]; dss=[]
         for h in range(2):
@@ -62,9 +63,9 @@
             kh=jnp.where(keep,ks[0:n,:],zero)
             vh=jnp.where(keep,vs[0:n,:],zero)
             s=dot(kh,q,NT)
-            tri=lax.broadcasted_iota(jnp.int32,(BQ,BQ),0)<=lax.broadcasted_iota(jnp.int32,(BQ,BQ),1)
-            diag=jnp.where(tri,s[n-BQ:,:],MASKED)
-            s=diag if n==BQ else jnp.concatenate([s[:n-BQ],diag],0)
+            tri=lax.broadcasted_iota(jnp.int32,(BACKWARD_ROWS,BACKWARD_ROWS),0)<=lax.broadcasted_iota(jnp.int32,(BACKWARD_ROWS,BACKWARD_ROWS),1)
+            diag=jnp.where(tri,s[n-BACKWARD_ROWS:,:],MASKED)
+            s=diag if n==BACKWARD_ROWS else jnp.concatenate([s[:n-BACKWARD_ROWS],diag],0)
             p=jnp.exp(s-l_ref[0,h:h+1,rows])
             dp=dot(vh,g,NT)
             delta=jnp.sum(p*dp,axis=0,keepdims=True)
@@ -74,11 +75,10 @@
         ga=jnp.concatenate([jnp.where(low,g,zero),jnp.where(low,zero,g)],0)
         dva[0:n,:]+=dot(jnp.concatenate(ps,1),ga,NN)
         dka[0:n,:]+=dot(jnp.concatenate(dss,1),qa,NN)
-        k=ks[0:n,:]
-        dqt=jnp.concatenate([dot(ks[0:n,0:64],dss[0],TN),dot(ks[0:n,64:128],dss[1],TN)],0)
+        dqt=jnp.concatenate([dot(kt[0:64,0:n],dss[0],NN),dot(kt[64:128,0:n],dss[1],NN)],0)
         dq=(dqt.T*0.125).astype(BF)
-        for j in range(BQ//128):
-            dq_ref[pl.ds(place_of(i*(BQ//128)+j,core,half),128),:]=dq[j*128:j*128+128]
+        for j in range(BACKWARD_ROWS//128):
+            dq_ref[pl.ds(place_of(i*(BACKWARD_ROWS//128)+j,core,half),128),:]=dq[j*128:j*128+128]
     for b in range(seq//128):
         at=pl.ds(place_of(b,core,half),128)
         dk_ref[at,:]=dka[b*128:b*128+128,:].astype(BF)
@@ -88,9 +88,9 @@
     low=lax.broadcasted_iota(jnp.int32,(1,128),1)<HEAD_DIM
     zero=jnp.zeros((),BF)
     valid=mask_ref[:,0:1]>0
-    k=k_ref[...]; v=v_ref[...]
-    for i in range(seq//BQ):
-        rows=slice(i*BQ,(i+1)*BQ)
+    k=k_ref[...]; vt=v_ref[...].T
+    for i in range(seq//CROSS_ROWS):
+        rows=slice(i*CROSS_ROWS,(i+1)*CROSS_ROWS)
         q=(q_ref[rows,:].astype(F32)*0.125).astype(BF)
         outs=[]
         for h in range(2):
@@ -100,17 +100,17 @@
             e=jnp.exp(s-m)
             t=jnp.sum(e,axis=0,keepdims=True)
             l_ref[0,h:h+1,rows]=m+jnp.log(t)
-            outs.append(dot(v[:,h*64:h*64+64],e.astype(BF),TN)*(1.0/t))
+            outs.append(dot(vt[h*64:h*64+64,:],e.astype(BF),NN)*(1.0/t))
         o_ref[rows,:]=jnp.concatenate(outs,0).T.astype(BF)
 
 def cross_bwd_kernel(mask_ref, q_ref, k_ref, v_ref, g_ref, l_ref, dq_ref, dk_ref, dv_ref, *, seq):
     low=lax.broadcasted_iota(jnp.int32,(1,128),1)<HEAD_DIM
     zero=jnp.zeros((),BF)
     valid=mask_ref[:,0:1]>0
-    k=k_ref[...]; v=v_ref[...]
+    k=k_ref[...]; v=v_ref[...]; kt=k.T
     dk=jnp.zeros(k.shape,F32); dv=jnp.zeros(k.shape,F32)
-    for i in range(seq//BQ):
-        rows=slice(i*BQ,(i+1)*BQ)
+    for i in range(seq//CROSS_ROWS):
+        rows=slice(i*CROSS_ROWS,(i+1)*CROSS_ROWS)
         q=(q_ref[rows,:].astype(F32)*0.125).astype(BF); g=g_ref[rows,:]
         ps=[]; dss=[]; dqs=[]
         for h in range(2):
@@ -122,7 +122,7 @@
             delta=jnp.sum(p*dp,axis=0,keepdims=True)
             ds=(p*(dp-delta)).astype(BF)
             ps.append(p.astype(BF)); dss.append(ds)
-            dqs.append(dot(k[:,h*64:h*64+64],ds,TN))
+            dqs.append(dot(kt[h*64:h*64+64,:],ds,NN))
         qa=jnp.concatenate([jnp.where(low,q,zero),jnp.where(low,zero,q)],0)
         ga=jnp.concatenate([jnp.where(low,g,zero),jnp.where(low,zero,g)],0)
         dv=dv+dot(jnp.concatenate(ps,1),ga,NN)
@@ -132,12 +132,12 @@
 
 def col(rows): return pl.BlockSpec((rows,128),lambda p,*_:(0,p))
 LSPEC=pl.BlockSpec((1,2,None),lambda p,*_:(p,0,0))
-def params(): return pltpu.CompilerParams(vmem_limit_bytes=48*1024*1024)
+def params(mib=32): return pltpu.CompilerParams(vmem_limit_bytes=mib*1024*1024)
 def self_fwd(core,q,k,v):
     seq,cols=q.shape; pairs=cols//128
     return pl.pallas_call(lambda *r: self_fwd_kernel(*r,seq=seq),
         grid_spec=pltpu.PrefetchScalarGridSpec(num_scalar_prefetch=1,grid=(pairs,),in_specs=[col(seq)]*3,
-            out_specs=[col(seq),pl.BlockSpec((1,2,seq),lambda p,*_:(p,0,0))],scratch_shapes=[pltpu.VMEM((seq,128),BF)]*3),
+            out_specs=[col(seq),pl.BlockSpec((1,2,seq),lambda p,*_:(p,0,0))],scratch_shapes=[pltpu.VMEM((seq,128),BF)]*2+[pltpu.VMEM((128,seq),BF)]),
         out_shape=[jax.ShapeDtypeStruct((seq,cols),BF),jax.ShapeDtypeStruct((pairs,2,seq),F32)],
         compiler_params=params(),
         cost_estimate=TINY,name="self_forward")(core,q,k,v)
@@ -145,7 +145,7 @@
     seq,cols=q.shape; pairs=cols//128
     return pl.pallas_call(lambda *r: self_bwd_kernel(*r,seq=seq),
         grid_spec=pltpu.PrefetchScalarGridSpec(num_scalar_prefetch=1,grid=(pairs,),in_specs=[col(seq)]*4+[pl.BlockSpec((1,2,seq),lambda p,*_:(p,0,0))],
-            out_specs=[col(seq)]*3,scratch_shapes=[pltpu.VMEM((seq,128),BF)]*4+[pltpu.VMEM((seq,128),F32)]*2),
+            out_specs=[col(seq)]*3,scratch_shapes=[pltpu.VMEM((seq,128),BF)]*4+[pltpu.VMEM((128,seq),BF)]+[pltpu.VMEM((seq,128),F32)]*2),
         out_shape=[jax.ShapeDtypeStruct((seq,cols),BF)]*3,
         compiler_params=params(),
         cost_estimate=TINY,name="self_backward")(core,q,k,v,g,l)
@@ -577,20 +577,15 @@
         other = dot(left[half:], right, dims).astype(BF)
         return dot(left[:half], right, dims) + swap_core(other).astype(F32)
 
-    def sum_all(value):
-        bit = 1
-        while bit < size:
-            value = value + swap_dp(value, size, bit)
-            bit *= 2
-        value = value + move_mp(value, PAIR)
-        return value + move_mp(value, ACROSS)
-
-    def sum_fast(value):
+    def sum_chips(value):
         value = value + swap_core(value)
         for i in range(0, len(bits), 2):
             pair = bits[i : i + 2]
             others = pair + [sum(pair)] if len(pair) == 2 else pair
             value = value + sum(swap_dp(value, size, b) for b in others)
+        return value
+
+    def sum_line(value):
         shifts = [[(i, (i + k) % lines) for i in range(lines)] for k in range(1, lines)]
         return value + sum(move_mp(value, pairs) for pairs in shifts)
 
@@ -617,16 +612,13 @@
     self_line = jnp.stack(moved, 0)
     self_whole = phase_first(self_line)
     image_line = bring_line(image_core)
-    self_whole, own_cross, image_line = tie(self_whole, own_cross, image_line)
     cross_line = lax.all_gather(own_cross, "mp", axis=0)
     found_self = whole_on(self_line, self_whole)
+    found_self, image_line, cross_line = tie(found_self, image_line, cross_line)
     image_all = both(bring_last(image_line))
     cross_line, own_up = tie(cross_line, own_hidden[:1])
     up_line = lax.all_gather(own_up, "mp", axis=0)
     cot_core = bring_core(cotangent)
-    up_line, column_down, cot_core = tie(up_line, column_down, cot_core)
-    weights_down = lax.all_gather(column_down, "mp", axis=0)
-    cot_line = bring_line(cot_core)
 
     which = mp % items
     mine = lax.dynamic_index_in_dim(text_states, which, 0, keepdims=False)
@@ -639,29 +631,29 @@
     core_index = core.astype(jnp.int32).reshape(1)
 
     half = image_all.shape[0] // 2
-    found_self, image_all = tie(found_self, image_all)
     weights_self = assemble(found_self)
     gain_rows = assemble_gains(found_self)
     image_float = image_all.astype(F32)
     image_own = image_float[:half]
     unit, _ = norm_parts(image_float)
     h1 = (unit * gain_rows[0] + gain_rows[1]).astype(BF)
-    h1, cross_line = tie(h1, cross_line)
     cross_whole = phase_first(cross_line)
     q1, k1, v1 = (dot(h1, weights_self[j], NN).astype(BF) for j in range(3))
     o1, l1 = self_fwd(core_index, q1, k1, v1)
-    o1, cross_whole = tie(o1, cross_whole)
+    o1, cross_whole, up_line, column_down, cot_core = tie(o1, cross_whole, up_line, column_down, cot_core)
+    cot_line = bring_line(cot_core)
+    weights_down = lax.all_gather(column_down, "mp", axis=0)
     found_cross = whole_on(cross_line, cross_whole)
     r1 = image_own + joined(o1, weights_self[3], NT)
     unit, _ = norm_parts(r1)
     h2 = both((unit * gain_rows[2] + gain_rows[3]).astype(BF))
-    h2, found_cross, up_line = tie(h2, found_cross, up_line)
+    h2, found_cross = tie(h2, found_cross)
     up_whole = phase_first(up_line)
     weights_cross = assemble(found_cross)
     q2 = dot(h2, weights_cross[0], NN).astype(BF)
     k2, v2 = (dot(text, weights_cross[j], NN).astype(BF) for j in (1, 2))
     o2, l2 = cross_fwd(valid, q2, k2, v2)
-    o2, up_whole = tie(o2, up_whole)
+    o2, up_whole, cot_line = tie(o2, up_whole, cot_line)
     found_up = whole_on(up_line, up_whole)
     r2 = r1 + joined(o2, weights_cross[3], NT)
     unit, _ = norm_parts(r2)
@@ -726,7 +718,7 @@
     do1, far_cross = tie(do1, far_cross)
     total_cross = back_total(send_cross, far_cross, cut_columns, glue_columns)
     dq1, dk1, dv1 = self_bwd(core_index, q1, k1, v1, do1, l1)
-    dq1, dk1, dv1, text_line, layer_line, near_down = tie(dq1, dk1, dv1, text_line, layer_line, near_down)
+    dq1, dk1, dv1, near_down = tie(dq1, dk1, dv1, near_down)
     send_self = pieces([h1, z1], [(0, v, v.shape[1], 0) for v in (dq1, dk1, dv1)] + [(1, o1, o1.shape[1], 0)])
     far_self = back_far(send_self, cut_columns)
     send_self, dq1, dk1, dv1, total_cross = tie(send_self, dq1, dk1, dv1, total_cross)
@@ -743,9 +735,11 @@
     back, gain_one, shift_two = norm_back(image_own, dh1, gain_rows[0])
     image_own_grad = (dr1 + back).astype(BF)
     gains_total = jnp.stack([gain_one, shift_two, gain_three, shift_four, gain_five, shift_six])
+    gains_total = sum_line(gains_total)
+    gains_total, image_own_grad = tie(gains_total, image_own_grad)
     image_line = give_line(image_own_grad, run)
     total_self, gains_total = tie(total_self, gains_total)
-    gains_total = sum_all(gains_total)
+    gains_total = sum_chips(gains_total)
     near_self = scatter_shift(lay(back_sum(total_self)))
     near_self, image_line, near_cross, near_up, near_down = tie(near_self, image_line, near_cross, near_up, near_down)
     shard_down = scatter_core(near_down)
@@ -764,7 +758,7 @@
     hidden_shard = jnp.concatenate([shard_up, shard_down], 0)
     square_total = jnp.sum(input_shard * input_shard) + jnp.sum(output_shard * output_shard)
     square_total = square_total + jnp.sum(hidden_shard * hidden_shard) + jnp.sum(gains_shard * gains_shard)
-    global_norm = jnp.sqrt(sum_fast(jnp.full((8, 128), square_total)))[0, 0]
+    global_norm = jnp.sqrt(sum_line(sum_chips(jnp.full((8, 128), square_total))))[0, 0]
     factor = jnp.minimum(1.0, CLIP_LIMIT / (global_norm + 1e-06))
     input_updated, input_moment, input_square = adam_update(
         input_weights, input_shard, input_momentum, input_variance, factor, LEARN_RATE, WEIGHT_DECAY

time: 584 us -> 552 us (0.945)
  Pallas kernels: 137 us -> 105 us
  waiting for transfers between devices: 176 us -> 147 us
  local copies, waits for them, and re-layouts: 30.4 us -> 48 us
  starting transfers between devices: 83.2 us -> 98 us
    unnamed x176 -> x208, local copies, waits for them, and re-layouts: 15.9 us -> 33.7 us
    ppermute x11 -> x12, starting transfers between devices: 12.9 us -> 23.5 us  [move_mp(): return lax.ppermute(value, 'mp', pairs)]
    all_gather x1, waiting for transfers between devices: 11.8 us -> 3.36 us  [per_device(): up_line = lax.all_gather(own_up, 'mp', axis=0)]
    all_to_all x3, waiting for transfers between devices: 7.43 us -> 0.01 us  [give_line(): lax.all_to_all(value.reshape(lines, rows, width), 'mp', 0, 0, tiled=True)]
    ppermute x11 -> x12, waiting for transfers between devices: 35.4 us -> 29 us  [move_mp(): return lax.ppermute(value, 'mp', pairs)]
    pallas_call x4, Pallas kernels: 21.2 us -> 14.9 us  [hidden_down(): pl.pallas_call(hidden_down_kernel, grid=(depth // blk,), in_specs=[pl.Blo...]
    ppermute x66 -> x67, waiting for transfers between devices: 101 us -> 95.8 us  [swap_dp(): return lax.ppermute(value, 'dp', [(i, i ^ bit) for i in range(size)])]
    ppermute x66 -> x67, starting transfers between devices: 48.2 us -> 49 us  [swap_dp(): return lax.ppermute(value, 'dp', [(i, i ^ bit) for i in range(size)])]
  transfers between devices with their start and end apart: 88 -> 90, of which waited for: 32 -> 32; matrix products, arithmetic and copies ran while one was open for 24% -> 24% of each run, Pallas kernels for 24% -> 19%
where the time goes in v4:
time: 552 us; the launch traced here: 547 us
  waiting for transfers between devices  147 us (27%)
  Pallas kernels  105 us (19%)
  starting transfers between devices  98 us (18%)
  other arithmetic  90.9 us (16%)
  local copies, waits for them, and re-layouts  48 us (9%)
  matrix products  38 us (7%)
  between operations  19.7 us (4%)
    ppermute x67, waiting for transfers between devices, swap_dp(): return lax.ppermute(value, 'dp', [(i, i ^ bit) for i in range(size)])  95.8 us
    ppermute x67, starting transfers between devices, swap_dp(): return lax.ppermute(value, 'dp', [(i, i ^ bit) for i in range(size)])  49 us
    dot_general x24, matrix products, dot(): return lax.dot_general(a, b, dims, preferred_element_type=F32)  38 us
    unnamed x208, local copies, waits for them, and re-layouts  33.7 us
    ppermute x12, waiting for transfers between devices, move_mp(): return lax.ppermute(value, 'mp', pairs)  29 us
    ppermute x12, starting transfers between devices, move_mp(): return lax.ppermute(value, 'mp', pairs)  23.5 us
    pallas_call x1, Pallas kernels, self_bwd(): pl.pallas_call(lambda *r: self_bwd_kernel(*r, seq=seq), grid_spec=pltpu.P...  17.2 us
    all_to_all x3, starting transfers between devices, give_line(): lax.all_to_all(value.reshape(lines, rows, width), 'mp', 0, 0, tiled=True)  16.6 us
  transfers between devices with their start and end apart: 90, of which 32 were waited for; matrix products, arithmetic and copies ran while one was open for 24% of the time, Pallas kernels for 19%

profile of v4, /device:TPU:0, one launch (start us, length us, event | category | flops | bytes accessed | tf_op | source)
XLA Modules:
  0.0 546.6 jit_solution(5441385754741626578)
XLA Ops:
  20.3 3.7 collective-permute-start.3
  33.5 13.4 %collective-permute-done.4 = bf16[4,264,128]{2,1,0:T(8,128)(2,1)S(1)} collective-permute-done((bf16[4,264,128]{2,1,0:T(8,128)(2,1)S(1)}, bf16[4,264,128]{2,1,0:T(8,128)(2,1)S(1)}, u32[]{:S(2)}, u32[]{:S(2)}) %collective-permute-start.4) | collective-permute-done | bytes 270368 | tf_op jit(solution)/shard_map/ppermute | solution.py:345
  48.1 4.2 all-to-all-start
  55.4 16.3 %collective-permute-done.12.b_ref.refs_1_ = bf16[4,4,264,128]{3,2,1,0:T(8,128)(2,1)S(1)} collective-permute-done((bf16[4,4,264,128]{3,2,1,0:T(8,128)(2,1)S(1)}, bf16[4,4,264,128]{3,2,1,0:T(8,128)(2,1)S(1)}, u32[]{:S(2)}, u32[]{:S(2)}) %collective-permute-start.12) | collective-permute-done | bytes 1081376 | tf_op jit(solution)/shard_map/ppermute | solution.py:341
  78.1 13.9 %all-to-all-done = bf16[4,128,1024]{2,1,0:T(8,128)(2,1)} async-done(((bf16[4,128,1024]{2,1,0:T(8,128)(2,1)}), bf16[4,128,1024]{2,1,0:T(8,128)(2,1)}, u32[]{:S(2)}, u32[]{:S(2)}) %all-to-all-start) | async-done | bytes 1048608 | tf_op jit(solution)/shard_map/all_to_all | solution.py:557
  117.1 11.4 %self_forward.1 = (bf16[1024,512]{1,0:T(8,128)(2,1)S(1)}, f32[4,2,1024]{2,1,0:T(2,128)S(1)}) custom-call(s32[1]{0:T(128)} %bitcast.23.r_0_, bf16[1024,512]{1,0:T(8,128)(2,1)S(1)} %convolution_convert_fusion.7.r_1_, bf16[1024,512]{1,0:T(8,128)(2,1)S(1)} %convolution_convert_fusion.6.r_2_, bf16[1024,512]{1,0:T(8,128)(2,1)S(1)} %convolution_convert_fusion.5.r_3_), custom_call_target="tpu_custom_call" | custom-call | flops 1 | bytes 1 | tf_op jit(solution)/shard_map/self_forward/pallas_call | solution.py:138
  143.0 4.2 all-to-all-start.1
  157.0 9.1 %collective-permute-done.22.refs_3_ = bf16[2,4,256,128]{3,2,1,0:T(8,128)(2,1)} collective-permute-done((bf16[2,4,256,128]{3,2,1,0:T(8,128)(2,1)}, bf16[2,4,256,128]{3,2,1,0:T(8,128)(2,1)}, u32[]{:S(2)}, u32[]{:S(2)}) %collective-permute-start.22) | collective-permute-done | bytes 524320 | tf_op jit(solution)/shard_map/ppermute | solution.py:341
  172.7 4.1 cross_forward.1
  177.7 10.1 %collective-permute-done.25.b_ref.refs_1_ = bf16[4,1,256,512]{3,2,1,0:T(8,128)(2,1)S(1)} collective-permute-done((bf16[4,1,256,512]{3,2,1,0:T(8,128)(2,1)}, bf16[4,1,256,512]{3,2,1,0:T(8,128)(2,1)S(1)}, u32[]{:S(2)}, u32[]{:S(2)}) %collective-permute-start.25) | collective-permute-done | bytes 1048608 | tf_op jit(solution)/shard_map/ppermute | solution.py:341
  204.4 11.0 %collective-permute-done.29.refs_3_ = bf16[2,1,256,512]{3,2,1,0:T(8,128)(2,1)S(1)} collective-permute-done((bf16[2,1,256,512]{3,2,1,0:T(8,128)(2,1)S(1)}, bf16[2,1,256,512]{3,2,1,0:T(8,128)(2,1)S(1)}, u32[]{:S(2)}, u32[]{:S(2)}) %collective-permute-start.29) | collective-permute-done | bytes 524320 | tf_op jit(solution)/shard_map/ppermute | solution.py:341
  218.5 10.7 %hidden_up.1 = (bf16[1024,2048]{1,0:T(8,128)(2,1)S(1)}, bf16[1024,2048]{1,0:T(8,128)(2,1)S(1)}) custom-call(bf16[1024,1024]{1,0:T(8,128)(2,1)S(1)} %pad_maximum_fusion.2.h_ref.refs_0_, bf16[4,1024,512]{2,1,0:T(8,128)(2,1)S(1)} %place_hidden.1.w_ref), custom_call_target="tpu_custom_call" | custom-call | flops 1 | bytes 1 | tf_op jit(solution)/shard_map/hidden_up/pallas_call | solution.py:219
  235.7 5.7 %token_grad.1 = bf16[4,1024,512]{2,1,0:T(8,128)(2,1)S(1)} custom-call(bf16[1024,1024]{1,0:T(8,128)(2,1)S(1)} %pad_maximum_fusion.3.a_ref.g_ref, bf16[1024,2048]{1,0:T(8,128)(2,1)S(1)} %get-tuple-element.196.b_ref.a_ref), custom_call_target="tpu_custom_call" | custom-call | flops 1 | bytes 1 | tf_op jit(solution)/shard_map/token_grad/pallas_call | solution.py:309
  250.7 7.2 %hidden_slope.1.a_ref.refs_1_ = bf16[1024,2048]{1,0:T(8,128)(2,1)S(1)} custom-call(bf16[1024,1024]{1,0:T(8,128)(2,1)S(1)} %copy-done.14, bf16[4,1024,512]{2,1,0:T(8,128)(2,1)S(1)} %bitcast.270, bf16[1024,2048]{1,0:T(8,128)(2,1)S(1)} %copy-done.25), custom_call_target="tpu_custom_call" | custom-call | flops 1 | bytes 1 | tf_op jit(solution)/shard_map/hidden_slope/pallas_call | solution.py:233
  257.9 4.3 hidden_down.5
  272.1 3.8 hidden_down.7
  279.2 3.9 fusion.49
  284.1 5.9 %piece_grads.3 = (bf16[4,256,512]{2,1,0:T(8,128)(2,1)S(1)}, bf16[4,256,512]{2,1,0:T(8,128)(2,1)S(1)}, bf16[4,256,512]{2,1,0:T(8,128)(2,1)S(1)}, bf16[4,256,512]{2,1,0:T(8,128)(2,1)S(1)}) custom-call(s32[1]{0:T(128)} %bitcast.31.chip_ref, bf16[1024,1024]{1,0:T(8,128)(2,1)S(1)} %pad_maximum_fusion.2.h_ref.refs_0_, bf16[1024,2048]{1,0:T(8,128)(2,1)S(1)} %copy-done.2), custom_call_target="tpu_custom_call" | custom-call | flops 1 | bytes 1 | tf_op jit(solution)/shard_map/piece_grads/pallas_call | solution.py:296
  298.3 10.2 %collective-permute-done.34 = bf16[2,256,512]{2,1,0:T(8,128)(2,1)S(1)} collective-permute-done((bf16[2,256,512]{2,1,0:T(8,128)(2,1)S(1)}, bf16[2,256,512]{2,1,0:T(8,128)(2,1)S(1)}, u32[]{:S(2)}, u32[]{:S(2)}) %collective-permute-start.34) | collective-permute-done | bytes 524320 | tf_op jit(solution)/shard_map/ppermute | solution.py:341
  315.6 5.4 cross_backward.1
  327.9 4.0 piece_grads.4
  353.9 6.4 %all-to-all-start.4 = ((bf16[4,16,1024]{2,1,0:T(8,128)(2,1)}), bf16[4,16,1024]{2,1,0:T(8,128)(2,1)S(1)}, u32[]{:S(2)}, u32[]{:S(2)}) async-start(bf16[4,16,1024]{2,1,0:T(8,128)(2,1)} %fusion.30), calls=%async_computation.7 | async-start | bytes 262144 | tf_op jit(solution)/shard_map/all_to_all | solution.py:563
  360.3 3.5 convolution_convert_fusion.2.r_4_
  363.8 4.1 collective-permute-done.42
  374.4 6.3 %all-to-all-start.2 = ((bf16[4,128,1024]{2,1,0:T(8,128)(2,1)}), bf16[4,128,1024]{2,1,0:T(8,128)(2,1)}, u32[]{:S(2)}, u32[]{:S(2)}) async-start(bf16[4,128,1024]{2,1,0:T(8,128)(2,1)} %bitcast.280), calls=%async_computation.3 | async-start | bytes 2097152 | tf_op jit(solution)/shard_map/all_to_all | solution.py:563
  389.4 17.2 %self_backward.1 = (bf16[1024,512]{1,0:T(8,128)(2,1)S(1)}, bf16[1024,512]{1,0:T(8,128)(2,1)S(1)}, bf16[1024,512]{1,0:T(8,128)(2,1)S(1)}) custom-call(s32[1]{0:T(128)} %bitcast.23.r_0_, bf16[1024,512]{1,0:T(8,128)(2,1)S(1)} %copy-done.29, bf16[1024,512]{1,0:T(8,128)(2,1)S(1)} %copy-done.27, bf16[1024,512]{1,0:T(8,128)(2,1)S(1)} %convolution_convert_fusion.5.r_3_, ...), custom_call_target="tpu_custom_call" | custom-call | flops 1 | bytes 1 | tf_op jit(solution)/shard_map/self_backward/pallas_call | solution.py:146
  406.6 6.2 %piece_grads.5 = (bf16[4,256,512]{2,1,0:T(8,128)(2,1)S(1)}, bf16[4,256,512]{2,1,0:T(8,128)(2,1)S(1)}, bf16[4,256,512]{2,1,0:T(8,128)(2,1)S(1)}, bf16[4,256,512]{2,1,0:T(8,128)(2,1)S(1)}) custom-call(s32[1]{0:T(128)} %bitcast.31.chip_ref, bf16[1024,1024]{1,0:T(8,128)(2,1)S(1)} %copy-done.23, bf16[1024,1024]{1,0:T(8,128)(2,1)S(1)} %pad_maximum_fusion.5.refs_1_, ...), custom_call_target="tpu_custom_call" | custom-call | flops 1 | bytes 1 | tf_op jit(solution)/shard_map/piece_grads/pallas_call | solution.py:296
  426.6 3.8 convert_add_fusion
  445.9 3.9 all-to-all-start.3
  450.6 13.7 %collective-permute-done.54 = bf16[4,256,512]{2,1,0:T(8,128)(2,1)} collective-permute-done((bf16[4,256,512]{2,1,0:T(8,128)(2,1)}, bf16[4,256,512]{2,1,0:T(8,128)(2,1)}, u32[]{:S(2)}, u32[]{:S(2)}) %collective-permute-start.54) | collective-permute-done | bytes 1048608 | tf_op jit(solution)/shard_map/ppermute | solution.py:341
  481.6 13.1 %collective-permute-done.59 = bf16[4,256,128]{2,1,0:T(8,128)(2,1)S(1)} collective-permute-done((bf16[4,256,128]{2,1,0:T(8,128)(2,1)S(1)}, bf16[4,256,128]{2,1,0:T(8,128)(2,1)S(1)}, u32[]{:S(2)}, u32[]{:S(2)}) %collective-permute-start.59) | collective-permute-done | bytes 262176 | tf_op jit(solution)/shard_map/ppermute | solution.py:345
  516.9 6.1 %collective-permute-start.76 = (f32[8,128]{1,0:T(8,128)S(1)}, f32[8,128]{1,0:T(8,128)S(1)}, u32[]{:S(2)}, u32[]{:S(2)}) collective-permute-start(f32[8,128]{1,0:T(8,128)S(1)} %add_add_fusion.7), channel_id=1, source_target_pairs={{0,1},{1,2},{2,3},{3,0},{4,5},{5,6},{6,7},{7,4},{8,9},{9,10},{10,1... | collective-permute-start | bytes 12296 | tf_op jit(solution)/shard_map/ppermute | solution.py:345
  (594 shorter events, 280.1 us)
Async XLA Ops:
  24.0 22.9 %collective-permute-start.4 = (bf16[4,264,128]{2,1,0:T(8,128)(2,1)S(1)}, bf16[4,264,128]{2,1,0:T(8,128)(2,1)S(1)}, u32[]{:S(2)}, u32[]{:S(2)}) collective-permute-start(bf16[4,264,128]{2,1,0:T(8,128)(2,1)S(1)} %fusion.24), channel_id=1, source_target_pairs={{0,2},{1,3},{2,0},{3,1},{4,6},{5,7},{6,4},{7,5},{8,10},{9,11},{10,... | collective-permute-start | bytes 811016 | tf_op jit(solution)/shard_map/ppermute | solution.py:345
  24.0 22.9 %collective-permute-start.5 = (bf16[4,264,128]{2,1,0:T(8,128)(2,1)S(1)}, bf16[4,264,128]{2,1,0:T(8,128)(2,1)S(1)}, u32[]{:S(2)}, u32[]{:S(2)}) collective-permute-start(bf16[4,264,128]{2,1,0:T(8,128)(2,1)S(1)} %fusion.24), channel_id=1, source_target_pairs={{0,1},{1,2},{2,3},{3,0},{4,5},{5,6},{6,7},{7,4},{8,9},{9,10},{10,1... | collective-permute-start | bytes 811016 | tf_op jit(solution)/shard_map/ppermute | solution.py:345
  47.0 24.7 %collective-permute-start.12 = (bf16[4,4,264,128]{3,2,1,0:T(8,128)(2,1)S(1)}, bf16[4,4,264,128]{3,2,1,0:T(8,128)(2,1)S(1)}, u32[]{:S(2)}, u32[]{:S(2)}) collective-permute-start(bf16[4,4,264,128]{3,2,1,0:T(8,128)(2,1)S(1)} %pad_maximum_fusion.6.refs_0_), channel_id=1, source_target_pairs={{0,8},{4,12},{8,0},{12,4},{16,24},{20,28},{24,16},{28,20},{1,9},{5... | collective-permute-start | bytes 3244040 | tf_op jit(solution)/shard_map/ppermute | solution.py:341
  47.6 24.3 %collective-permute-start.13 = (bf16[4,4,264,128]{3,2,1,0:T(8,128)(2,1)S(1)}, bf16[4,4,264,128]{3,2,1,0:T(8,128)(2,1)S(1)}, u32[]{:S(2)}, u32[]{:S(2)}) collective-permute-start(bf16[4,4,264,128]{3,2,1,0:T(8,128)(2,1)S(1)} %pad_maximum_fusion.6.refs_0_), channel_id=1, source_target_pairs={{0,16},{4,20},{8,24},{12,28},{16,0},{20,4},{24,8},{28,12},{1,17},{... | collective-permute-start | bytes 3244040 | tf_op jit(solution)/shard_map/ppermute | solution.py:341
  48.1 43.9 %all-to-all-start = ((bf16[4,128,1024]{2,1,0:T(8,128)(2,1)}), bf16[4,128,1024]{2,1,0:T(8,128)(2,1)}, u32[]{:S(2)}, u32[]{:S(2)}) async-start(bf16[4,128,1024]{2,1,0:T(8,128)(2,1)} %pad_maximum_fusion.7), calls=%async_computation | async-start | bytes 2097152 | tf_op jit(solution)/shard_map/all_to_all | solution.py:557
  52.4 42.1 %all-gather.7.cloned.1.call-start = ((), (), s32[]{:S(2)}) async-start(), calls=%async_computation.11 | async-start | bytes 1310720 | tf_op jit(solution)/shard_map/all_gather | solution.py:615
  53.1 78.8 %all-gather.9.cloned.1.call-start = ((), (), s32[]{:S(2)}) async-start(), calls=%async_computation.12 | async-start | bytes 1310720 | tf_op jit(solution)/shard_map/all_gather | solution.py:620
  73.6 20.9 %collective-permute-start.14 = (bf16[2,4,264,128]{3,2,1,0:T(8,128)(2,1)}, bf16[2,4,264,128]{3,2,1,0:T(8,128)(2,1)}, u32[]{:S(2)}, u32[]{:S(2)}) collective-permute-start(bf16[2,4,264,128]{3,2,1,0:T(8,128)(2,1)} %get-tuple-element.141), channel_id=1, source_target_pairs={{0,8},{4,12},{8,0},{12,4},{16,24},{20,28},{24,16},{28,20},{1,9},{5... | collective-permute-start | bytes 1622024 | tf_op jit(solution)/shard_map/ppermute | solution.py:341
  94.5 34.0 %collective-permute-start.17 = (bf16[4,4,256,128]{3,2,1,0:T(8,128)(2,1)}, bf16[4,4,256,128]{3,2,1,0:T(8,128)(2,1)}, u32[]{:S(2)}, u32[]{:S(2)}) collective-permute-start(bf16[4,4,256,128]{3,2,1,0:T(8,128)(2,1)} %bitcast.273), channel_id=1, source_target_pairs={{0,8},{4,12},{8,0},{12,4},{16,24},{20,28},{24,16},{28,20},{1,9},{5... | collective-permute-start | bytes 3145736 | tf_op jit(solution)/shard_map/ppermute | solution.py:341
  96.1 32.5 %collective-permute-start.18 = (bf16[4,4,256,128]{3,2,1,0:T(8,128)(2,1)}, bf16[4,4,256,128]{3,2,1,0:T(8,128)(2,1)}, u32[]{:S(2)}, u32[]{:S(2)}) collective-permute-start(bf16[4,4,256,128]{3,2,1,0:T(8,128)(2,1)} %bitcast.274), channel_id=1, source_target_pairs={{0,16},{4,20},{8,24},{12,28},{16,0},{20,4},{24,8},{28,12},{1,17},{... | collective-permute-start | bytes 3145736 | tf_op jit(solution)/shard_map/ppermute | solution.py:341
  143.0 47.3 %all-to-all-start.1 = ((bf16[4,128,1024]{2,1,0:T(8,128)(2,1)}), bf16[4,128,1024]{2,1,0:T(8,128)(2,1)}, u32[]{:S(2)}, u32[]{:S(2)}) async-start(bf16[4,128,1024]{2,1,0:T(8,128)(2,1)} %pad_maximum_fusion.10), calls=%async_computation.1 | async-start | bytes 2097152 | tf_op jit(solution)/shard_map/all_to_all | solution.py:557
  147.3 97.4 %all-gather.11.cloned.1.call-start = ((), (), s32[]{:S(2)}) async-start(), calls=%async_computation.13 | async-start | bytes 5242880 | tf_op jit(solution)/shard_map/all_gather | solution.py:645
  154.0 169.8 %reduce-scatter.4.cloned.1.call-start = ((), (), s32[]{:S(2)}) async-start(), calls=%async_computation.8 | async-start | bytes 5242880 | tf_op jit(solution)/shard_map/reduce_scatter | solution.py:675
  154.1 33.7 %collective-permute-start.25 = (bf16[4,1,256,512]{3,2,1,0:T(8,128)(2,1)}, bf16[4,1,256,512]{3,2,1,0:T(8,128)(2,1)S(1)}, u32[]{:S(2)}, u32[]{:S(2)}) collective-permute-start(bf16[4,1,256,512]{3,2,1,0:T(8,128)(2,1)} %bitcast.35.refs_0_), channel_id=1, source_target_pairs={{0,8},{4,12},{8,0},{12,4},{16,24},{20,28},{24,16},{28,20},{1,9},{5... | collective-permute-start | bytes 3145736 | tf_op jit(solution)/shard_map/ppermute | solution.py:341
  154.7 34.3 %collective-permute-start.26 = (bf16[4,1,256,512]{3,2,1,0:T(8,128)(2,1)}, bf16[4,1,256,512]{3,2,1,0:T(8,128)(2,1)S(1)}, u32[]{:S(2)}, u32[]{:S(2)}) collective-permute-start(bf16[4,1,256,512]{3,2,1,0:T(8,128)(2,1)} %bitcast.35.refs_0_), channel_id=1, source_target_pairs={{0,16},{4,20},{8,24},{12,28},{16,0},{20,4},{24,8},{28,12},{1,17},{... | collective-permute-start | bytes 3145736 | tf_op jit(solution)/shard_map/ppermute | solution.py:341
  275.9 20.7 %collective-permute-start.36 = (bf16[512,1024]{1,0:T(8,128)(2,1)S(1)}, bf16[512,1024]{1,0:T(8,128)(2,1)S(1)}, u32[]{:S(2)}, u32[]{:S(2)}) collective-permute-start(bf16[512,1024]{1,0:T(8,128)(2,1)S(1)} %hidden_down.7), channel_id=1, source_target_pairs={{0,4},{4,0},{8,12},{12,8},{16,20},{20,16},{24,28},{28,24},{1,5},{5... | collective-permute-start | bytes 3145736 | tf_op jit(solution)/shard_map/ppermute | solution.py:341
  310.9 38.3 %collective-permute-start.41 = (bf16[4,256,512]{2,1,0:T(8,128)(2,1)}, bf16[4,256,512]{2,1,0:T(8,128)(2,1)}, u32[]{:S(2)}, u32[]{:S(2)}) collective-permute-start(bf16[4,256,512]{2,1,0:T(8,128)(2,1)} %pad_maximum_fusion.16), channel_id=1, source_target_pairs={{0,16},{4,20},{8,24},{12,28},{16,0},{20,4},{24,8},{28,12},{1,17},{... | collective-permute-start | bytes 3145736 | tf_op jit(solution)/shard_map/ppermute | solution.py:341
  312.6 36.6 %collective-permute-start.40 = (bf16[4,256,512]{2,1,0:T(8,128)(2,1)}, bf16[4,256,512]{2,1,0:T(8,128)(2,1)}, u32[]{:S(2)}, u32[]{:S(2)}) collective-permute-start(bf16[4,256,512]{2,1,0:T(8,128)(2,1)} %pad_maximum_fusion.15), channel_id=1, source_target_pairs={{0,8},{4,12},{8,0},{12,4},{16,24},{20,28},{24,16},{28,20},{1,9},{5... | collective-permute-start | bytes 3145736 | tf_op jit(solution)/shard_map/ppermute | solution.py:341
  347.0 34.3 %collective-permute-start.45 = (bf16[1,256,512]{2,1,0:T(8,128)(2,1)}, bf16[1,256,512]{2,1,0:T(8,128)(2,1)}, u32[]{:S(2)}, u32[]{:S(2)}) collective-permute-start(bf16[1,256,512]{2,1,0:T(8,128)(2,1)} %pad_maximum_fusion.27), channel_id=1, source_target_pairs={{0,8},{4,12},{8,0},{12,4},{16,24},{20,28},{24,16},{28,20},{1,9},{5... | collective-permute-start | bytes 786440 | tf_op jit(solution)/shard_map/ppermute | solution.py:341
  348.4 33.0 %collective-permute-start.47 = (bf16[1,256,512]{2,1,0:T(8,128)(2,1)}, bf16[1,256,512]{2,1,0:T(8,128)(2,1)}, u32[]{:S(2)}, u32[]{:S(2)}) collective-permute-start(bf16[1,256,512]{2,1,0:T(8,128)(2,1)} %pad_maximum_fusion.28), channel_id=1, source_target_pairs={{0,16},{4,20},{8,24},{12,28},{16,0},{20,4},{24,8},{28,12},{1,17},{... | collective-permute-start | bytes 786440 | tf_op jit(solution)/shard_map/ppermute | solution.py:341
  353.9 20.5 %all-to-all-start.4 = ((bf16[4,16,1024]{2,1,0:T(8,128)(2,1)}), bf16[4,16,1024]{2,1,0:T(8,128)(2,1)S(1)}, u32[]{:S(2)}, u32[]{:S(2)}) async-start(bf16[4,16,1024]{2,1,0:T(8,128)(2,1)} %fusion.30), calls=%async_computation.7 | async-start | bytes 262144 | tf_op jit(solution)/shard_map/all_to_all | solution.py:563
  370.1 45.9 %collective-permute-start.49 = (bf16[4,256,512]{2,1,0:T(8,128)(2,1)}, bf16[4,256,512]{2,1,0:T(8,128)(2,1)}, u32[]{:S(2)}, u32[]{:S(2)}) collective-permute-start(bf16[4,256,512]{2,1,0:T(8,128)(2,1)} %pad_maximum_fusion.18), channel_id=1, source_target_pairs={{0,16},{4,20},{8,24},{12,28},{16,0},{20,4},{24,8},{28,12},{1,17},{... | collective-permute-start | bytes 3145736 | tf_op jit(solution)/shard_map/ppermute | solution.py:341
  372.9 43.0 %collective-permute-start.48 = (bf16[4,256,512]{2,1,0:T(8,128)(2,1)}, bf16[4,256,512]{2,1,0:T(8,128)(2,1)}, u32[]{:S(2)}, u32[]{:S(2)}) collective-permute-start(bf16[4,256,512]{2,1,0:T(8,128)(2,1)} %pad_maximum_fusion.17), channel_id=1, source_target_pairs={{0,8},{4,12},{8,0},{12,4},{16,24},{20,28},{24,16},{28,20},{1,9},{5... | collective-permute-start | bytes 3145736 | tf_op jit(solution)/shard_map/ppermute | solution.py:341
  374.4 71.5 %all-to-all-start.2 = ((bf16[4,128,1024]{2,1,0:T(8,128)(2,1)}), bf16[4,128,1024]{2,1,0:T(8,128)(2,1)}, u32[]{:S(2)}, u32[]{:S(2)}) async-start(bf16[4,128,1024]{2,1,0:T(8,128)(2,1)} %bitcast.280), calls=%async_computation.3 | async-start | bytes 2097152 | tf_op jit(solution)/shard_map/all_to_all | solution.py:563
  380.7 114.2 %reduce-scatter.8.cloned.1.call-start = ((), (), s32[]{:S(2)}) async-start(), calls=%async_computation.10 | async-start | bytes 1310720 | tf_op jit(solution)/shard_map/reduce_scatter | solution.py:534
  385.6 109.3 %reduce-scatter.6.cloned.1.call-start = ((), (), s32[]{:S(2)}) async-start(), calls=%async_computation.9 | async-start | bytes 1310720 | tf_op jit(solution)/shard_map/reduce_scatter | solution.py:534
  439.6 24.7 %collective-permute-start.54 = (bf16[4,256,512]{2,1,0:T(8,128)(2,1)}, bf16[4,256,512]{2,1,0:T(8,128)(2,1)}, u32[]{:S(2)}, u32[]{:S(2)}) collective-permute-start(bf16[4,256,512]{2,1,0:T(8,128)(2,1)} %pad_maximum_fusion.20), channel_id=1, source_target_pairs={{0,16},{4,20},{8,24},{12,28},{16,0},{20,4},{24,8},{28,12},{1,17},{... | collective-permute-start | bytes 3145736 | tf_op jit(solution)/shard_map/ppermute | solution.py:341
  442.6 24.4 %collective-permute-start.53 = (bf16[4,256,512]{2,1,0:T(8,128)(2,1)}, bf16[4,256,512]{2,1,0:T(8,128)(2,1)}, u32[]{:S(2)}, u32[]{:S(2)}) collective-permute-start(bf16[4,256,512]{2,1,0:T(8,128)(2,1)} %pad_maximum_fusion.19), channel_id=1, source_target_pairs={{0,8},{4,12},{8,0},{12,4},{16,24},{20,28},{24,16},{28,20},{1,9},{5... | collective-permute-start | bytes 3145736 | tf_op jit(solution)/shard_map/ppermute | solution.py:341
  445.9 49.1 %all-to-all-start.3 = ((bf16[4,128,1024]{2,1,0:T(8,128)(2,1)}), bf16[4,128,1024]{2,1,0:T(8,128)(2,1)S(1)}, u32[]{:S(2)}, u32[]{:S(2)}) async-start(bf16[4,128,1024]{2,1,0:T(8,128)(2,1)} %bitcast.281), calls=%async_computation.4 | async-start | bytes 2097152 | tf_op jit(solution)/shard_map/all_to_all | solution.py:563
  471.1 23.7 %collective-permute-start.59 = (bf16[4,256,128]{2,1,0:T(8,128)(2,1)S(1)}, bf16[4,256,128]{2,1,0:T(8,128)(2,1)S(1)}, u32[]{:S(2)}, u32[]{:S(2)}) collective-permute-start(bf16[4,256,128]{2,1,0:T(8,128)(2,1)S(1)} %get-tuple-element.314), channel_id=1, source_target_pairs={{0,2},{1,3},{2,0},{3,1},{4,6},{5,7},{6,4},{7,5},{8,10},{9,11},{10,... | collective-permute-start | bytes 786440 | tf_op jit(solution)/shard_map/ppermute | solution.py:345
  471.6 23.1 %collective-permute-start.60 = (bf16[4,256,128]{2,1,0:T(8,128)(2,1)S(1)}, bf16[4,256,128]{2,1,0:T(8,128)(2,1)S(1)}, u32[]{:S(2)}, u32[]{:S(2)}) collective-permute-start(bf16[4,256,128]{2,1,0:T(8,128)(2,1)S(1)} %get-tuple-element.313), channel_id=1, source_target_pairs={{0,3},{1,0},{2,1},{3,2},{4,7},{5,4},{6,5},{7,6},{8,11},{9,8},{10,9... | collective-permute-start | bytes 786440 | tf_op jit(solution)/shard_map/ppermute | solution.py:345
  478.4 29.6 %collective-permute-start.37 = (bf16[2,128,1024]{2,1,0:T(8,128)(2,1)}, bf16[2,128,1024]{2,1,0:T(8,128)(2,1)}, u32[]{:S(2)}, u32[]{:S(2)}) collective-permute-start(bf16[2,128,1024]{2,1,0:T(8,128)(2,1)} %broadcast_select_fusion.4), channel_id=1, source_target_pairs={{0,4},{4,0},{8,12},{12,8},{16,20},{20,16},{24,28},{28,24},{1,5},{5... | collective-permute-start | bytes 1572872 | tf_op jit(solution)/shard_map/ppermute | solution.py:341
  (162 other events, 1025.2 us)
Sparse Core Ops, SparseCore 0:
  55.4 39.1 all-gather.6
  106.3 25.5 all-gather.8
  154.1 87.6 all-gather.10
  244.8 78.9 reduce-scatter.3
  385.8 36.1 reduce-scatter.7
  426.2 29.9 reduce-scatter.5
